TPU v7x, 32 devices: a whole 2x2x4 slice. The times are simulated.
32 devices in a mesh: groups: 2 (over y), probe: 4 (over z), depth: 2 (over x), tile: 2 (over core).
Axes of the slice: x: 2, y: 2, z: 4, core: 2. Of those that a mesh axis runs over, the one named last changes fastest.
Arguments:
- stored_waves: bfloat16 [2, 16, 2, 256, 256], P('depth', ('groups', 'probe', 'tile')), parts along dimension 1, may hold values from -6 to 6
- transmission: bfloat16 [2, 16, 2, 256, 256], P('depth', ('groups', 'probe', 'tile')), parts along dimension 1
- residual: float32 [16, 2, 256, 256], P(('groups', 'probe', 'tile')), parts along dimension 0, may hold values from -0.6 to 0.6
- offsets: int32 [16, 2], P('groups'), parts along dimension 0, may hold values from 0 to 256
- slot_position: int32 [16], P(('groups', 'probe', 'tile')), parts along dimension 0, may hold values from 0 to 7, each once
Outputs:
- object_gradient: float32 [4, 2, 512, 512], P('groups', 'depth', 'probe', 'tile'), parts along dimension 0
There are 2 independent parts, one for each index of `groups`. A program takes and returns all parts, laid end to end along the dimension named above; each array names one. Nothing has to cross between parts.
Inputs may be any that keep to these rules, and one draw needn't show every extreme that they name: `slot_position`: every scan position is held by exactly one slot.
All inputs are finite; a program needn't handle non-finite values.
Results may differ from a plain program's by a relative error of at most 0.0032.
Values may be sent and summed in bfloat16 or wider, within the bound.
No kernel may reach another device: no remote copies, remote signals or barrier semaphores. Data moves between devices by JAX's collectives and lax.ppermute only.
A program may use at most 64 MiB of HBM per device.

v0:
```python
import math

import jax
import jax.numpy as jnp
from jax import lax
from jax.sharding import PartitionSpec as P

OBJ = 512


def from_behind(value, axis, steps):
    count = lax.axis_size(axis)
    leading, last = (max(0, -steps), min(count, count - steps))
    return lax.ppermute(value, axis, [(source, source + steps) for source in range(leading, last)])


def dft_tables(side_length):
    counter = lax.iota(jnp.int32, side_length)
    turns = counter[:, None] * counter[None, :] % side_length
    angle = turns.astype(jnp.float32) * (2.0 * math.pi / side_length)
    frequency = ((counter + side_length // 2) % side_length - side_length // 2).astype(jnp.float32)
    phase_angle = (
        0.5
        * (frequency[:, None] * frequency[:, None] + frequency[None, :] * frequency[None, :])
        / side_length
    )
    return (jnp.cos(angle), jnp.sin(angle), jnp.cos(phase_angle), jnp.sin(phase_angle))


def left_apply(matrix, field):
    return jnp.einsum("kn,pnm->pkm", matrix, field, precision=lax.Precision.HIGHEST)


def right_apply(matrix, field):
    return jnp.einsum("pnm,mk->pnk", field, matrix, precision=lax.Precision.HIGHEST)


def complex_left(tables, direction_sign, real_part, imag_part):
    cosine = tables[0]
    sine_table = tables[1]
    return (
        left_apply(cosine, real_part) - direction_sign * left_apply(sine_table, imag_part),
        left_apply(cosine, imag_part) + direction_sign * left_apply(sine_table, real_part),
    )


def complex_right(tables, direction_sign, real_part, imag_part):
    cosine = tables[0]
    sine_table = tables[1]
    return (
        right_apply(cosine, real_part) - direction_sign * right_apply(sine_table, imag_part),
        right_apply(cosine, imag_part) + direction_sign * right_apply(sine_table, real_part),
    )


def back_propagate(tables, real_part, imag_part):
    side_length = real_part.shape[-1]
    spec_real, spec_imag = complex_left(tables, -1.0, real_part, imag_part)
    spec_real, spec_imag = complex_right(tables, -1.0, spec_real, spec_imag)
    turn_real = spec_real * tables[2] - spec_imag * tables[3]
    turn_imag = spec_real * tables[3] + spec_imag * tables[2]
    back_real, back_imag = complex_left(tables, 1.0, turn_real, turn_imag)
    back_real, back_imag = complex_right(tables, 1.0, back_real, back_imag)
    inverse_area = 1.0 / (side_length * side_length)
    return (back_real * inverse_area, back_imag * inverse_area)


def per_device(stored_waves, transmission, residual, offsets, slot_position):
    slot_count = stored_waves.shape[1]
    side_length = stored_waves.shape[-1]
    depth_count = lax.axis_size("depth")
    depth_index = lax.axis_index("depth")
    is_top = depth_index == depth_count - 1
    tables = dft_tables(side_length)
    every_position = lax.iota(jnp.int32, offsets.shape[0])
    matches = (slot_position[:, None] == every_position[None, :]).astype(jnp.int32)
    own_offsets = jnp.sum(matches[:, :, None] * offsets[None, :, :], axis=1)
    slice_waves = stored_waves[0]
    slice_layers = transmission[0]
    empty_region = jnp.zeros((2, 1, OBJ, OBJ), jnp.float32)

    def advance(incoming, region, front_size):

        def start_top():
            return (residual[:, 0], residual[:, 1])

        def start_below():
            return back_propagate(
                tables, incoming[:, 0].astype(jnp.float32), incoming[:, 1].astype(jnp.float32)
            )

        adjoint_real, adjoint_imag = lax.cond(is_top, start_top, start_below)
        waves_here = slice_waves.astype(jnp.float32)
        layers_here = slice_layers.astype(jnp.float32)
        grad_real = waves_here[:, 0] * adjoint_real + waves_here[:, 1] * adjoint_imag
        grad_imag = waves_here[:, 0] * adjoint_imag - waves_here[:, 1] * adjoint_real
        handed = jnp.stack(
            [
                layers_here[:, 0] * adjoint_real + layers_here[:, 1] * adjoint_imag,
                layers_here[:, 0] * adjoint_imag - layers_here[:, 1] * adjoint_real,
            ],
            1,
        ).astype(jnp.bfloat16)
        gradient = jnp.stack([grad_real, grad_imag], 0)

        def add_patch(number, region):
            patch_value = lax.dynamic_index_in_dim(gradient, number, 1, keepdims=True)
            anchor = jnp.int32(0)
            corner = (anchor, anchor, own_offsets[number, 0], own_offsets[number, 1])
            current = lax.dynamic_slice(region, corner, (2, 1, side_length, side_length))
            return lax.dynamic_update_slice(region, current + patch_value, corner)

        return (handed, lax.fori_loop(0, front_size, add_patch, region))

    front_size = slot_count

    def handoff(handed):
        return from_behind(handed, "depth", -1)

    resting = jnp.zeros((front_size, 2, side_length, side_length), jnp.bfloat16)

    def one_turn(turn, incoming, region):
        front = (turn - (depth_count - 1 - depth_index)) * front_size
        active = (front >= 0) & (front + front_size <= slot_count)
        return lax.cond(
            active, lambda: advance(incoming, region, front_size), lambda: (resting, region)
        )

    start_state = one_turn(0, resting, empty_region)

    def loop_body(turn, carry):
        return one_turn(turn, handoff(carry[0]), carry[1])

    final_state = lax.fori_loop(1, depth_count, loop_body, start_state)
    region = final_state[1]
    strips = lax.psum_scatter(region, "probe", scatter_dimension=2, tiled=True)
    return lax.psum_scatter(strips, "tile", scatter_dimension=3, tiled=True)


def solution(mesh):
    return jax.shard_map(
        per_device,
        mesh=mesh,
        in_specs=(
            P("depth", ("groups", "probe", "tile"), None, None, None),
            P("depth", ("groups", "probe", "tile"), None, None, None),
            P(("groups", "probe", "tile"), None, None, None),
            P("groups", None),
            P(("groups", "probe", "tile")),
        ),
        out_specs=P("groups", "depth", "probe", "tile"),
        check_vma=False,
    )
```

profile of v0, /device:TPU:0, one launch (start us, length us, event | category | flops | bytes accessed | tf_op | source)
XLA Modules:
  0.0 116.7 jit_solution(14352994091525498350)
XLA Ops:
  6.5 0.0 reduce-scatter.3.cloned.1.call-start
  6.5 1.0 fusion.46
  8.2 1.0 fusion.41
  9.3 0.8 multiply_reduce_fusion.2
  10.1 1.6 %conditional.4 = (bf16[1,2,256,256]{3,2,1,0:T(8,128)(2,1)S(1)}, f32[2,1,512,512]{3,2,1,0:T(8,128)}) conditional(s32[]{:T(128)} %convert_element_type.146, () %tuple.50, (bf16[1,1,2,256,256]{4,3,2,1,0:T(8,128)(2,1)}, pred[]{:T(512)}, f32[256,256]{1,0:T(8,128)S(1)}, f32[256,256]{1,0:T(8,128)S(1)}, f32[256,256]{1,0:T(8,128)S(1)}, ...), branch_computations={%region_1.2_spmd, %region_2.7_spmd} | conditional | flops 2418671872 | bytes 22817092 | solution.py:125
  10.1 1.6 %broadcast_in_dim.4 = f32[2,1,512,512]{3,2,1,0:T(8,128)} broadcast(f32[]{:T(128)} %constant.80.clone), dimensions={} | broadcast | bytes 2097156 | tf_op jit(solution)/shard_map/broadcast_in_dim | solution.py:80
  11.7 1.3 %collective-permute-start = (bf16[1,2,256,256]{3,2,1,0:T(8,128)(2,1)S(1)}, bf16[1,2,256,256]{3,2,1,0:T(8,128)(2,1)S(1)}, u32[]{:S(2)}, u32[]{:S(2)}) collective-permute-start(bf16[1,2,256,256]{3,2,1,0:T(8,128)(2,1)S(1)} %get-tuple-element.329), channel_id=1, source_target_pairs={{2,0},{3,1},{6,4},{7,5},{10,8},{11,9},{14,12},{15,13},{18,16},{19,... | collective-permute-start | bytes 786440 | tf_op jit(solution)/shard_map/while/body/eval_jaxpr/ppermute | solution.py:14
  13.0 20.8 %collective-permute-done = bf16[1,2,256,256]{3,2,1,0:T(8,128)(2,1)S(1)} collective-permute-done((bf16[1,2,256,256]{3,2,1,0:T(8,128)(2,1)S(1)}, bf16[1,2,256,256]{3,2,1,0:T(8,128)(2,1)S(1)}, u32[]{:S(2)}, u32[]{:S(2)}) %collective-permute-start) | collective-permute-done | bytes 262176 | tf_op jit(solution)/shard_map/while/body/eval_jaxpr/ppermute | solution.py:14
  33.7 21.4 %conditional.5 = (f32[2,1,512,512]{3,2,1,0:T(8,128)}) conditional(s32[]{:T(128)} %convert_element_type.145, f32[2,1,512,512]{3,2,1,0:T(8,128)} %get-tuple-element.328, (s32[1,2]{1,0:T(1,128)S(1)}, f32[2,1,512,512]{3,2,1,0:T(8,128)}, bf16[1,2,256,256]{3,2,1,0:T(8,128)(2,1)}, pred[]{:T(512)}, bf16[1,2,256,256]{3,2,1,0:T(8,128)(2,1)S(1)}, ...), branch_computations={%region_7.8_spmd, %region_8.11_spmd} | conditional | flops 3223322624 | bytes 21758268 | solution.py:125
  33.7 0.0 copy-start.1
  33.7 8.6 %conditional.1 = (f32[1,256,256]{2,1,0:T(8,128)S(1)}, f32[1,256,256]{2,1,0:T(8,128)S(1)}) conditional(s32[]{:T(128)} %convert_element_type.103, (bf16[1,2,256,256]{3,2,1,0:T(8,128)(2,1)S(1)}, f32[256,256]{1,0:T(8,128)S(1)}, f32[256,256]{1,0:T(8,128)S(1)}, f32[256,256]{1,0:T(8,128)S(1)}, f32[256,256]{1,0:T(8,128)S(1)}, ...), branch_computations={%region_9.9_spmd, %region_10.10_spmd} | conditional | flops 3222536192 | bytes 15728656 | solution.py:92
  33.7 0.3 fusion.32
  34.1 0.3 fusion.27
  34.4 0.6 fusion.54
  35.0 0.3 fusion.28
  35.3 0.3 fusion.25
  35.7 0.6 fusion.23
  36.3 0.6 fusion.55
  36.9 0.6 multiply_add_fusion.2
  37.5 0.6 fusion.58
  38.1 0.6 fusion.20
  38.7 0.6 fusion.56
  39.3 0.6 fusion.21
  40.0 0.6 fusion.57
  40.6 0.6 fusion.19
  41.2 0.6 fusion.59
  41.8 0.6 fusion.17
  42.4 0.6 fusion.53
  46.9 0.0 copy-done.1
  47.0 0.1 add_bitcast_fusion.1
  47.0 1.4 %maximum_add_fusion = f32[2,1,256,256]{3,2,1,0:T(8,128)S(1)} fusion(f32[1,1,256,256]{3,2,1,0:T(8,128)S(1)} %get-tuple-element.353, f32[1,1,256,256]{3,2,1,0:T(8,128)S(1)} %get-tuple-element.352, f32[2,1,512,512]{3,2,1,0:T(8,128)} %get-tuple-element.298, s32[]{:T(128)S(6)} %select_n.86, s32[]{:T(128)S(6)} %select_n.87), kind=kLoop, calls=%fused_computation.75 | loop fusion | flops 262144 | bytes 1572872 | tf_op jit(solution)/shard_map/while/body/eval_jaxpr/cond/branch_1_fun/while/body/eval_jaxpr/add | solution.py:111
  48.4 6.8 %dynamic_update_slice.9 = f32[2,1,512,512]{3,2,1,0:T(8,128)} dynamic-update-slice(f32[2,1,512,512]{3,2,1,0:T(8,128)} %get-tuple-element.298, f32[2,1,256,256]{3,2,1,0:T(8,128)S(1)} %maximum_add_fusion, s32[]{:T(128)} %constant.89.clone, s32[]{:T(128)} %constant.89.clone, s32[]{:T(128)S(6)} %select_n.86, s32[]{:T(128)S(6)} %select_n.87) | dynamic-update-slice | bytes 1048580 | tf_op jit(solution)/shard_map/while/body/eval_jaxpr/cond/branch_1_fun/while/body/eval_jaxpr/dynamic_update_slice | solution.py:111
  55.2 0.0 reduce-scatter.3.cloned.1.call-update
  55.2 0.0 reduce-scatter.5.cloned.1.call-start
  55.3 45.0 %reduce-scatter.3.cloned.1.call-done = f32[2,1,128,512]{3,2,1,0:T(8,128)} async-done(((f32[2,1,512,512]{3,2,1,0:T(8,128)}), f32[2,1,128,512]{3,2,1,0:T(8,128)}) %reduce-scatter.3.cloned.1.call-update) | async-done | bytes 524304 | tf_op jit(solution)/shard_map/reduce_scatter | solution.py:136
  100.2 0.0 reduce-scatter.5.cloned.1.call-update
  100.2 9.6 %reduce-scatter.5.cloned.1.call-done = f32[2,1,128,256]{3,2,1,0:T(8,128)} async-done(((f32[2,1,128,512]{3,2,1,0:T(8,128)}), f32[2,1,128,256]{3,2,1,0:T(8,128)}) %reduce-scatter.5.cloned.1.call-update) | async-done | bytes 262160 | tf_op jit(solution)/shard_map/reduce_scatter | solution.py:137
  (4 shorter events, 0.1 us)
Async XLA Ops:
  6.5 93.7 %reduce-scatter.3.cloned.1.call-start = ((), (), s32[]{:S(2)}) async-start(), calls=%async_computation.2 | async-start | bytes 2621440 | tf_op jit(solution)/shard_map/reduce_scatter | solution.py:136
  11.7 22.0 %collective-permute-start = (bf16[1,2,256,256]{3,2,1,0:T(8,128)(2,1)S(1)}, bf16[1,2,256,256]{3,2,1,0:T(8,128)(2,1)S(1)}, u32[]{:S(2)}, u32[]{:S(2)}) collective-permute-start(bf16[1,2,256,256]{3,2,1,0:T(8,128)(2,1)S(1)} %get-tuple-element.329), channel_id=1, source_target_pairs={{2,0},{3,1},{6,4},{7,5},{10,8},{11,9},{14,12},{15,13},{18,16},{19,... | collective-permute-start | bytes 786440 | tf_op jit(solution)/shard_map/while/body/eval_jaxpr/ppermute | solution.py:14
  33.7 13.2 %copy-start.1 = (bf16[1,2,256,256]{3,2,1,0:T(8,128)(2,1)S(1)}, bf16[1,2,256,256]{3,2,1,0:T(8,128)(2,1)}, u32[]{:S(2)}) copy-start(bf16[1,2,256,256]{3,2,1,0:T(8,128)(2,1)} %get-tuple-element.300) | copy-start | bytes 786436 | tf_op jit(solution)/shard_map/while/body/eval_jaxpr/cond
  55.2 54.6 %reduce-scatter.5.cloned.1.call-start = ((), (), s32[]{:S(2)}) async-start(), calls=%async_computation.3 | async-start | bytes 786432 | tf_op jit(solution)/shard_map/reduce_scatter | solution.py:137
Sparse Core Ops, SparseCore 0:
  55.3 44.8 reduce-scatter.2
  102.6 7.2 reduce-scatter.4
where the time goes:
time: 117 us
  waiting for transfers between devices  75.4 us (64%)
  between operations  14.1 us (12%)
  local copies, waits for them, and re-layouts  8.98 us (8%)
  matrix products  8.53 us (7%)
  other arithmetic  4.32 us (4%)
  loops' own time  4.1 us (4%)
  starting transfers between devices  1.32 us (1%)
    reduce_scatter x1, waiting for transfers between devices, per_device(): strips = lax.psum_scatter(region, 'probe', scatter_dimension=2, tiled=True)  45 us
    ppermute x1, waiting for transfers between devices, from_behind(): lax.ppermute(value, axis, [(source, source + steps) for source in range(l...  20.8 us
    reduce_scatter x1, waiting for transfers between devices, per_device(): return lax.psum_scatter(strips, 'tile', scatter_dimension=3, tiled=True)  9.61 us
    dynamic_update_slice x1, local copies, waits for them, and re-layouts, add_patch(): return lax.dynamic_update_slice(region, current + patch_value, corner)  6.76 us
    dot_general x8, matrix products, right_apply(): jnp.einsum('pnm,mk->pnk', field, matrix, precision=lax.Precision.HIGHEST)  4.81 us
    another operation x2, loops' own time, one_turn(): lax.cond(active, lambda: advance(incoming, region, front_size), lambda: (...  3.99 us
    dot_general x8, matrix products, left_apply(): jnp.einsum('kn,pnm->pkm', matrix, field, precision=lax.Precision.HIGHEST)  3.71 us
  transfers between devices with their start and end apart: 3, of which 3 were waited for; matrix products, arithmetic and copies ran while one was open for 0% of the time, Pallas kernels for 0%

commit v1 on v0

v1 whole, which is shorter than its diff:
```python
import functools
import math

import jax
import jax.numpy as jnp
import numpy as np
from jax import lax
from jax.experimental import pallas as pl
from jax.experimental.pallas import tpu as pltpu
from jax.sharding import PartitionSpec as P

OBJ = 512
TAIL = 16


def propagator(side):
    counter = np.arange(side)
    frequency = (counter + side // 2) % side - side // 2
    chirp = np.exp(0.5j * frequency.astype(np.float64) ** 2 / side)
    ring = np.fft.ifft(chirp)
    ring = 0.5 * (ring + ring[(-counter) % side])
    matrix = ring[(counter[:, None] - counter[None, :]) % side]
    parts = np.stack([matrix.real, matrix.imag]).astype(np.float32)
    high = parts.astype(jnp.bfloat16)
    low = (parts - high.astype(np.float32)).astype(jnp.bfloat16)
    return np.concatenate([high[0], high[1], low[0], low[1]], axis=0)


def mm(a, b):
    return jnp.dot(a, b, preferred_element_type=jnp.float32)


def split(x):
    high = x.astype(jnp.bfloat16)
    return high, (x - high.astype(jnp.float32)).astype(jnp.bfloat16)


def send_kernel(
    slot_ref, offsets_ref, table_ref, waves_ref, layer_ref, residual_ref,
    adj_own_ref, adj_other_ref, wave_own_ref, wave_other_ref, adj_ref, wave_ref,
):
    side = waves_ref.shape[-1]
    half = side // 2
    top = lax.axis_index("depth") == 1
    parity = lax.rem(lax.axis_index("probe"), 2)
    slot = slot_ref[0]
    cy, cx = offsets_ref[slot, 0], offsets_ref[slot, 1]
    rows = lax.broadcasted_iota(jnp.int32, (side, side), 0)
    cols = lax.broadcasted_iota(jnp.int32, (side, side), 1)
    roll_rows = (cols == ((rows - cy) & (side - 1))).astype(jnp.bfloat16)
    roll_cols = (rows == ((cols - cx) & (side - 1))).astype(jnp.bfloat16)

    def rolled(stacked):
        moved = mm(stacked, roll_cols).astype(jnp.bfloat16)
        return [
            mm(roll_rows, moved[n * side : (n + 1) * side]).astype(jnp.bfloat16)
            for n in range(stacked.shape[0] // side)
        ]

    @pl.when(top)
    def _():
        res_r, res_i = residual_ref[0], residual_ref[1]
        lay_r, lay_i = layer_ref[0].astype(jnp.float32), layer_ref[1].astype(jnp.float32)
        wav_r, wav_i = waves_ref[0].astype(jnp.float32), waves_ref[1].astype(jnp.float32)
        handed_r = (lay_r * res_r + lay_i * res_i).astype(jnp.bfloat16)
        handed_i = (lay_r * res_i - lay_i * res_r).astype(jnp.bfloat16)
        grad_r = (wav_r * res_r + wav_i * res_i).astype(jnp.bfloat16)
        grad_i = (wav_r * res_i - wav_i * res_r).astype(jnp.bfloat16)
        hr, hi, gr, gi = rolled(jnp.concatenate([handed_r, handed_i, grad_r, grad_i], axis=0))
        wave_ref[0] = gr
        wave_ref[1] = gi
        handed = jnp.concatenate([hr, hi], axis=0)
        tables = [table_ref[n * side : (n + 1) * side] for n in range(4)]
        by_r = mm(handed, tables[2]) + mm(handed, tables[0])
        by_i = mm(handed, tables[3]) + mm(handed, tables[1])
        mid_r = by_r[:side] - by_i[side:]
        mid_i = by_r[side:] + by_i[:side]
        mrh, mrl = split(mid_r)
        mih, mil = split(mid_i)
        tall, short = table_ref[...], table_ref[: 2 * side]
        hi_r, hi_i = mm(tall, mrh), mm(tall, mih)
        lo_r, lo_i = mm(short, mrl), mm(short, mil)
        rr = hi_r[:side] + (hi_r[2 * side : 3 * side] + lo_r[:side])
        ir = hi_r[side : 2 * side] + (hi_r[3 * side :] + lo_r[side:])
        ri = hi_i[:side] + (hi_i[2 * side : 3 * side] + lo_i[:side])
        ii = hi_i[side : 2 * side] + (hi_i[3 * side :] + lo_i[side:])
        adj_ref[0] = (rr - ii).astype(jnp.bfloat16)
        adj_ref[1] = (ri + ir).astype(jnp.bfloat16)

    @pl.when(jnp.logical_not(top))
    def _():
        wr, wi = rolled(jnp.concatenate([waves_ref[0], waves_ref[1]], axis=0))
        wave_ref[0] = wr
        wave_ref[1] = wi
        adj_ref[...] = jnp.zeros_like(adj_ref)

    line = lax.broadcasted_iota(jnp.int32, (TAIL, side), 0)
    tail = jnp.where(line == 0, cy.astype(jnp.float32), cx.astype(jnp.float32)).astype(jnp.bfloat16)
    own = pl.ds(pl.multiple_of(parity * half, half), half)
    other = pl.ds(pl.multiple_of((1 - parity) * half, half), half)
    adj_own_ref[...] = adj_ref[:, own]
    adj_other_ref[...] = adj_ref[:, other]
    wave_own_ref[:, :half] = wave_ref[:, own]
    wave_other_ref[:, :half] = wave_ref[:, other]
    for part in range(2):
        wave_own_ref[part, half:] = tail
        wave_other_ref[part, half:] = tail


def gather_kernel(w0, w1, w2, w3, a0, a1, a2, a3, keep_ref, send_ref):
    half, side = a0.shape[1], a0.shape[2]
    place = lax.axis_index("probe")
    top = lax.axis_index("depth") == 1
    upper = place >= 2
    right = lax.axis_index("tile") == 1
    parity = lax.rem(place, 2)
    rows = (lax.broadcasted_iota(jnp.int32, (half, side), 0) + parity * half).astype(jnp.float32)
    cols = lax.broadcasted_iota(jnp.int32, (half, side), 1).astype(jnp.float32)
    keep = [jnp.zeros((half, side), jnp.float32)] * 2
    send = [jnp.zeros((half, side), jnp.float32)] * 2
    zero = jnp.zeros((half, side), jnp.float32)
    for w, a in ((w0, a0), (w1, a1), (w2, a2), (w3, a3)):
        tail = w[0, half:].astype(jnp.float32)
        cy, cx = tail[0:1], tail[1:2]
        wr, wi = w[0, :half].astype(jnp.float32), w[1, :half].astype(jnp.float32)
        ar, ai = a[0].astype(jnp.float32), a[1].astype(jnp.float32)
        here = (cols < cx) == right
        mine = (rows < cy) == upper
        gr = jnp.where(here, jnp.where(top, wr, wr * ar + wi * ai), zero)
        gi = jnp.where(here, jnp.where(top, wi, wr * ai - wi * ar), zero)
        keep = [keep[0] + jnp.where(mine, gr, zero), keep[1] + jnp.where(mine, gi, zero)]
        send = [send[0] + jnp.where(mine, zero, gr), send[1] + jnp.where(mine, zero, gi)]
    for part in range(2):
        keep_ref[part] = keep[part]
        send_ref[part] = send[part].astype(jnp.bfloat16)


def two_slices(stored_waves, transmission, residual, offsets, slot_position):
    side = stored_waves.shape[-1]
    half = side // 2
    table = jnp.asarray(propagator(side))
    vmem, smem = (pl.BlockSpec(memory_space=m) for m in (pltpu.VMEM, pltpu.SMEM))
    block = jax.ShapeDtypeStruct((2, half, side), jnp.bfloat16)
    tailed = jax.ShapeDtypeStruct((2, half + TAIL, side), jnp.bfloat16)
    adj_own, adj_other, wave_own, wave_other = pl.pallas_call(
        send_kernel,
        out_shape=(block, block, tailed, tailed),
        in_specs=[smem, smem, vmem, vmem, vmem, vmem],
        out_specs=(vmem,) * 4,
        scratch_shapes=[pltpu.VMEM((2, side, side), jnp.bfloat16)] * 2,
        compiler_params=pltpu.CompilerParams(vmem_limit_bytes=32 * 1024 * 1024),
        name="adjoint_and_rolls",
    )(slot_position, offsets, table, stored_waves[0, 0], transmission[0, 0], residual[0])

    probe_count = lax.axis_size("probe")
    swap_tile = [(0, 1), (1, 0)]
    flip = [(2 * z + d, 2 * z + 1 - d) for z in range(probe_count) for d in range(2)]
    flip_z1 = [(2 * z + d, 2 * (z ^ 1) + 1 - d) for z in range(probe_count) for d in range(2)]
    z1 = [(z, z ^ 1) for z in range(probe_count)]
    z2 = [(z, z ^ 2) for z in range(probe_count)]
    a_own = lax.ppermute(adj_own, ("probe", "depth"), flip)
    a_next = lax.ppermute(adj_other, ("probe", "depth"), flip_z1)
    w_next = lax.ppermute(wave_other, "probe", z1)
    w_side = lax.ppermute(wave_own, "tile", swap_tile)
    a_side = lax.ppermute(a_own, "tile", swap_tile)
    w_next_side = lax.ppermute(w_next, "tile", swap_tile)
    a_next_side = lax.ppermute(a_next, "tile", swap_tile)
    keep, send = pl.pallas_call(
        gather_kernel,
        out_shape=(jax.ShapeDtypeStruct((2, half, side), jnp.float32), block),
        in_specs=[vmem] * 8,
        out_specs=(vmem,) * 2,
        compiler_params=pltpu.CompilerParams(vmem_limit_bytes=32 * 1024 * 1024),
        name="masked_sums",
    )(wave_own, w_side, w_next, w_next_side, a_own, a_side, a_next, a_next_side)
    got = lax.ppermute(send, "probe", z2)
    return (keep + got.astype(jnp.float32))[:, None]


def times(a, b, spec):
    return jnp.einsum(spec, a, b, precision=lax.Precision.HIGHEST)


def back_propagate(field):
    side = field.shape[-1]
    table = jnp.asarray(propagator(side)).astype(jnp.float32).reshape(2, 2, side, side)
    real, imag = table[0] + table[1]
    for spec in ("kn,pnm->pkm", "mk,pnm->pnk"):
        fr, fi = field[:, 0], field[:, 1]
        field = jnp.stack(
            [times(real, fr, spec) - times(imag, fi, spec), times(real, fi, spec) + times(imag, fr, spec)], 1
        )
    return field


def any_slices(stored_waves, transmission, residual, offsets, slot_position):
    slot_count, side = stored_waves.shape[1], stored_waves.shape[-1]
    depth_count, depth_index = lax.axis_size("depth"), lax.axis_index("depth")
    waves = stored_waves[0].astype(jnp.float32)
    layers = transmission[0].astype(jnp.float32)

    def conj_times(a, b):
        return jnp.stack([a[:, 0] * b[:, 0] + a[:, 1] * b[:, 1], a[:, 0] * b[:, 1] - a[:, 1] * b[:, 0]], 1)

    adjoint = residual
    for turn in range(1, depth_count):
        handed = conj_times(layers, adjoint).astype(jnp.bfloat16)
        got = lax.ppermute(handed, "depth", [(d, d - 1) for d in range(1, depth_count)])
        active = depth_index == depth_count - 1 - turn
        adjoint = lax.cond(active, lambda: back_propagate(got.astype(jnp.float32)), lambda: adjoint)
    gradient = jnp.moveaxis(conj_times(waves, adjoint), 1, 0)
    corners = offsets[slot_position]

    def add_patch(number, region):
        patch = lax.dynamic_index_in_dim(gradient, number, 1, keepdims=True)
        corner = (0, 0, corners[number, 0], corners[number, 1])
        current = lax.dynamic_slice(region, corner, patch.shape)
        return lax.dynamic_update_slice(region, current + patch, corner)

    region = lax.fori_loop(0, slot_count, add_patch, jnp.zeros((2, 1, OBJ, OBJ), jnp.float32))
    strips = lax.psum_scatter(region, "probe", scatter_dimension=2, tiled=True)
    return lax.psum_scatter(strips, "tile", scatter_dimension=3, tiled=True)


def solution(mesh):
    sizes = dict(mesh.shape)

    def per_device(stored_waves, *rest):
        small = (sizes["depth"], sizes["probe"], sizes["tile"], stored_waves.shape[1]) == (2, 4, 2, 1)
        return (two_slices if small else any_slices)(stored_waves, *rest)

    slots = ("groups", "probe", "tile")
    return jax.shard_map(
        per_device,
        mesh=mesh,
        in_specs=(
            P("depth", slots, None, None, None),
            P("depth", slots, None, None, None),
            P(slots, None, None, None),
            P("groups", None),
            P(slots),
        ),
        out_specs=P("groups", "depth", "probe", "tile"),
        check_vma=False,
    )
```

time: 117 us -> 30.3 us (0.26)
  waiting for transfers between devices: 75.4 us -> 14.3 us
  between operations: 14.1 us -> 0.69 us
  matrix products: 8.53 us -> 0 us
  starting transfers between devices: 1.32 us -> 8.6 us
  local copies, waits for them, and re-layouts: 8.98 us -> 4.07 us
  loops' own time: 4.1 us -> 0 us
  other arithmetic: 4.32 us -> 0.73 us
  Pallas kernels: 0 us -> 1.71 us
    reduce_scatter x2 -> x0, waiting for transfers between devices: 54.6 us -> none  [the longest x1 45 us: per_device(): strips = lax.psum_scatter(region, 'probe', scatter_dimension=2, tiled=True)]
    dot_general x16 -> x0, matrix products: 8.53 us -> none  [the longest x8 4.81 us: right_apply(): jnp.einsum('pnm,mk->pnk', field, matrix, precision=lax.Precision.HIGHEST)]
    ppermute x1 -> x8, starting transfers between devices: 1.28 us -> 8.6 us  [the longest x1 3.09 us: two_slices(): w_next = lax.ppermute(wave_other, 'probe', z1)]
    dynamic_update_slice x1 -> x0, local copies, waits for them, and re-layouts: 6.76 us -> none  [add_patch(): return lax.dynamic_update_slice(region, current + patch_value, corner)]
    ppermute x1 -> x8, waiting for transfers between devices: 20.8 us -> 14.3 us  [the longest x1 6.67 us: two_slices(): got = lax.ppermute(send, 'probe', z2)]
    another operation x3 -> x0, loops' own time: 4.1 us -> none  [the longest x2 3.99 us: one_turn(): lax.cond(active, lambda: advance(incoming, region, front_size), lambda: (...]
    unnamed x0 -> x11, local copies, waits for them, and re-layouts: none -> 4.07 us
    sin x2 -> x0, other arithmetic: 2.04 us -> none  [the longest x1 1.03 us: dft_tables(): jnp.sin(angle)]
  transfers between devices with their start and end apart: 3 -> 8, of which waited for: 3 -> 6; matrix products, arithmetic and copies ran while one was open for 0% -> 0% of each run, Pallas kernels for 0% -> 0%
where the time goes in v1:
time: 30.3 us; the launch traced here: 30.1 us
  waiting for transfers between devices  14.3 us (47%)
  starting transfers between devices  8.6 us (28%)
  local copies, waits for them, and re-layouts  4.07 us (13%)
  Pallas kernels  1.71 us (6%)
  other arithmetic  0.73 us (2%)
  between operations  0.69 us (2%)
    ppermute x1, waiting for transfers between devices, two_slices(): got = lax.ppermute(send, 'probe', z2)  6.67 us
    ppermute x1, waiting for transfers between devices, two_slices(): a_own = lax.ppermute(adj_own, ('probe', 'depth'), flip)  4.27 us
    unnamed x11, local copies, waits for them, and re-layouts  4.07 us
    ppermute x1, starting transfers between devices, two_slices(): w_next = lax.ppermute(wave_other, 'probe', z1)  3.09 us
    ppermute x1, starting transfers between devices, two_slices(): a_own = lax.ppermute(adj_own, ('probe', 'depth'), flip)  2.84 us
    ppermute x1, starting transfers between devices, two_slices(): got = lax.ppermute(send, 'probe', z2)  2.65 us
    pallas_call x1, Pallas kernels, two_slices(): pl.pallas_call(send_kernel, out_shape=(block, block, tailed, tailed), in_...  1.18 us
    ppermute x1, waiting for transfers between devices, two_slices(): w_next = lax.ppermute(wave_other, 'probe', z1)  1 us
  transfers between devices with their start and end apart: 8, of which 6 were waited for; matrix products, arithmetic and copies ran while one was open for 0% of the time, Pallas kernels for 0%

profile of v1, /device:TPU:0, one launch (start us, length us, event | category | flops | bytes accessed | tf_op | source)
XLA Modules:
  0.0 30.1 jit_solution(3032637394986428399)
XLA Ops:
  0.0 0.0 copy-start.4
  0.7 0.0 copy-done.4
  0.7 0.1 copy.7.offsets_ref
  0.8 0.0 copy-start
  0.8 1.0 %copy-done = f32[1,2,256,256]{3,2,1,0:T(8,128)S(1)} copy-done((f32[1,2,256,256]{3,2,1,0:T(8,128)S(1)}, f32[1,2,256,256]{3,2,1,0:T(8,128)}, u32[]{:S(2)}) %copy-start) | copy-done | bytes 524312
  1.8 0.0 copy-start.1
  1.8 1.0 %copy-done.1 = bf16[1024,256]{1,0:T(8,128)(2,1)S(1)} copy-done((bf16[1024,256]{1,0:T(8,128)(2,1)S(1)}, bf16[1024,256]{1,0:T(8,128)(2,1)}, u32[]{:S(2)}) %copy-start.1) | copy-done | bytes 524312
  2.8 0.0 copy-start.2
  2.8 0.9 %copy-done.2 = bf16[1,1,2,256,256]{4,3,2,1,0:T(8,128)(2,1)S(1)} copy-done((bf16[1,1,2,256,256]{4,3,2,1,0:T(8,128)(2,1)S(1)}, bf16[1,1,2,256,256]{4,3,2,1,0:T(8,128)(2,1)}, u32[]{:S(2)}) %copy-start.2) | copy-done | bytes 262168
  3.8 0.0 copy-start.3
  3.8 0.9 %copy-done.3 = bf16[1,1,2,256,256]{4,3,2,1,0:T(8,128)(2,1)S(1)} copy-done((bf16[1,1,2,256,256]{4,3,2,1,0:T(8,128)(2,1)S(1)}, bf16[1,1,2,256,256]{4,3,2,1,0:T(8,128)(2,1)}, u32[]{:S(2)}) %copy-start.3) | copy-done | bytes 262168
  4.7 1.2 %adjoint_and_rolls.1 = (bf16[2,128,256]{2,1,0:T(8,128)(2,1)S(1)}, bf16[2,128,256]{2,1,0:T(8,128)(2,1)S(1)}, bf16[2,144,256]{2,1,0:T(8,128)(2,1)S(1)}, bf16[2,144,256]{2,1,0:T(8,128)(2,1)S(1)}) custom-call(s32[1]{0:T(128)S(6)} %copy.9.slot_ref, s32[8,2]{1,0:T(8,128)S(1)} %copy.7.offsets_ref, bf16[1024,256]{1,0:T(8,128)(2,1)S(1)} %copy-done.1, ...), custom_call_target="tpu_custom_call" | custom-call | tf_op jit(solution)/shard_map/adjoint_and_rolls/pallas_call | solution.py:145
  5.9 3.1 %collective-permute-start.1 = (bf16[2,144,256]{2,1,0:T(8,128)(2,1)S(1)}, bf16[2,144,256]{2,1,0:T(8,128)(2,1)S(1)}, u32[]{:S(2)}, u32[]{:S(2)}) collective-permute-start(bf16[2,144,256]{2,1,0:T(8,128)(2,1)S(1)} %get-tuple-element.12), channel_id=1, source_target_pairs={{0,4},{4,0},{8,12},{12,8},{1,5},{5,1},{9,13},{13,9},{2,6},{6,2},{1... | collective-permute-start | bytes 442376 | tf_op jit(solution)/shard_map/ppermute | solution.py:163
  9.0 2.8 %collective-permute-start.3 = (bf16[2,128,256]{2,1,0:T(8,128)(2,1)S(1)}, bf16[2,128,256]{2,1,0:T(8,128)(2,1)S(1)}, u32[]{:S(2)}, u32[]{:S(2)}) collective-permute-start(bf16[2,128,256]{2,1,0:T(8,128)(2,1)S(1)} %get-tuple-element.13), channel_id=1, source_target_pairs={{0,2},{2,0},{4,6},{6,4},{8,10},{10,8},{12,14},{14,12},{1,3},{3,1},... | collective-permute-start | bytes 393224 | tf_op jit(solution)/shard_map/ppermute | solution.py:161
  11.9 0.0 collective-permute-start.5
  11.9 0.0 collective-permute-start
  11.9 1.0 %collective-permute-done.1.w2 = bf16[2,144,256]{2,1,0:T(8,128)(2,1)S(1)} collective-permute-done((bf16[2,144,256]{2,1,0:T(8,128)(2,1)S(1)}, bf16[2,144,256]{2,1,0:T(8,128)(2,1)S(1)}, u32[]{:S(2)}, u32[]{:S(2)}) %collective-permute-start.1) | collective-permute-done | bytes 147488 | tf_op jit(solution)/shard_map/ppermute | solution.py:163
  12.9 0.0 collective-permute-start.2
  12.9 4.3 %collective-permute-done.3.a0 = bf16[2,128,256]{2,1,0:T(8,128)(2,1)S(1)} collective-permute-done((bf16[2,128,256]{2,1,0:T(8,128)(2,1)S(1)}, bf16[2,128,256]{2,1,0:T(8,128)(2,1)S(1)}, u32[]{:S(2)}, u32[]{:S(2)}) %collective-permute-start.3) | collective-permute-done | bytes 131104 | tf_op jit(solution)/shard_map/ppermute | solution.py:161
  17.1 0.0 collective-permute-start.4
  17.2 1.0 %collective-permute-done.5.a2 = bf16[2,128,256]{2,1,0:T(8,128)(2,1)S(1)} collective-permute-done((bf16[2,128,256]{2,1,0:T(8,128)(2,1)S(1)}, bf16[2,128,256]{2,1,0:T(8,128)(2,1)S(1)}, u32[]{:S(2)}, u32[]{:S(2)}) %collective-permute-start.5) | collective-permute-done | bytes 131104 | tf_op jit(solution)/shard_map/ppermute | solution.py:162
  18.1 0.0 collective-permute-start.6
  18.1 0.0 collective-permute-done.w1
  18.1 0.4 %collective-permute-done.4.a1 = bf16[2,128,256]{2,1,0:T(8,128)(2,1)S(1)} collective-permute-done((bf16[2,128,256]{2,1,0:T(8,128)(2,1)S(1)}, bf16[2,128,256]{2,1,0:T(8,128)(2,1)S(1)}, u32[]{:S(2)}, u32[]{:S(2)}) %collective-permute-start.4) | collective-permute-done | bytes 131104 | tf_op jit(solution)/shard_map/ppermute | solution.py:165
  18.5 1.0 %collective-permute-done.6.a3 = bf16[2,128,256]{2,1,0:T(8,128)(2,1)S(1)} collective-permute-done((bf16[2,128,256]{2,1,0:T(8,128)(2,1)S(1)}, bf16[2,128,256]{2,1,0:T(8,128)(2,1)S(1)}, u32[]{:S(2)}, u32[]{:S(2)}) %collective-permute-start.6) | collective-permute-done | bytes 131104 | tf_op jit(solution)/shard_map/ppermute | solution.py:167
  19.5 0.0 collective-permute-done.2.w3
  19.5 0.5 %masked_sums.1 = (f32[2,128,256]{2,1,0:T(8,128)S(1)}, bf16[2,128,256]{2,1,0:T(8,128)(2,1)S(1)}) custom-call(bf16[2,144,256]{2,1,0:T(8,128)(2,1)S(1)} %get-tuple-element.11.w0, bf16[2,144,256]{2,1,0:T(8,128)(2,1)S(1)} %collective-permute-done.w1, bf16[2,144,256]{2,1,0:T(8,128)(2,1)S(1)} %collective-permute-done.1.w2, ...), custom_call_target="tpu_custom_call" | custom-call | tf_op jit(solution)/shard_map/masked_sums/pallas_call | solution.py:168
  20.0 2.7 %collective-permute-start.7 = (bf16[2,128,256]{2,1,0:T(8,128)(2,1)S(1)}, bf16[2,128,256]{2,1,0:T(8,128)(2,1)S(1)}, u32[]{:S(2)}, u32[]{:S(2)}) collective-permute-start(bf16[2,128,256]{2,1,0:T(8,128)(2,1)S(1)} %get-tuple-element.16), channel_id=1, source_target_pairs={{0,8},{4,12},{8,0},{12,4},{1,9},{5,13},{9,1},{13,5},{2,10},{6,14},... | collective-permute-start | bytes 393224 | tf_op jit(solution)/shard_map/ppermute | solution.py:176
  22.7 6.7 %collective-permute-done.7 = bf16[2,128,256]{2,1,0:T(8,128)(2,1)S(1)} collective-permute-done((bf16[2,128,256]{2,1,0:T(8,128)(2,1)S(1)}, bf16[2,128,256]{2,1,0:T(8,128)(2,1)S(1)}, u32[]{:S(2)}, u32[]{:S(2)}) %collective-permute-start.7) | collective-permute-done | bytes 131104 | tf_op jit(solution)/shard_map/ppermute | solution.py:176
  29.3 0.7 %add_bitcast_fusion = f32[2,1,128,256]{3,2,1,0:T(8,128)} fusion(f32[2,128,256]{2,1,0:T(8,128)S(1)} %get-tuple-element.15, bf16[2,128,256]{2,1,0:T(8,128)(2,1)S(1)} %collective-permute-done.7), kind=kLoop, calls=%fused_computation | loop fusion | flops 131072 | bytes 655360 | tf_op jit(solution)/shard_map/broadcast_in_dim | solution.py:177
Async XLA Ops:
  0.0 0.7 %copy-start.4 = (s32[8,2]{0,1:T(2,128)S(1)}, s32[8,2]{0,1:T(2,128)}, u32[]{:S(2)}) copy-start(s32[8,2]{0,1:T(2,128)} %param.9) | copy-start | bytes 196
  0.8 1.0 %copy-start = (f32[1,2,256,256]{3,2,1,0:T(8,128)S(1)}, f32[1,2,256,256]{3,2,1,0:T(8,128)}, u32[]{:S(2)}) copy-start(f32[1,2,256,256]{3,2,1,0:T(8,128)} %param.8) | copy-start | bytes 1572868
  1.8 1.0 %copy-start.1 = (bf16[1024,256]{1,0:T(8,128)(2,1)S(1)}, bf16[1024,256]{1,0:T(8,128)(2,1)}, u32[]{:S(2)}) copy-start(bf16[1024,256]{1,0:T(8,128)(2,1)} %constant.2.clone.table_ref) | copy-start | bytes 1572868
  2.8 0.9 %copy-start.2 = (bf16[1,1,2,256,256]{4,3,2,1,0:T(8,128)(2,1)S(1)}, bf16[1,1,2,256,256]{4,3,2,1,0:T(8,128)(2,1)}, u32[]{:S(2)}) copy-start(bf16[1,1,2,256,256]{4,3,2,1,0:T(8,128)(2,1)} %param.6) | copy-start | bytes 786436
  3.8 0.9 %copy-start.3 = (bf16[1,1,2,256,256]{4,3,2,1,0:T(8,128)(2,1)S(1)}, bf16[1,1,2,256,256]{4,3,2,1,0:T(8,128)(2,1)}, u32[]{:S(2)}) copy-start(bf16[1,1,2,256,256]{4,3,2,1,0:T(8,128)(2,1)} %param.7) | copy-start | bytes 786436
  5.9 6.9 %collective-permute-start.1 = (bf16[2,144,256]{2,1,0:T(8,128)(2,1)S(1)}, bf16[2,144,256]{2,1,0:T(8,128)(2,1)S(1)}, u32[]{:S(2)}, u32[]{:S(2)}) collective-permute-start(bf16[2,144,256]{2,1,0:T(8,128)(2,1)S(1)} %get-tuple-element.12), channel_id=1, source_target_pairs={{0,4},{4,0},{8,12},{12,8},{1,5},{5,1},{9,13},{13,9},{2,6},{6,2},{1... | collective-permute-start | bytes 442376 | tf_op jit(solution)/shard_map/ppermute | solution.py:163
  9.0 8.1 %collective-permute-start.3 = (bf16[2,128,256]{2,1,0:T(8,128)(2,1)S(1)}, bf16[2,128,256]{2,1,0:T(8,128)(2,1)S(1)}, u32[]{:S(2)}, u32[]{:S(2)}) collective-permute-start(bf16[2,128,256]{2,1,0:T(8,128)(2,1)S(1)} %get-tuple-element.13), channel_id=1, source_target_pairs={{0,2},{2,0},{4,6},{6,4},{8,10},{10,8},{12,14},{14,12},{1,3},{3,1},... | collective-permute-start | bytes 393224 | tf_op jit(solution)/shard_map/ppermute | solution.py:161
  11.9 6.3 %collective-permute-start.5 = (bf16[2,128,256]{2,1,0:T(8,128)(2,1)S(1)}, bf16[2,128,256]{2,1,0:T(8,128)(2,1)S(1)}, u32[]{:S(2)}, u32[]{:S(2)}) collective-permute-start(bf16[2,128,256]{2,1,0:T(8,128)(2,1)S(1)} %get-tuple-element.14), channel_id=1, source_target_pairs={{0,6},{2,4},{4,2},{6,0},{8,14},{10,12},{12,10},{14,8},{1,7},{3,5},... | collective-permute-start | bytes 393224 | tf_op jit(solution)/shard_map/ppermute | solution.py:162
  11.9 6.3 %collective-permute-start = (bf16[2,144,256]{2,1,0:T(8,128)(2,1)S(1)}, bf16[2,144,256]{2,1,0:T(8,128)(2,1)S(1)}, u32[]{:S(2)}, u32[]{:S(2)}) collective-permute-start(bf16[2,144,256]{2,1,0:T(8,128)(2,1)S(1)} %get-tuple-element.11.w0), channel_id=1, source_target_pairs={{0,1},{1,0},{2,3},{3,2},{4,5},{5,4},{6,7},{7,6},{8,9},{9,8},{10,11... | collective-permute-start | bytes 442376 | tf_op jit(solution)/shard_map/ppermute | solution.py:164
  12.9 6.6 %collective-permute-start.2 = (bf16[2,144,256]{2,1,0:T(8,128)(2,1)S(1)}, bf16[2,144,256]{2,1,0:T(8,128)(2,1)S(1)}, u32[]{:S(2)}, u32[]{:S(2)}) collective-permute-start(bf16[2,144,256]{2,1,0:T(8,128)(2,1)S(1)} %collective-permute-done.1.w2), channel_id=1, source_target_pairs={{0,1},{1,0},{2,3},{3,2},{4,5},{5,4},{6,7},{7,6},{8,9},{9,8},{10,11... | collective-permute-start | bytes 442376 | tf_op jit(solution)/shard_map/ppermute | solution.py:166
  17.1 1.3 %collective-permute-start.4 = (bf16[2,128,256]{2,1,0:T(8,128)(2,1)S(1)}, bf16[2,128,256]{2,1,0:T(8,128)(2,1)S(1)}, u32[]{:S(2)}, u32[]{:S(2)}) collective-permute-start(bf16[2,128,256]{2,1,0:T(8,128)(2,1)S(1)} %collective-permute-done.3.a0), channel_id=1, source_target_pairs={{0,1},{1,0},{2,3},{3,2},{4,5},{5,4},{6,7},{7,6},{8,9},{9,8},{10,11... | collective-permute-start | bytes 393224 | tf_op jit(solution)/shard_map/ppermute | solution.py:165
  18.1 1.3 %collective-permute-start.6 = (bf16[2,128,256]{2,1,0:T(8,128)(2,1)S(1)}, bf16[2,128,256]{2,1,0:T(8,128)(2,1)S(1)}, u32[]{:S(2)}, u32[]{:S(2)}) collective-permute-start(bf16[2,128,256]{2,1,0:T(8,128)(2,1)S(1)} %collective-permute-done.5.a2), channel_id=1, source_target_pairs={{0,1},{1,0},{2,3},{3,2},{4,5},{5,4},{6,7},{7,6},{8,9},{9,8},{10,11... | collective-permute-start | bytes 393224 | tf_op jit(solution)/shard_map/ppermute | solution.py:167
  20.0 9.3 %collective-permute-start.7 = (bf16[2,128,256]{2,1,0:T(8,128)(2,1)S(1)}, bf16[2,128,256]{2,1,0:T(8,128)(2,1)S(1)}, u32[]{:S(2)}, u32[]{:S(2)}) collective-permute-start(bf16[2,128,256]{2,1,0:T(8,128)(2,1)S(1)} %get-tuple-element.16), channel_id=1, source_target_pairs={{0,8},{4,12},{8,0},{12,4},{1,9},{5,13},{9,1},{13,5},{2,10},{6,14},... | collective-permute-start | bytes 393224 | tf_op jit(solution)/shard_map/ppermute | solution.py:176

commit v2 on v1

v2 whole, which is shorter than its diff:
```python
import functools
import math

import jax
import jax.numpy as jnp
import numpy as np
from jax import lax
from jax.experimental import pallas as pl
from jax.experimental.pallas import tpu as pltpu
from jax.sharding import PartitionSpec as P

OBJ = 512
TAIL = 16


def propagator(side):
    counter = np.arange(side)
    frequency = (counter + side // 2) % side - side // 2
    chirp = np.exp(0.5j * frequency.astype(np.float64) ** 2 / side)
    ring = np.fft.ifft(chirp)
    ring = 0.5 * (ring + ring[(-counter) % side])
    matrix = ring[(counter[:, None] - counter[None, :]) % side]
    return np.stack([matrix.real, matrix.imag]).astype(np.float32)


def mm(a, b):
    return jnp.dot(a, b, preferred_element_type=jnp.float32)


def split(x):
    high = x.astype(jnp.bfloat16)
    return high, (x - high.astype(jnp.float32)).astype(jnp.bfloat16)


def rolls(side, cy, cx):
    down = lax.broadcasted_iota(jnp.int32, (side, side), 0)
    along = lax.broadcasted_iota(jnp.int32, (side, side), 1)
    rows = (along == ((down - cy) & (side - 1))).astype(jnp.bfloat16)
    cols = (down == ((along - cx) & (side - 1))).astype(jnp.bfloat16)
    return rows, cols


def rolled(parts, rows, cols):
    side = rows.shape[0]
    moved = mm(jnp.concatenate(parts, axis=0), cols).astype(jnp.bfloat16)
    return [mm(rows, moved[n * side : (n + 1) * side]).astype(jnp.bfloat16) for n in range(len(parts))]


def conj_times(a, b):
    return a[0] * b[0] + a[1] * b[1], a[0] * b[1] - a[1] * b[0]


def own_and_other(half):
    parity = lax.rem(lax.axis_index("probe"), 2)
    return (pl.ds(pl.multiple_of(n * half, half), half) for n in (parity, 1 - parity))


def send_kernel(
    slot_ref, offsets_hbm, table_hbm, layer_hbm, residual_hbm,
    own_ref, other_ref,
    offsets_ref, table_ref, layer_ref, residual_ref, sems,
):
    side = layer_ref.shape[-1]
    half = side // 2
    pairs = (
        (offsets_hbm, offsets_ref), (table_hbm, table_ref), (layer_hbm, layer_ref), (residual_hbm, residual_ref),
    )
    offsets_copy, table_copy, layer_copy, residual_copy = copies = [
        pltpu.make_async_copy(source, target, sems.at[n]) for n, (source, target) in enumerate(pairs)
    ]
    for copy in copies:
        copy.start()
    offsets_copy.wait()
    slot = slot_ref[0]
    cy, cx = offsets_ref[0, slot], offsets_ref[1, slot]
    parity = lax.rem(lax.axis_index("probe"), 2)
    down = (cy - parity * half) & (side - 1)
    line = lax.broadcasted_iota(jnp.int32, (TAIL, side), 0)
    tail = jnp.where(line == 0, cy.astype(jnp.float32), cx.astype(jnp.float32)).astype(jnp.bfloat16)
    own_ref[2 * half :] = tail
    other_ref[2 * half :] = tail
    top = lax.axis_index("depth") == 1

    def put(part, x):
        own_ref[part * half : (part + 1) * half] = x[:half]
        other_ref[part * half : (part + 1) * half] = x[half:]

    @pl.when(top)
    def _():
        table_copy.wait()
        (rhr, rlr), (rhi, rli) = (split(pltpu.roll(table_ref[n], cx, 1)) for n in range(2))
        (lhr, llr), (lhi, lli) = (split(pltpu.roll(table_ref[n], (side - down) & (side - 1), 1)) for n in range(2))
        layer_copy.wait()
        residual_copy.wait()
        layer = layer_ref[0].astype(jnp.float32), layer_ref[1].astype(jnp.float32)
        handed = conj_times(layer, (residual_ref[0], residual_ref[1]))
        vr, vi = (x.astype(jnp.bfloat16) for x in handed)
        field = jnp.concatenate([vr, vr, vi, vi], axis=1)
        middle = (
            mm(field, jnp.concatenate([rlr, rhr, -rli, -rhi], axis=0)),
            mm(field, jnp.concatenate([rli, rhi, rlr, rhr], axis=0)),
        )
        (mhr, mlr), (mhi, mli) = map(split, middle)
        field = jnp.concatenate([mlr, mhr, mhr, mli, mhi, mhi], axis=0)
        for part, x in enumerate(([lhr, llr, lhr, -lhi, -lli, -lhi], [lhi, lli, lhi, lhr, llr, lhr])):
            put(part, mm(jnp.concatenate(x, axis=1), field).astype(jnp.bfloat16))

    @pl.when(jnp.logical_not(top))
    def _():
        for copy in (layer_copy, residual_copy, table_copy):
            copy.wait()
        rows, cols = rolls(side, down, cx)
        for part, x in enumerate(rolled([residual_ref[n].astype(jnp.bfloat16) for n in range(2)], rows, cols)):
            put(part, x)


def sums_kernel(a0, a1, w0, w1, keep_ref, send_ref, side_keep_ref, side_send_ref):
    side = w0.shape[-1]
    half = side // 2
    place = lax.axis_index("probe")
    upper = place >= 2
    right = lax.axis_index("tile") == 1
    parity = lax.rem(place, 2)
    down = lax.broadcasted_iota(jnp.int32, (half, side), 0) + parity * half
    along = lax.broadcasted_iota(jnp.int32, (half, side), 1)
    every = lax.broadcasted_iota(jnp.int32, (side, side), 0)
    across = lax.broadcasted_iota(jnp.int32, (side, side), 1)
    zero = jnp.zeros((half, side), jnp.float32)
    slots = []
    for w, a in ((w0, a0), (w1, a1)):
        tail = a[2 * half :].astype(jnp.float32)
        cy, cx = tail[0:1].astype(jnp.int32), tail[1:2].astype(jnp.int32)
        rows = (along == ((down - cy) & (side - 1))).astype(jnp.bfloat16)
        cols = (every == ((across - cx) & (side - 1))).astype(jnp.bfloat16)
        moved = mm(rows, jnp.concatenate([w[0], w[1]], axis=1)).astype(jnp.bfloat16)
        moved = mm(jnp.concatenate([moved[:, :side], moved[:, side:]], axis=0), cols)
        wave = moved[:half], moved[half:]
        adjoint = a[:half].astype(jnp.float32), a[half : 2 * half].astype(jnp.float32)
        slots.append((conj_times(wave, adjoint), (down < cy) == upper, (along < cx) == right))
    for part in range(2):
        for ref, near, here in (
            (keep_ref, True, True), (send_ref, False, True), (side_keep_ref, True, False), (side_send_ref, False, False),
        ):
            total = zero
            for gradient, mine, own in slots:
                chosen = jnp.logical_and(mine if near else ~mine, own if here else ~own)
                total = total + jnp.where(chosen, gradient[part], zero)
            ref[part] = total.astype(ref.dtype)


def in_hbm(*arrays):
    return [pltpu.with_memory_space_constraint(x, pltpu.HBM) for x in arrays]


def two_slices(stored_waves, transmission, residual, offsets, slot_position):
    side = stored_waves.shape[-1]
    half = side // 2
    table = jnp.asarray(propagator(side))
    vmem, smem, hbm = (pl.BlockSpec(memory_space=m) for m in (pltpu.VMEM, pltpu.SMEM, pltpu.HBM))
    block, sums = (jax.ShapeDtypeStruct((2, half, side), t) for t in (jnp.bfloat16, jnp.float32))
    tailed = jax.ShapeDtypeStruct((2 * half + TAIL, side), jnp.bfloat16)
    params = pltpu.CompilerParams(vmem_limit_bytes=32 * 1024 * 1024)
    by_column = offsets.T
    waves = stored_waves[0, 0]
    adj_own, adj_other = pl.pallas_call(
        send_kernel,
        out_shape=(tailed, tailed),
        in_specs=[smem] + [hbm] * 4,
        out_specs=(vmem,) * 2,
        scratch_shapes=[
            pltpu.SMEM(by_column.shape, jnp.int32),
            pltpu.VMEM(table.shape, jnp.float32),
            pltpu.VMEM((2, side, side), jnp.bfloat16),
            pltpu.VMEM((2, side, side), jnp.float32),
            pltpu.SemaphoreType.DMA((4,)),
        ],
        compiler_params=params,
        name="adjoint",
    )(slot_position, *in_hbm(by_column, table, transmission[0, 0], residual[0]))

    probe_count = lax.axis_size("probe")
    swap_tile = [(0, 1), (1, 0)]
    flip = [(2 * z + d, 2 * z + 1 - d) for z in range(probe_count) for d in range(2)]
    flip_z1 = [(2 * z + d, 2 * (z ^ 1) + 1 - d) for z in range(probe_count) for d in range(2)]
    z1 = [(z, z ^ 1) for z in range(probe_count)]
    z2 = [(z, z ^ 2) for z in range(probe_count)]
    a_own = lax.ppermute(adj_own, ("probe", "depth"), flip)
    a_next = lax.ppermute(adj_other, ("probe", "depth"), flip_z1)
    w_next = lax.ppermute(waves, "probe", z1)
    keep, send, side_keep, side_send = pl.pallas_call(
        sums_kernel,
        out_shape=(sums, sums, block, block),
        in_specs=[vmem] * 4,
        out_specs=(vmem,) * 4,
        compiler_params=params,
        name="masked_sums",
    )(a_own, a_next, waves, w_next)
    send = send + lax.ppermute(side_send, "tile", swap_tile).astype(jnp.float32)
    got = lax.ppermute(send.astype(jnp.bfloat16), "probe", z2)
    keep = keep + lax.ppermute(side_keep, "tile", swap_tile).astype(jnp.float32)
    return (keep + got.astype(jnp.float32))[:, None]


def times(a, b, spec):
    return jnp.einsum(spec, a, b, precision=lax.Precision.HIGHEST)


def back_propagate(field):
    side = field.shape[-1]
    real, imag = jnp.asarray(propagator(side))
    for spec in ("kn,pnm->pkm", "mk,pnm->pnk"):
        fr, fi = field[:, 0], field[:, 1]
        field = jnp.stack(
            [times(real, fr, spec) - times(imag, fi, spec), times(real, fi, spec) + times(imag, fr, spec)], 1
        )
    return field


def any_slices(stored_waves, transmission, residual, offsets, slot_position):
    slot_count, side = stored_waves.shape[1], stored_waves.shape[-1]
    depth_count, depth_index = lax.axis_size("depth"), lax.axis_index("depth")
    waves = stored_waves[0].astype(jnp.float32)
    layers = transmission[0].astype(jnp.float32)

    def product(a, b):
        return jnp.stack(conj_times((a[:, 0], a[:, 1]), (b[:, 0], b[:, 1])), 1)

    adjoint = residual
    for turn in range(1, depth_count):
        handed = product(layers, adjoint).astype(jnp.bfloat16)
        got = lax.ppermute(handed, "depth", [(d, d - 1) for d in range(1, depth_count)])
        active = depth_index == depth_count - 1 - turn
        adjoint = lax.cond(active, lambda: back_propagate(got.astype(jnp.float32)), lambda: adjoint)
    gradient = jnp.moveaxis(product(waves, adjoint), 1, 0)
    corners = offsets[slot_position]

    def add_patch(number, region):
        patch = lax.dynamic_index_in_dim(gradient, number, 1, keepdims=True)
        corner = (0, 0, corners[number, 0], corners[number, 1])
        current = lax.dynamic_slice(region, corner, patch.shape)
        return lax.dynamic_update_slice(region, current + patch, corner)

    region = lax.fori_loop(0, slot_count, add_patch, jnp.zeros((2, 1, OBJ, OBJ), jnp.float32))
    strips = lax.psum_scatter(region, "probe", scatter_dimension=2, tiled=True)
    return lax.psum_scatter(strips, "tile", scatter_dimension=3, tiled=True)


def solution(mesh):
    sizes = dict(mesh.shape)

    def per_device(stored_waves, *rest):
        small = (sizes["depth"], sizes["probe"], sizes["tile"], stored_waves.shape[1]) == (2, 4, 2, 1)
        return (two_slices if small else any_slices)(stored_waves, *rest)

    slots = ("groups", "probe", "tile")
    return jax.shard_map(
        per_device,
        mesh=mesh,
        in_specs=(
            P("depth", slots, None, None, None),
            P("depth", slots, None, None, None),
            P(slots, None, None, None),
            P("groups", None),
            P(slots),
        ),
        out_specs=P("groups", "depth", "probe", "tile"),
        check_vma=False,
    )
```

time: 30.3 us -> 26.4 us (0.87)
  local copies, waits for them, and re-layouts: 4.07 us -> 0.01 us
  Pallas kernels: 1.71 us -> 2.49 us
  waiting for transfers between devices: 14.3 us -> 13.9 us
    unnamed x11 -> x2, local copies, waits for them, and re-layouts: 4.07 us -> 0.01 us
    ppermute x1, waiting for transfers between devices: 4.27 us -> 6.37 us  [two_slices(): a_own = lax.ppermute(adj_own, ('probe', 'depth'), flip)]
    ppermute x6 -> x4, waiting for transfers between devices: 9.02 us -> 7.51 us  [the longest x1 6.67 us: two_slices(): got = lax.ppermute(send.astype(jnp.bfloat16), 'probe', z2)]
    ppermute x1, waiting for transfers between devices: 0.97 us -> 0.01 us  [two_slices(): a_next = lax.ppermute(adj_other, ('probe', 'depth'), flip_z1)]
    pallas_call x2, Pallas kernels: 1.71 us -> 2.49 us  [the longest x1 1.83 us: two_slices(): pl.pallas_call(send_kernel, out_shape=(tailed, tailed), in_specs=[smem] +...]
    ppermute x1, starting transfers between devices: 2.84 us -> 2.19 us  [two_slices(): a_own = lax.ppermute(adj_own, ('probe', 'depth'), flip)]
    ppermute x6 -> x4, starting transfers between devices: 5.75 us -> 6.24 us  [the longest x1 3.02 us: two_slices(): w_next = lax.ppermute(waves, 'probe', z1)]
  transfers between devices with their start and end apart: 8 -> 6, of which waited for: 6 -> 3; matrix products, arithmetic and copies ran while one was open for 0% -> 0% of each run, Pallas kernels for 0% -> 7%
where the time goes in v2:
time: 26.4 us; the launch traced here: 26.3 us
  waiting for transfers between devices  13.9 us (53%)
  starting transfers between devices  8.44 us (32%)
  Pallas kernels  2.49 us (9%)
  other arithmetic  0.78 us (3%)
  between operations  0.7 us (3%)
    ppermute x1, waiting for transfers between devices, two_slices(): got = lax.ppermute(send.astype(jnp.bfloat16), 'probe', z2)  6.67 us
    ppermute x1, waiting for transfers between devices, two_slices(): a_own = lax.ppermute(adj_own, ('probe', 'depth'), flip)  6.37 us
    ppermute x1, starting transfers between devices, two_slices(): w_next = lax.ppermute(waves, 'probe', z1)  3.02 us
    ppermute x1, starting transfers between devices, two_slices(): got = lax.ppermute(send.astype(jnp.bfloat16), 'probe', z2)  2.65 us
    ppermute x1, starting transfers between devices, two_slices(): a_own = lax.ppermute(adj_own, ('probe', 'depth'), flip)  2.19 us
    pallas_call x1, Pallas kernels, two_slices(): pl.pallas_call(send_kernel, out_shape=(tailed, tailed), in_specs=[smem] +...  1.83 us
    ppermute x1, waiting for transfers between devices, two_slices(): send = send + lax.ppermute(side_send, 'tile', swap_tile).astype(jnp.float32)  0.84 us
    broadcast_in_dim x1, other arithmetic, two_slices(): return (keep + got.astype(jnp.float32))[:, None]  0.75 us
  transfers between devices with their start and end apart: 6, of which 3 were waited for; matrix products, arithmetic and copies ran while one was open for 0% of the time, Pallas kernels for 7%

profile of v2, /device:TPU:0, one launch (start us, length us, event | category | flops | bytes accessed | tf_op | source)
XLA Modules:
  0.0 26.3 jit_solution(5882107716790998572)
XLA Ops:
  0.0 3.0 %collective-permute-start.2 = (bf16[2,256,256]{2,1,0:T(8,128)(2,1)}, bf16[2,256,256]{2,1,0:T(8,128)(2,1)S(1)}, u32[]{:S(2)}, u32[]{:S(2)}) collective-permute-start(bf16[2,256,256]{2,1,0:T(8,128)(2,1)} %bitcast.8), channel_id=1, source_target_pairs={{0,4},{4,0},{8,12},{12,8},{1,5},{5,1},{9,13},{13,9},{2,6},{6,2},{1... | collective-permute-start | bytes 786440 | tf_op jit(solution)/shard_map/ppermute | solution.py:189
  3.7 0.0 copy-start
  3.7 1.8 %adjoint.1 = (bf16[272,256]{1,0:T(8,128)(2,1)S(1)}, bf16[272,256]{1,0:T(8,128)(2,1)S(1)}) custom-call(s32[1]{0:T(128)S(6)} %copy.8.slot_ref, s32[2,8]{1,0:T(2,128)} %bitcast.12, f32[2,256,256]{2,1,0:T(8,128)} %constant.2.clone.table_hbm, bf16[2,256,256]{2,1,0:T(8,128)(2,1)} %bitcast.11, f32[2,256,256]{2,1,0:T(8,128)} %bitcast.10), custom_call_target="tpu_custom_call" | custom-call | tf_op jit(solution)/shard_map/adjoint/pallas_call | solution.py:165
  5.5 2.2 %collective-permute-start = (bf16[272,256]{1,0:T(8,128)(2,1)S(1)}, bf16[272,256]{1,0:T(8,128)(2,1)S(1)}, u32[]{:S(2)}, u32[]{:S(2)}) collective-permute-start(bf16[272,256]{1,0:T(8,128)(2,1)S(1)} %get-tuple-element.11), channel_id=1, source_target_pairs={{0,2},{2,0},{4,6},{6,4},{8,10},{10,8},{12,14},{14,12},{1,3},{3,1},... | collective-permute-start | bytes 417800 | tf_op jit(solution)/shard_map/ppermute | solution.py:187
  7.7 0.0 collective-permute-start.1
  7.7 6.4 %collective-permute-done.a0 = bf16[272,256]{1,0:T(8,128)(2,1)S(1)} collective-permute-done((bf16[272,256]{1,0:T(8,128)(2,1)S(1)}, bf16[272,256]{1,0:T(8,128)(2,1)S(1)}, u32[]{:S(2)}, u32[]{:S(2)}) %collective-permute-start) | collective-permute-done | bytes 139296 | tf_op jit(solution)/shard_map/ppermute | solution.py:187
  14.1 0.0 collective-permute-done.1.a1
  14.1 0.0 collective-permute-done.2.w1
  14.1 0.0 copy-done
  14.1 0.7 %masked_sums.1 = (f32[2,128,256]{2,1,0:T(8,128)S(1)}, f32[2,128,256]{2,1,0:T(8,128)S(1)}, bf16[2,128,256]{2,1,0:T(8,128)(2,1)S(1)}, bf16[2,128,256]{2,1,0:T(8,128)(2,1)S(1)}) custom-call(bf16[272,256]{1,0:T(8,128)(2,1)S(1)} %collective-permute-done.a0, bf16[272,256]{1,0:T(8,128)(2,1)S(1)} %collective-permute-done.1.a1, bf16[2,256,256]{2,1,0:T(8,128)(2,1)S(1)} %bitcast.9, ...), custom_call_target="tpu_custom_call" | custom-call | tf_op jit(solution)/shard_map/masked_sums/pallas_call | solution.py:190
  14.8 0.1 collective-permute-start.4
  14.9 0.5 %collective-permute-start.3 = (bf16[2,128,256]{2,1,0:T(8,128)(2,1)S(1)}, bf16[2,128,256]{2,1,0:T(8,128)(2,1)S(1)}, u32[]{:S(2)}, u32[]{:S(2)}) collective-permute-start(bf16[2,128,256]{2,1,0:T(8,128)(2,1)S(1)} %get-tuple-element.14), channel_id=1, source_target_pairs={{0,1},{1,0},{2,3},{3,2},{4,5},{5,4},{6,7},{7,6},{8,9},{9,8},{10,11... | collective-permute-start | bytes 393224 | tf_op jit(solution)/shard_map/ppermute | solution.py:200
  15.4 0.8 %collective-permute-done.4 = bf16[2,128,256]{2,1,0:T(8,128)(2,1)S(1)} collective-permute-done((bf16[2,128,256]{2,1,0:T(8,128)(2,1)S(1)}, bf16[2,128,256]{2,1,0:T(8,128)(2,1)S(1)}, u32[]{:S(2)}, u32[]{:S(2)}) %collective-permute-start.4) | collective-permute-done | bytes 131104 | tf_op jit(solution)/shard_map/ppermute | solution.py:198
  16.2 2.7 %collective-permute-start.5 = (bf16[2,128,256]{2,1,0:T(8,128)(2,1)S(1)}, bf16[2,128,256]{2,1,0:T(8,128)(2,1)S(1)}, u32[]{:S(2)}, u32[]{:S(2)}) collective-permute-start(bf16[2,128,256]{2,1,0:T(8,128)(2,1)S(1)} %add_convert_fusion), channel_id=1, source_target_pairs={{0,8},{4,12},{8,0},{12,4},{1,9},{5,13},{9,1},{13,5},{2,10},{6,14},... | collective-permute-start | bytes 393224 | tf_op jit(solution)/shard_map/ppermute | solution.py:199
  18.9 0.0 collective-permute-done.3
  18.9 6.7 %collective-permute-done.5 = bf16[2,128,256]{2,1,0:T(8,128)(2,1)S(1)} collective-permute-done((bf16[2,128,256]{2,1,0:T(8,128)(2,1)S(1)}, bf16[2,128,256]{2,1,0:T(8,128)(2,1)S(1)}, u32[]{:S(2)}, u32[]{:S(2)}) %collective-permute-start.5) | collective-permute-done | bytes 131104 | tf_op jit(solution)/shard_map/ppermute | solution.py:199
  25.5 0.7 %add_bitcast_fusion = f32[2,1,128,256]{3,2,1,0:T(8,128)} fusion(bf16[2,128,256]{2,1,0:T(8,128)(2,1)S(1)} %collective-permute-done.5, f32[2,128,256]{2,1,0:T(8,128)S(1)} %get-tuple-element.13, bf16[2,128,256]{2,1,0:T(8,128)(2,1)S(1)} %collective-permute-done.3), kind=kLoop, calls=%fused_computation | loop fusion | flops 262144 | bytes 786432 | tf_op jit(solution)/shard_map/broadcast_in_dim | solution.py:201
  (1 shorter events, 0.0 us)
Async XLA Ops:
  0.0 14.1 %collective-permute-start.2 = (bf16[2,256,256]{2,1,0:T(8,128)(2,1)}, bf16[2,256,256]{2,1,0:T(8,128)(2,1)S(1)}, u32[]{:S(2)}, u32[]{:S(2)}) collective-permute-start(bf16[2,256,256]{2,1,0:T(8,128)(2,1)} %bitcast.8), channel_id=1, source_target_pairs={{0,4},{4,0},{8,12},{12,8},{1,5},{5,1},{9,13},{13,9},{2,6},{6,2},{1... | collective-permute-start | bytes 786440 | tf_op jit(solution)/shard_map/ppermute | solution.py:189
  3.7 10.4 %copy-start = (bf16[1,1,2,256,256]{4,3,2,1,0:T(8,128)(2,1)S(1)}, bf16[1,1,2,256,256]{4,3,2,1,0:T(8,128)(2,1)}, u32[]{:S(2)}) copy-start(bf16[1,1,2,256,256]{4,3,2,1,0:T(8,128)(2,1)} %param.6) | copy-start | bytes 786436
  5.5 8.6 %collective-permute-start = (bf16[272,256]{1,0:T(8,128)(2,1)S(1)}, bf16[272,256]{1,0:T(8,128)(2,1)S(1)}, u32[]{:S(2)}, u32[]{:S(2)}) collective-permute-start(bf16[272,256]{1,0:T(8,128)(2,1)S(1)} %get-tuple-element.11), channel_id=1, source_target_pairs={{0,2},{2,0},{4,6},{6,4},{8,10},{10,8},{12,14},{14,12},{1,3},{3,1},... | collective-permute-start | bytes 417800 | tf_op jit(solution)/shard_map/ppermute | solution.py:187
  7.7 6.4 %collective-permute-start.1 = (bf16[272,256]{1,0:T(8,128)(2,1)S(1)}, bf16[272,256]{1,0:T(8,128)(2,1)S(1)}, u32[]{:S(2)}, u32[]{:S(2)}) collective-permute-start(bf16[272,256]{1,0:T(8,128)(2,1)S(1)} %get-tuple-element.12), channel_id=1, source_target_pairs={{0,6},{2,4},{4,2},{6,0},{8,14},{10,12},{12,10},{14,8},{1,7},{3,5},... | collective-permute-start | bytes 417800 | tf_op jit(solution)/shard_map/ppermute | solution.py:188
  14.8 1.4 %collective-permute-start.4 = (bf16[2,128,256]{2,1,0:T(8,128)(2,1)S(1)}, bf16[2,128,256]{2,1,0:T(8,128)(2,1)S(1)}, u32[]{:S(2)}, u32[]{:S(2)}) collective-permute-start(bf16[2,128,256]{2,1,0:T(8,128)(2,1)S(1)} %get-tuple-element.16), channel_id=1, source_target_pairs={{0,1},{1,0},{2,3},{3,2},{4,5},{5,4},{6,7},{7,6},{8,9},{9,8},{10,11... | collective-permute-start | bytes 393224 | tf_op jit(solution)/shard_map/ppermute | solution.py:198
  14.9 4.0 %collective-permute-start.3 = (bf16[2,128,256]{2,1,0:T(8,128)(2,1)S(1)}, bf16[2,128,256]{2,1,0:T(8,128)(2,1)S(1)}, u32[]{:S(2)}, u32[]{:S(2)}) collective-permute-start(bf16[2,128,256]{2,1,0:T(8,128)(2,1)S(1)} %get-tuple-element.14), channel_id=1, source_target_pairs={{0,1},{1,0},{2,3},{3,2},{4,5},{5,4},{6,7},{7,6},{8,9},{9,8},{10,11... | collective-permute-start | bytes 393224 | tf_op jit(solution)/shard_map/ppermute | solution.py:200
  16.2 9.3 %collective-permute-start.5 = (bf16[2,128,256]{2,1,0:T(8,128)(2,1)S(1)}, bf16[2,128,256]{2,1,0:T(8,128)(2,1)S(1)}, u32[]{:S(2)}, u32[]{:S(2)}) collective-permute-start(bf16[2,128,256]{2,1,0:T(8,128)(2,1)S(1)} %add_convert_fusion), channel_id=1, source_target_pairs={{0,8},{4,12},{8,0},{12,4},{1,9},{5,13},{9,1},{13,5},{2,10},{6,14},... | collective-permute-start | bytes 393224 | tf_op jit(solution)/shard_map/ppermute | solution.py:199

commit v3 on v2

--- a/solution.py
+++ b/solution.py
@@ -10,7 +10,7 @@
 from jax.sharding import PartitionSpec as P
 
 OBJ = 512
-TAIL = 16
+CORNER_ROWS = 16
 
 
 def propagator(side):
@@ -56,42 +56,35 @@
 
 
 def send_kernel(
-    slot_ref, offsets_hbm, table_hbm, layer_hbm, residual_hbm,
-    own_ref, other_ref,
-    offsets_ref, table_ref, layer_ref, residual_ref, sems,
+    token_ref, slot_ref, offsets_hbm, layer_hbm, table_ref, residual_ref,
+    own_ref, other_ref, corner_ref,
+    offsets_ref, layer_ref, sems,
 ):
     side = layer_ref.shape[-1]
     half = side // 2
-    pairs = (
-        (offsets_hbm, offsets_ref), (table_hbm, table_ref), (layer_hbm, layer_ref), (residual_hbm, residual_ref),
-    )
-    offsets_copy, table_copy, layer_copy, residual_copy = copies = [
-        pltpu.make_async_copy(source, target, sems.at[n]) for n, (source, target) in enumerate(pairs)
-    ]
-    for copy in copies:
-        copy.start()
+    del token_ref
+    offsets_copy = pltpu.make_async_copy(offsets_hbm, offsets_ref, sems.at[0])
+    layer_copy = pltpu.make_async_copy(layer_hbm, layer_ref, sems.at[1])
+    offsets_copy.start()
+    layer_copy.start()
     offsets_copy.wait()
     slot = slot_ref[0]
     cy, cx = offsets_ref[0, slot], offsets_ref[1, slot]
     parity = lax.rem(lax.axis_index("probe"), 2)
     down = (cy - parity * half) & (side - 1)
-    line = lax.broadcasted_iota(jnp.int32, (TAIL, side), 0)
-    tail = jnp.where(line == 0, cy.astype(jnp.float32), cx.astype(jnp.float32)).astype(jnp.bfloat16)
-    own_ref[2 * half :] = tail
-    other_ref[2 * half :] = tail
+    line = lax.broadcasted_iota(jnp.int32, corner_ref.shape, 0)
+    corner_ref[...] = jnp.where(line == 0, cy.astype(jnp.float32), cx.astype(jnp.float32)).astype(jnp.bfloat16)
     top = lax.axis_index("depth") == 1
 
     def put(part, x):
-        own_ref[part * half : (part + 1) * half] = x[:half]
-        other_ref[part * half : (part + 1) * half] = x[half:]
+        own_ref[part] = x[:half]
+        other_ref[part] = x[half:]
 
     @pl.when(top)
     def _():
-        table_copy.wait()
         (rhr, rlr), (rhi, rli) = (split(pltpu.roll(table_ref[n], cx, 1)) for n in range(2))
         (lhr, llr), (lhi, lli) = (split(pltpu.roll(table_ref[n], (side - down) & (side - 1), 1)) for n in range(2))
         layer_copy.wait()
-        residual_copy.wait()
         layer = layer_ref[0].astype(jnp.float32), layer_ref[1].astype(jnp.float32)
         handed = conj_times(layer, (residual_ref[0], residual_ref[1]))
         vr, vi = (x.astype(jnp.bfloat16) for x in handed)
@@ -107,45 +100,55 @@
 
     @pl.when(jnp.logical_not(top))
     def _():
-        for copy in (layer_copy, residual_copy, table_copy):
-            copy.wait()
+        layer_copy.wait()
         rows, cols = rolls(side, down, cx)
         for part, x in enumerate(rolled([residual_ref[n].astype(jnp.bfloat16) for n in range(2)], rows, cols)):
             put(part, x)
 
 
-def sums_kernel(a0, a1, w0, w1, keep_ref, send_ref, side_keep_ref, side_send_ref):
+def waves_kernel(c0, c1, w0, w1, near_ref, next_ref):
     side = w0.shape[-1]
     half = side // 2
-    place = lax.axis_index("probe")
-    upper = place >= 2
-    right = lax.axis_index("tile") == 1
-    parity = lax.rem(place, 2)
+    parity = lax.rem(lax.axis_index("probe"), 2)
     down = lax.broadcasted_iota(jnp.int32, (half, side), 0) + parity * half
     along = lax.broadcasted_iota(jnp.int32, (half, side), 1)
     every = lax.broadcasted_iota(jnp.int32, (side, side), 0)
     across = lax.broadcasted_iota(jnp.int32, (side, side), 1)
-    zero = jnp.zeros((half, side), jnp.float32)
-    slots = []
-    for w, a in ((w0, a0), (w1, a1)):
-        tail = a[2 * half :].astype(jnp.float32)
-        cy, cx = tail[0:1].astype(jnp.int32), tail[1:2].astype(jnp.int32)
+    for corner, w, out in ((c0, w0, near_ref), (c1, w1, next_ref)):
+        corner = corner[...].astype(jnp.float32)
+        cy, cx = corner[0:1].astype(jnp.int32), corner[1:2].astype(jnp.int32)
         rows = (along == ((down - cy) & (side - 1))).astype(jnp.bfloat16)
         cols = (every == ((across - cx) & (side - 1))).astype(jnp.bfloat16)
         moved = mm(rows, jnp.concatenate([w[0], w[1]], axis=1)).astype(jnp.bfloat16)
-        moved = mm(jnp.concatenate([moved[:, :side], moved[:, side:]], axis=0), cols)
-        wave = moved[:half], moved[half:]
-        adjoint = a[:half].astype(jnp.float32), a[half : 2 * half].astype(jnp.float32)
-        slots.append((conj_times(wave, adjoint), (down < cy) == upper, (along < cx) == right))
+        moved = mm(jnp.concatenate([moved[:, :side], moved[:, side:]], axis=0), cols).astype(jnp.bfloat16)
+        out[0] = moved[:half]
+        out[1] = moved[half:]
+
+
+def sums_kernel(near, c0, c1, a0, a1, w0, w1, here_ref, side_ref):
+    half, side = a0.shape[1:]
+    place = lax.axis_index("probe")
+    strip = (place >= 2) == near
+    right = lax.axis_index("tile") == 1
+    down = lax.broadcasted_iota(jnp.int32, (half, side), 0) + lax.rem(place, 2) * half
+    along = lax.broadcasted_iota(jnp.int32, (half, side), 1)
+    zero = jnp.zeros((half, side), jnp.float32)
+    here = side_sums = (zero, zero)
+    for corner, w, a in ((c0, w0, a0), (c1, w1, a1)):
+        corner = corner[...].astype(jnp.float32)
+        cy, cx = corner[0:1].astype(jnp.int32), corner[1:2].astype(jnp.int32)
+        wave, adjoint = ((x[0].astype(jnp.float32), x[1].astype(jnp.float32)) for x in (w, a))
+        inside, own = (down < cy) == strip, (along < cx) == right
+        gradient = [jnp.where(inside, x, zero) for x in conj_times(wave, adjoint)]
+        here = [total + jnp.where(own, x, zero) for total, x in zip(here, gradient)]
+        side_sums = [total + jnp.where(own, zero, x) for total, x in zip(side_sums, gradient)]
     for part in range(2):
-        for ref, near, here in (
-            (keep_ref, True, True), (send_ref, False, True), (side_keep_ref, True, False), (side_send_ref, False, False),
-        ):
-            total = zero
-            for gradient, mine, own in slots:
-                chosen = jnp.logical_and(mine if near else ~mine, own if here else ~own)
-                total = total + jnp.where(chosen, gradient[part], zero)
-            ref[part] = total.astype(ref.dtype)
+        here_ref[part] = here[part]
+        side_ref[part] = side_sums[part].astype(jnp.bfloat16)
+
+
+def token_kernel(out_ref):
+    out_ref[...] = jnp.zeros_like(out_ref)
 
 
 def in_hbm(*arrays):
@@ -158,25 +161,30 @@
     table = jnp.asarray(propagator(side))
     vmem, smem, hbm = (pl.BlockSpec(memory_space=m) for m in (pltpu.VMEM, pltpu.SMEM, pltpu.HBM))
     block, sums = (jax.ShapeDtypeStruct((2, half, side), t) for t in (jnp.bfloat16, jnp.float32))
-    tailed = jax.ShapeDtypeStruct((2 * half + TAIL, side), jnp.bfloat16)
     params = pltpu.CompilerParams(vmem_limit_bytes=32 * 1024 * 1024)
     by_column = offsets.T
-    waves = stored_waves[0, 0]
-    adj_own, adj_other = pl.pallas_call(
+    token = pl.pallas_call(
+        token_kernel,
+        out_shape=jax.ShapeDtypeStruct((8, 128), jnp.float32),
+        out_specs=vmem,
+        compiler_params=params,
+        cost_estimate=pl.CostEstimate(flops=3 * 10**8, bytes_accessed=0, transcendentals=0),
+        name="token",
+    )()
+    waves, token = lax.optimization_barrier((stored_waves[0, 0], token))
+    adj_own, adj_other, corner = pl.pallas_call(
         send_kernel,
-        out_shape=(tailed, tailed),
-        in_specs=[smem] + [hbm] * 4,
-        out_specs=(vmem,) * 2,
+        out_shape=(block, block, jax.ShapeDtypeStruct((CORNER_ROWS, side), jnp.bfloat16)),
+        in_specs=[vmem, smem, hbm, hbm, vmem, vmem],
+        out_specs=(vmem,) * 3,
         scratch_shapes=[
             pltpu.SMEM(by_column.shape, jnp.int32),
-            pltpu.VMEM(table.shape, jnp.float32),
             pltpu.VMEM((2, side, side), jnp.bfloat16),
-            pltpu.VMEM((2, side, side), jnp.float32),
-            pltpu.SemaphoreType.DMA((4,)),
+            pltpu.SemaphoreType.DMA((2,)),
         ],
         compiler_params=params,
         name="adjoint",
-    )(slot_position, *in_hbm(by_column, table, transmission[0, 0], residual[0]))
+    )(token, slot_position, *in_hbm(by_column, transmission[0, 0]), table, residual[0])
 
     probe_count = lax.axis_size("probe")
     swap_tile = [(0, 1), (1, 0)]
@@ -187,16 +195,28 @@
     a_own = lax.ppermute(adj_own, ("probe", "depth"), flip)
     a_next = lax.ppermute(adj_other, ("probe", "depth"), flip_z1)
     w_next = lax.ppermute(waves, "probe", z1)
-    keep, send, side_keep, side_send = pl.pallas_call(
-        sums_kernel,
-        out_shape=(sums, sums, block, block),
+    corner_next = lax.ppermute(corner, "probe", z1)
+    w_own, w_next = pl.pallas_call(
+        waves_kernel,
+        out_shape=(block, block),
         in_specs=[vmem] * 4,
-        out_specs=(vmem,) * 4,
+        out_specs=(vmem,) * 2,
         compiler_params=params,
-        name="masked_sums",
-    )(a_own, a_next, waves, w_next)
-    send = send + lax.ppermute(side_send, "tile", swap_tile).astype(jnp.float32)
-    got = lax.ppermute(send.astype(jnp.bfloat16), "probe", z2)
+        name="rolled_waves",
+    )(corner, corner_next, waves, w_next)
+    (send, side_send), (keep, side_keep) = (
+        pl.pallas_call(
+            functools.partial(sums_kernel, near),
+            out_shape=(sums, block),
+            in_specs=[vmem] * 6,
+            out_specs=(vmem,) * 2,
+            compiler_params=params,
+            name="near_sums" if near else "far_sums",
+        )(corner, corner_next, a_own, a_next, w_own, w_next)
+        for near in (False, True)
+    )
+    send = (send + lax.ppermute(side_send, "tile", swap_tile).astype(jnp.float32)).astype(jnp.bfloat16)
+    got = lax.ppermute(send, "probe", z2)
     keep = keep + lax.ppermute(side_keep, "tile", swap_tile).astype(jnp.float32)
     return (keep + got.astype(jnp.float32))[:, None]
 

time: 26.4 us -> 25.5 us (0.966)
  waiting for transfers between devices: 13.9 us -> 11.3 us
  starting transfers between devices: 8.44 us -> 10.2 us
    ppermute x1, waiting for transfers between devices: 6.37 us -> 0.01 us  [two_slices(): a_own = lax.ppermute(adj_own, ('probe', 'depth'), flip)]
    ppermute x2 -> x3, waiting for transfers between devices: 7.51 us -> 10.7 us  [the longest x1 6.66 us: two_slices(): got = lax.ppermute(send, 'probe', z2)]
    ppermute x2 -> x3, starting transfers between devices: 2.72 us -> 4.27 us  [the longest x1 2.66 us: two_slices(): got = lax.ppermute(send, 'probe', z2)]
    ppermute x1, waiting for transfers between devices: 0.01 us -> 0.55 us  [two_slices(): a_next = lax.ppermute(adj_other, ('probe', 'depth'), flip_z1)]
    pallas_call x2 -> x5, Pallas kernels: 2.49 us -> 2.37 us  [the longest x1 1.49 us: two_slices(): pl.pallas_call(send_kernel, out_shape=(block, block, jax.ShapeDtypeStruct...]
  transfers between devices with their start and end apart: 6 -> 7, of which waited for: 3 -> 4; matrix products, arithmetic and copies ran while one was open for 0% -> 0% of each run, Pallas kernels for 7% -> 8%
where the time goes in v3:
time: 25.5 us; the launch traced here: 25.4 us
  waiting for transfers between devices  11.3 us (44%)
  starting transfers between devices  10.2 us (40%)
  Pallas kernels  2.37 us (9%)
  other arithmetic  0.77 us (3%)
  between operations  0.73 us (3%)
    ppermute x1, waiting for transfers between devices, two_slices(): got = lax.ppermute(send, 'probe', z2)  6.66 us
    ppermute x1, waiting for transfers between devices, two_slices(): corner_next = lax.ppermute(corner, 'probe', z1)  3.53 us
    ppermute x1, starting transfers between devices, two_slices(): w_next = lax.ppermute(waves, 'probe', z1)  3.09 us
    ppermute x1, starting transfers between devices, two_slices(): got = lax.ppermute(send, 'probe', z2)  2.66 us
    ppermute x1, starting transfers between devices, two_slices(): a_own = lax.ppermute(adj_own, ('probe', 'depth'), flip)  2.3 us
    ppermute x1, starting transfers between devices, two_slices(): corner_next = lax.ppermute(corner, 'probe', z1)  1.54 us
    pallas_call x1, Pallas kernels, two_slices(): pl.pallas_call(send_kernel, out_shape=(block, block, jax.ShapeDtypeStruct...  1.49 us
    broadcast_in_dim x1, other arithmetic, two_slices(): return (keep + got.astype(jnp.float32))[:, None]  0.75 us
  transfers between devices with their start and end apart: 7, of which 4 were waited for; matrix products, arithmetic and copies ran while one was open for 0% of the time, Pallas kernels for 8%

profile of v3, /device:TPU:0, one launch (start us, length us, event | category | flops | bytes accessed | tf_op | source)
XLA Modules:
  0.0 25.4 jit_solution(12345153410620038528)
XLA Ops:
  0.0 0.0 copy-start.1
  0.0 0.0 copy-start
  0.0 3.1 %collective-permute-start.3 = (bf16[2,256,256]{2,1,0:T(8,128)(2,1)}, bf16[2,256,256]{2,1,0:T(8,128)(2,1)S(1)}, u32[]{:S(2)}, u32[]{:S(2)}) collective-permute-start(bf16[2,256,256]{2,1,0:T(8,128)(2,1)} %bitcast.9), channel_id=1, source_target_pairs={{0,4},{4,0},{8,12},{12,8},{1,5},{5,1},{9,13},{13,9},{2,6},{6,2},{1... | collective-permute-start | bytes 786440 | tf_op jit(solution)/shard_map/ppermute | solution.py:197
  3.8 0.0 copy-done.1
  3.8 0.0 copy-done
  3.8 0.0 copy-start.2
  3.8 1.5 %adjoint.1 = (bf16[2,128,256]{2,1,0:T(8,128)(2,1)S(1)}, bf16[2,128,256]{2,1,0:T(8,128)(2,1)S(1)}, bf16[16,256]{1,0:T(8,128)(2,1)S(1)}) custom-call(f32[8,128]{1,0:T(8,128)S(1)} %token_.1.token_ref, s32[1]{0:T(128)S(6)} %copy.8.slot_ref, s32[2,8]{1,0:T(2,128)} %bitcast.12, bf16[2,256,256]{2,1,0:T(8,128)(2,1)} %bitcast.11, f32[2,256,256]{2,1,0:T(8,128)S(1)} %copy-done.1, ...), custom_call_target="tpu_custom_call" | custom-call | tf_op jit(solution)/shard_map/adjoint/pallas_call | solution.py:175
  5.3 2.3 %collective-permute-start.1 = (bf16[2,128,256]{2,1,0:T(8,128)(2,1)S(1)}, bf16[2,128,256]{2,1,0:T(8,128)(2,1)S(1)}, u32[]{:S(2)}, u32[]{:S(2)}) collective-permute-start(bf16[2,128,256]{2,1,0:T(8,128)(2,1)S(1)} %get-tuple-element.18), channel_id=1, source_target_pairs={{0,2},{2,0},{4,6},{6,4},{8,10},{10,8},{12,14},{14,12},{1,3},{3,1},... | collective-permute-start | bytes 393224 | tf_op jit(solution)/shard_map/ppermute | solution.py:195
  7.6 0.0 collective-permute-start.2
  7.6 1.5 %collective-permute-start = (bf16[16,256]{1,0:T(8,128)(2,1)S(1)}, bf16[16,256]{1,0:T(8,128)(2,1)S(1)}, u32[]{:S(2)}, u32[]{:S(2)}) collective-permute-start(bf16[16,256]{1,0:T(8,128)(2,1)S(1)} %get-tuple-element.17.c0), channel_id=1, source_target_pairs={{0,4},{4,0},{8,12},{12,8},{1,5},{5,1},{9,13},{13,9},{2,6},{6,2},{1... | collective-permute-start | bytes 24584 | tf_op jit(solution)/shard_map/ppermute | solution.py:198
  9.1 3.5 %collective-permute-done.c1 = bf16[16,256]{1,0:T(8,128)(2,1)S(1)} collective-permute-done((bf16[16,256]{1,0:T(8,128)(2,1)S(1)}, bf16[16,256]{1,0:T(8,128)(2,1)S(1)}, u32[]{:S(2)}, u32[]{:S(2)}) %collective-permute-start) | collective-permute-done | bytes 8224 | tf_op jit(solution)/shard_map/ppermute | solution.py:198
  12.6 0.0 collective-permute-done.3.w1
  12.7 0.0 copy-done.2
  12.7 0.4 %rolled_waves.1 = (bf16[2,128,256]{2,1,0:T(8,128)(2,1)S(1)}, bf16[2,128,256]{2,1,0:T(8,128)(2,1)S(1)}) custom-call(bf16[16,256]{1,0:T(8,128)(2,1)S(1)} %get-tuple-element.17.c0, bf16[16,256]{1,0:T(8,128)(2,1)S(1)} %collective-permute-done.c1, bf16[2,256,256]{2,1,0:T(8,128)(2,1)S(1)} %bitcast.10, bf16[2,256,256]{2,1,0:T(8,128)(2,1)S(1)} %collective-permute-done.3.w1), custom_call_target="tpu_custom_call" | custom-call | tf_op jit(solution)/shard_map/rolled_waves/pallas_call | solution.py:199
  13.1 0.0 collective-permute-done.1.a0
  13.1 0.5 %collective-permute-done.2.a1 = bf16[2,128,256]{2,1,0:T(8,128)(2,1)S(1)} collective-permute-done((bf16[2,128,256]{2,1,0:T(8,128)(2,1)S(1)}, bf16[2,128,256]{2,1,0:T(8,128)(2,1)S(1)}, u32[]{:S(2)}, u32[]{:S(2)}) %collective-permute-start.2) | collective-permute-done | bytes 131104 | tf_op jit(solution)/shard_map/ppermute | solution.py:196
  13.6 0.2 far_sums.1
  13.9 0.1 collective-permute-start.5
  13.9 0.2 near_sums.1
  14.2 0.6 %collective-permute-start.4 = (bf16[2,128,256]{2,1,0:T(8,128)(2,1)S(1)}, bf16[2,128,256]{2,1,0:T(8,128)(2,1)S(1)}, u32[]{:S(2)}, u32[]{:S(2)}) collective-permute-start(bf16[2,128,256]{2,1,0:T(8,128)(2,1)S(1)} %get-tuple-element.24), channel_id=1, source_target_pairs={{0,1},{1,0},{2,3},{3,2},{4,5},{5,4},{6,7},{7,6},{8,9},{9,8},{10,11... | collective-permute-start | bytes 393224 | tf_op jit(solution)/shard_map/ppermute | solution.py:220
  14.7 0.5 %collective-permute-done.5 = bf16[2,128,256]{2,1,0:T(8,128)(2,1)S(1)} collective-permute-done((bf16[2,128,256]{2,1,0:T(8,128)(2,1)S(1)}, bf16[2,128,256]{2,1,0:T(8,128)(2,1)S(1)}, u32[]{:S(2)}, u32[]{:S(2)}) %collective-permute-start.5) | collective-permute-done | bytes 131104 | tf_op jit(solution)/shard_map/ppermute | solution.py:218
  15.3 2.7 %collective-permute-start.6 = (bf16[2,128,256]{2,1,0:T(8,128)(2,1)S(1)}, bf16[2,128,256]{2,1,0:T(8,128)(2,1)S(1)}, u32[]{:S(2)}, u32[]{:S(2)}) collective-permute-start(bf16[2,128,256]{2,1,0:T(8,128)(2,1)S(1)} %add_convert_fusion), channel_id=1, source_target_pairs={{0,8},{4,12},{8,0},{12,4},{1,9},{5,13},{9,1},{13,5},{2,10},{6,14},... | collective-permute-start | bytes 393224 | tf_op jit(solution)/shard_map/ppermute | solution.py:219
  18.0 0.0 collective-permute-done.4
  18.0 6.7 %collective-permute-done.6 = bf16[2,128,256]{2,1,0:T(8,128)(2,1)S(1)} collective-permute-done((bf16[2,128,256]{2,1,0:T(8,128)(2,1)S(1)}, bf16[2,128,256]{2,1,0:T(8,128)(2,1)S(1)}, u32[]{:S(2)}, u32[]{:S(2)}) %collective-permute-start.6) | collective-permute-done | bytes 131104 | tf_op jit(solution)/shard_map/ppermute | solution.py:219
  24.6 0.7 %add_bitcast_fusion = f32[2,1,128,256]{3,2,1,0:T(8,128)} fusion(bf16[2,128,256]{2,1,0:T(8,128)(2,1)S(1)} %collective-permute-done.6, f32[2,128,256]{2,1,0:T(8,128)S(1)} %get-tuple-element.23, bf16[2,128,256]{2,1,0:T(8,128)(2,1)S(1)} %collective-permute-done.4), kind=kLoop, calls=%fused_computation | loop fusion | flops 262144 | bytes 786432 | tf_op jit(solution)/shard_map/broadcast_in_dim | solution.py:221
  (2 shorter events, 0.0 us)
Async XLA Ops:
  0.0 3.8 %copy-start.1 = (f32[2,256,256]{2,1,0:T(8,128)S(1)}, f32[2,256,256]{2,1,0:T(8,128)}, u32[]{:S(2)}) copy-start(f32[2,256,256]{2,1,0:T(8,128)} %constant.2.clone.table_ref) | copy-start | bytes 1572868
  0.0 3.8 %copy-start = (f32[1,2,256,256]{3,2,1,0:T(8,128)S(1)}, f32[1,2,256,256]{3,2,1,0:T(8,128)}, u32[]{:S(2)}) copy-start(f32[1,2,256,256]{3,2,1,0:T(8,128)} %param.8) | copy-start | bytes 1572868
  0.0 12.6 %collective-permute-start.3 = (bf16[2,256,256]{2,1,0:T(8,128)(2,1)}, bf16[2,256,256]{2,1,0:T(8,128)(2,1)S(1)}, u32[]{:S(2)}, u32[]{:S(2)}) collective-permute-start(bf16[2,256,256]{2,1,0:T(8,128)(2,1)} %bitcast.9), channel_id=1, source_target_pairs={{0,4},{4,0},{8,12},{12,8},{1,5},{5,1},{9,13},{13,9},{2,6},{6,2},{1... | collective-permute-start | bytes 786440 | tf_op jit(solution)/shard_map/ppermute | solution.py:197
  3.8 8.9 %copy-start.2 = (bf16[1,1,2,256,256]{4,3,2,1,0:T(8,128)(2,1)S(1)}, bf16[1,1,2,256,256]{4,3,2,1,0:T(8,128)(2,1)}, u32[]{:S(2)}) copy-start(bf16[1,1,2,256,256]{4,3,2,1,0:T(8,128)(2,1)} %param.6) | copy-start | bytes 786436
  5.3 7.8 %collective-permute-start.1 = (bf16[2,128,256]{2,1,0:T(8,128)(2,1)S(1)}, bf16[2,128,256]{2,1,0:T(8,128)(2,1)S(1)}, u32[]{:S(2)}, u32[]{:S(2)}) collective-permute-start(bf16[2,128,256]{2,1,0:T(8,128)(2,1)S(1)} %get-tuple-element.18), channel_id=1, source_target_pairs={{0,2},{2,0},{4,6},{6,4},{8,10},{10,8},{12,14},{14,12},{1,3},{3,1},... | collective-permute-start | bytes 393224 | tf_op jit(solution)/shard_map/ppermute | solution.py:195
  7.6 6.1 %collective-permute-start.2 = (bf16[2,128,256]{2,1,0:T(8,128)(2,1)S(1)}, bf16[2,128,256]{2,1,0:T(8,128)(2,1)S(1)}, u32[]{:S(2)}, u32[]{:S(2)}) collective-permute-start(bf16[2,128,256]{2,1,0:T(8,128)(2,1)S(1)} %get-tuple-element.19), channel_id=1, source_target_pairs={{0,6},{2,4},{4,2},{6,0},{8,14},{10,12},{12,10},{14,8},{1,7},{3,5},... | collective-permute-start | bytes 393224 | tf_op jit(solution)/shard_map/ppermute | solution.py:196
  7.6 5.1 %collective-permute-start = (bf16[16,256]{1,0:T(8,128)(2,1)S(1)}, bf16[16,256]{1,0:T(8,128)(2,1)S(1)}, u32[]{:S(2)}, u32[]{:S(2)}) collective-permute-start(bf16[16,256]{1,0:T(8,128)(2,1)S(1)} %get-tuple-element.17.c0), channel_id=1, source_target_pairs={{0,4},{4,0},{8,12},{12,8},{1,5},{5,1},{9,13},{13,9},{2,6},{6,2},{1... | collective-permute-start | bytes 24584 | tf_op jit(solution)/shard_map/ppermute | solution.py:198
  13.9 1.4 %collective-permute-start.5 = (bf16[2,128,256]{2,1,0:T(8,128)(2,1)S(1)}, bf16[2,128,256]{2,1,0:T(8,128)(2,1)S(1)}, u32[]{:S(2)}, u32[]{:S(2)}) collective-permute-start(bf16[2,128,256]{2,1,0:T(8,128)(2,1)S(1)} %get-tuple-element.26), channel_id=1, source_target_pairs={{0,1},{1,0},{2,3},{3,2},{4,5},{5,4},{6,7},{7,6},{8,9},{9,8},{10,11... | collective-permute-start | bytes 393224 | tf_op jit(solution)/shard_map/ppermute | solution.py:218
  14.2 3.8 %collective-permute-start.4 = (bf16[2,128,256]{2,1,0:T(8,128)(2,1)S(1)}, bf16[2,128,256]{2,1,0:T(8,128)(2,1)S(1)}, u32[]{:S(2)}, u32[]{:S(2)}) collective-permute-start(bf16[2,128,256]{2,1,0:T(8,128)(2,1)S(1)} %get-tuple-element.24), channel_id=1, source_target_pairs={{0,1},{1,0},{2,3},{3,2},{4,5},{5,4},{6,7},{7,6},{8,9},{9,8},{10,11... | collective-permute-start | bytes 393224 | tf_op jit(solution)/shard_map/ppermute | solution.py:220
  15.3 9.3 %collective-permute-start.6 = (bf16[2,128,256]{2,1,0:T(8,128)(2,1)S(1)}, bf16[2,128,256]{2,1,0:T(8,128)(2,1)S(1)}, u32[]{:S(2)}, u32[]{:S(2)}) collective-permute-start(bf16[2,128,256]{2,1,0:T(8,128)(2,1)S(1)} %add_convert_fusion), channel_id=1, source_target_pairs={{0,8},{4,12},{8,0},{12,4},{1,9},{5,13},{9,1},{13,5},{2,10},{6,14},... | collective-permute-start | bytes 393224 | tf_op jit(solution)/shard_map/ppermute | solution.py:219

commit v4 on v3

--- a/solution.py
+++ b/solution.py
@@ -145,6 +145,10 @@
     for part in range(2):
         here_ref[part] = here[part]
         side_ref[part] = side_sums[part].astype(jnp.bfloat16)
+
+
+def copy_kernel(in_ref, *refs):
+    refs[-1][...] = in_ref[...]
 
 
 def token_kernel(out_ref):
@@ -190,8 +194,7 @@
     swap_tile = [(0, 1), (1, 0)]
     flip = [(2 * z + d, 2 * z + 1 - d) for z in range(probe_count) for d in range(2)]
     flip_z1 = [(2 * z + d, 2 * (z ^ 1) + 1 - d) for z in range(probe_count) for d in range(2)]
-    z1 = [(z, z ^ 1) for z in range(probe_count)]
-    z2 = [(z, z ^ 2) for z in range(probe_count)]
+    z1, z2 = ([(z, z ^ n) for z in range(probe_count)] for n in (1, 2))
     a_own = lax.ppermute(adj_own, ("probe", "depth"), flip)
     a_next = lax.ppermute(adj_other, ("probe", "depth"), flip_z1)
     w_next = lax.ppermute(waves, "probe", z1)
@@ -216,9 +219,29 @@
         for near in (False, True)
     )
     send = (send + lax.ppermute(side_send, "tile", swap_tile).astype(jnp.float32)).astype(jnp.bfloat16)
-    got = lax.ppermute(send, "probe", z2)
-    keep = keep + lax.ppermute(side_keep, "tile", swap_tile).astype(jnp.float32)
-    return (keep + got.astype(jnp.float32))[:, None]
+
+    def after(x, *earlier):
+        return pl.pallas_call(
+            copy_kernel,
+            out_shape=jax.ShapeDtypeStruct(x.shape, x.dtype),
+            in_specs=[vmem] * (1 + len(earlier)),
+            out_specs=vmem,
+            compiler_params=params,
+            name="after",
+        )(x, *earlier)
+
+    odd = lax.axis_index("probe") % 2 == 1
+    even_far, odd_far = (
+        [(2 * z + t, 2 * (z ^ 2) + t if z % 2 == turn else 2 * z + 1 - t) for z in range(probe_count) for t in range(2)]
+        for turn in range(2)
+    )
+    once = lax.ppermute(after(corner, send), "tile", swap_tile)
+    first = lax.ppermute(after(send, side_keep), ("probe", "tile"), even_far)
+    twice = lax.ppermute(after(corner, once), "tile", swap_tile)
+    near = lax.ppermute(after(side_keep, first), "tile", swap_tile)
+    third = lax.ppermute(after(send, twice), ("probe", "tile"), odd_far)
+    far = jnp.where(odd, third, first)
+    return (keep + (near.astype(jnp.float32) + far.astype(jnp.float32)))[:, None]
 
 
 def times(a, b, spec):

time: 25.5 us -> 24.4 us (0.957)
  waiting for transfers between devices: 11.3 us -> 9.92 us
    ppermute x2 -> x5, waiting for transfers between devices: 6.66 us -> 4.74 us  [the longest x1 1.31 us: two_slices(): near = lax.ppermute(after(side_keep, first), 'tile', swap_tile)]
    ppermute x1, waiting for transfers between devices: 0.53 us -> 1.09 us  [two_slices(): lax.ppermute(side_send, 'tile', swap_tile).astype(jnp.float32)]
    ppermute x2 -> x5, starting transfers between devices: 3.22 us -> 3.14 us  [the longest x1 2.66 us: two_slices(): first = lax.ppermute(after(send, side_keep), ('probe', 'tile'), even_far)]
  transfers between devices with their start and end apart: 7 -> 10, of which waited for: 4 -> 7; matrix products, arithmetic and copies ran while one was open for 0% -> 0% of each run, Pallas kernels for 8% -> 9%
where the time goes in v4:
time: 24.4 us; the launch traced here: 24 us
  starting transfers between devices  10.1 us (41%)
  waiting for transfers between devices  9.92 us (41%)
  Pallas kernels  2.4 us (10%)
  other arithmetic  0.79 us (3%)
  between operations  0.77 us (3%)
    ppermute x1, waiting for transfers between devices, two_slices(): corner_next = lax.ppermute(corner, 'probe', z1)  3.53 us
    ppermute x1, starting transfers between devices, two_slices(): w_next = lax.ppermute(waves, 'probe', z1)  3.09 us
    ppermute x1, starting transfers between devices, two_slices(): first = lax.ppermute(after(send, side_keep), ('probe', 'tile'), even_far)  2.66 us
    ppermute x1, starting transfers between devices, two_slices(): a_own = lax.ppermute(adj_own, ('probe', 'depth'), flip)  2.3 us
    ppermute x1, starting transfers between devices, two_slices(): corner_next = lax.ppermute(corner, 'probe', z1)  1.54 us
    pallas_call x1, Pallas kernels, two_slices(): pl.pallas_call(send_kernel, out_shape=(block, block, jax.ShapeDtypeStruct...  1.49 us
    ppermute x1, waiting for transfers between devices, two_slices(): near = lax.ppermute(after(side_keep, first), 'tile', swap_tile)  1.31 us
    ppermute x1, waiting for transfers between devices, two_slices(): first = lax.ppermute(after(send, side_keep), ('probe', 'tile'), even_far)  1.25 us
  transfers between devices with their start and end apart: 10, of which 7 were waited for; matrix products, arithmetic and copies ran while one was open for 0% of the time, Pallas kernels for 9%

profile of v4, /device:TPU:0, one launch (start us, length us, event | category | flops | bytes accessed | tf_op | source)
XLA Modules:
  0.0 24.0 jit_solution(1544666448565207365)
XLA Ops:
  0.0 0.0 copy-start.1
  0.0 0.0 copy-start
  0.0 3.1 %collective-permute-start.3 = (bf16[2,256,256]{2,1,0:T(8,128)(2,1)}, bf16[2,256,256]{2,1,0:T(8,128)(2,1)S(1)}, u32[]{:S(2)}, u32[]{:S(2)}) collective-permute-start(bf16[2,256,256]{2,1,0:T(8,128)(2,1)} %bitcast.9), channel_id=1, source_target_pairs={{0,4},{4,0},{8,12},{12,8},{1,5},{5,1},{9,13},{13,9},{2,6},{6,2},{1... | collective-permute-start | bytes 786440 | tf_op jit(solution)/shard_map/ppermute | solution.py:200
  3.8 0.0 copy-done.1
  3.8 0.0 copy-done
  3.8 0.0 copy-start.2
  3.8 1.5 %adjoint.1 = (bf16[2,128,256]{2,1,0:T(8,128)(2,1)S(1)}, bf16[2,128,256]{2,1,0:T(8,128)(2,1)S(1)}, bf16[16,256]{1,0:T(8,128)(2,1)S(1)}) custom-call(f32[8,128]{1,0:T(8,128)S(1)} %token_.1.token_ref, s32[1]{0:T(128)S(6)} %copy.8.slot_ref, s32[2,8]{1,0:T(2,128)} %bitcast.12, bf16[2,256,256]{2,1,0:T(8,128)(2,1)} %bitcast.11, f32[2,256,256]{2,1,0:T(8,128)S(1)} %copy-done.1, ...), custom_call_target="tpu_custom_call" | custom-call | tf_op jit(solution)/shard_map/adjoint/pallas_call | solution.py:179
  5.3 2.3 %collective-permute-start.1 = (bf16[2,128,256]{2,1,0:T(8,128)(2,1)S(1)}, bf16[2,128,256]{2,1,0:T(8,128)(2,1)S(1)}, u32[]{:S(2)}, u32[]{:S(2)}) collective-permute-start(bf16[2,128,256]{2,1,0:T(8,128)(2,1)S(1)} %get-tuple-element.18), channel_id=1, source_target_pairs={{0,2},{2,0},{4,6},{6,4},{8,10},{10,8},{12,14},{14,12},{1,3},{3,1},... | collective-permute-start | bytes 393224 | tf_op jit(solution)/shard_map/ppermute | solution.py:198
  7.6 0.0 collective-permute-start.2
  7.6 1.5 %collective-permute-start = (bf16[16,256]{1,0:T(8,128)(2,1)S(1)}, bf16[16,256]{1,0:T(8,128)(2,1)S(1)}, u32[]{:S(2)}, u32[]{:S(2)}) collective-permute-start(bf16[16,256]{1,0:T(8,128)(2,1)S(1)} %get-tuple-element.17.c0.in_ref), channel_id=1, source_target_pairs={{0,4},{4,0},{8,12},{12,8},{1,5},{5,1},{9,13},{13,9},{2,6},{6,2},{1... | collective-permute-start | bytes 24584 | tf_op jit(solution)/shard_map/ppermute | solution.py:201
  9.1 3.5 %collective-permute-done.c1 = bf16[16,256]{1,0:T(8,128)(2,1)S(1)} collective-permute-done((bf16[16,256]{1,0:T(8,128)(2,1)S(1)}, bf16[16,256]{1,0:T(8,128)(2,1)S(1)}, u32[]{:S(2)}, u32[]{:S(2)}) %collective-permute-start) | collective-permute-done | bytes 8224 | tf_op jit(solution)/shard_map/ppermute | solution.py:201
  12.6 0.0 collective-permute-done.3.w1
  12.7 0.0 copy-done.2
  12.7 0.4 %rolled_waves.1 = (bf16[2,128,256]{2,1,0:T(8,128)(2,1)S(1)}, bf16[2,128,256]{2,1,0:T(8,128)(2,1)S(1)}) custom-call(bf16[16,256]{1,0:T(8,128)(2,1)S(1)} %get-tuple-element.17.c0.in_ref, bf16[16,256]{1,0:T(8,128)(2,1)S(1)} %collective-permute-done.c1, bf16[2,256,256]{2,1,0:T(8,128)(2,1)S(1)} %bitcast.10, bf16[2,256,256]{2,1,0:T(8,128)(2,1)S(1)} %collective-permute-done.3.w1), custom_call_target="tpu_custom_call" | custom-call | tf_op jit(solution)/shard_map/rolled_waves/pallas_call | solution.py:202
  13.1 0.0 collective-permute-done.1.a0
  13.1 0.5 %collective-permute-done.2.a1 = bf16[2,128,256]{2,1,0:T(8,128)(2,1)S(1)} collective-permute-done((bf16[2,128,256]{2,1,0:T(8,128)(2,1)S(1)}, bf16[2,128,256]{2,1,0:T(8,128)(2,1)S(1)}, u32[]{:S(2)}, u32[]{:S(2)}) %collective-permute-start.2) | collective-permute-done | bytes 131104 | tf_op jit(solution)/shard_map/ppermute | solution.py:199
  13.6 0.2 far_sums.1
  13.9 0.1 collective-permute-start.4
  13.9 0.2 near_sums.1
  14.2 1.1 %collective-permute-done.4 = bf16[2,128,256]{2,1,0:T(8,128)(2,1)S(1)} collective-permute-done((bf16[2,128,256]{2,1,0:T(8,128)(2,1)S(1)}, bf16[2,128,256]{2,1,0:T(8,128)(2,1)S(1)}, u32[]{:S(2)}, u32[]{:S(2)}) %collective-permute-start.4) | collective-permute-done | bytes 131104 | tf_op jit(solution)/shard_map/ppermute | solution.py:221
  15.3 2.7 %collective-permute-start.5 = (bf16[2,128,256]{2,1,0:T(8,128)(2,1)S(1)}, bf16[2,128,256]{2,1,0:T(8,128)(2,1)S(1)}, u32[]{:S(2)}, u32[]{:S(2)}) collective-permute-start(bf16[2,128,256]{2,1,0:T(8,128)(2,1)S(1)} %after.5), channel_id=1, source_target_pairs={{0,8},{1,9},{4,5},{5,4},{8,0},{9,1},{12,13},{13,12},{2,10},{3,11},... | collective-permute-start | bytes 393224 | tf_op jit(solution)/shard_map/ppermute | solution.py:239
  18.0 0.0 collective-permute-start.7
  18.0 1.2 %collective-permute-done.7.refs_0_ = bf16[16,256]{1,0:T(8,128)(2,1)S(1)} collective-permute-done((bf16[16,256]{1,0:T(8,128)(2,1)S(1)}, bf16[16,256]{1,0:T(8,128)(2,1)S(1)}, u32[]{:S(2)}, u32[]{:S(2)}) %collective-permute-start.7) | collective-permute-done | bytes 8224 | tf_op jit(solution)/shard_map/ppermute | solution.py:238
  19.2 0.2 collective-permute-start.8
  19.3 1.0 %collective-permute-done.8.refs_0_ = bf16[16,256]{1,0:T(8,128)(2,1)S(1)} collective-permute-done((bf16[16,256]{1,0:T(8,128)(2,1)S(1)}, bf16[16,256]{1,0:T(8,128)(2,1)S(1)}, u32[]{:S(2)}, u32[]{:S(2)}) %collective-permute-start.8) | collective-permute-done | bytes 8224 | tf_op jit(solution)/shard_map/ppermute | solution.py:240
  20.4 0.2 collective-permute-start.9
  20.6 1.3 %collective-permute-done.5.refs_0_ = bf16[2,128,256]{2,1,0:T(8,128)(2,1)S(1)} collective-permute-done((bf16[2,128,256]{2,1,0:T(8,128)(2,1)S(1)}, bf16[2,128,256]{2,1,0:T(8,128)(2,1)S(1)}, u32[]{:S(2)}, u32[]{:S(2)}) %collective-permute-start.5) | collective-permute-done | bytes 131104 | tf_op jit(solution)/shard_map/ppermute | solution.py:239
  21.9 0.1 collective-permute-start.6
  22.0 0.0 collective-permute-done.9
  22.0 1.3 %collective-permute-done.6 = bf16[2,128,256]{2,1,0:T(8,128)(2,1)S(1)} collective-permute-done((bf16[2,128,256]{2,1,0:T(8,128)(2,1)S(1)}, bf16[2,128,256]{2,1,0:T(8,128)(2,1)S(1)}, u32[]{:S(2)}, u32[]{:S(2)}) %collective-permute-start.6) | collective-permute-done | bytes 131104 | tf_op jit(solution)/shard_map/ppermute | solution.py:241
  23.3 0.8 %add_bitcast_fusion = f32[2,1,128,256]{3,2,1,0:T(8,128)} fusion(f32[2,128,256]{2,1,0:T(8,128)S(1)} %get-tuple-element.23, bf16[2,128,256]{2,1,0:T(8,128)(2,1)S(1)} %collective-permute-done.6, bf16[2,128,256]{2,1,0:T(8,128)(2,1)S(1)} %collective-permute-done.9, bf16[2,128,256]{2,1,0:T(8,128)(2,1)S(1)} %collective-permute-done.5.refs_0_, pred[]{:T(512)S(6)} %eq.5), kind=kLoop, calls=%fused_computation | loop fusion | flops 327680 | bytes 917505 | tf_op jit(solution)/shard_map/broadcast_in_dim | solution.py:244
  (7 shorter events, 0.1 us)
Async XLA Ops:
  0.0 3.8 %copy-start.1 = (f32[2,256,256]{2,1,0:T(8,128)S(1)}, f32[2,256,256]{2,1,0:T(8,128)}, u32[]{:S(2)}) copy-start(f32[2,256,256]{2,1,0:T(8,128)} %constant.21.clone.table_ref) | copy-start | bytes 1572868
  0.0 3.8 %copy-start = (f32[1,2,256,256]{3,2,1,0:T(8,128)S(1)}, f32[1,2,256,256]{3,2,1,0:T(8,128)}, u32[]{:S(2)}) copy-start(f32[1,2,256,256]{3,2,1,0:T(8,128)} %param.8) | copy-start | bytes 1572868
  0.0 12.6 %collective-permute-start.3 = (bf16[2,256,256]{2,1,0:T(8,128)(2,1)}, bf16[2,256,256]{2,1,0:T(8,128)(2,1)S(1)}, u32[]{:S(2)}, u32[]{:S(2)}) collective-permute-start(bf16[2,256,256]{2,1,0:T(8,128)(2,1)} %bitcast.9), channel_id=1, source_target_pairs={{0,4},{4,0},{8,12},{12,8},{1,5},{5,1},{9,13},{13,9},{2,6},{6,2},{1... | collective-permute-start | bytes 786440 | tf_op jit(solution)/shard_map/ppermute | solution.py:200
  3.8 8.9 %copy-start.2 = (bf16[1,1,2,256,256]{4,3,2,1,0:T(8,128)(2,1)S(1)}, bf16[1,1,2,256,256]{4,3,2,1,0:T(8,128)(2,1)}, u32[]{:S(2)}) copy-start(bf16[1,1,2,256,256]{4,3,2,1,0:T(8,128)(2,1)} %param.6) | copy-start | bytes 786436
  5.3 7.8 %collective-permute-start.1 = (bf16[2,128,256]{2,1,0:T(8,128)(2,1)S(1)}, bf16[2,128,256]{2,1,0:T(8,128)(2,1)S(1)}, u32[]{:S(2)}, u32[]{:S(2)}) collective-permute-start(bf16[2,128,256]{2,1,0:T(8,128)(2,1)S(1)} %get-tuple-element.18), channel_id=1, source_target_pairs={{0,2},{2,0},{4,6},{6,4},{8,10},{10,8},{12,14},{14,12},{1,3},{3,1},... | collective-permute-start | bytes 393224 | tf_op jit(solution)/shard_map/ppermute | solution.py:198
  7.6 6.1 %collective-permute-start.2 = (bf16[2,128,256]{2,1,0:T(8,128)(2,1)S(1)}, bf16[2,128,256]{2,1,0:T(8,128)(2,1)S(1)}, u32[]{:S(2)}, u32[]{:S(2)}) collective-permute-start(bf16[2,128,256]{2,1,0:T(8,128)(2,1)S(1)} %get-tuple-element.19), channel_id=1, source_target_pairs={{0,6},{2,4},{4,2},{6,0},{8,14},{10,12},{12,10},{14,8},{1,7},{3,5},... | collective-permute-start | bytes 393224 | tf_op jit(solution)/shard_map/ppermute | solution.py:199
  7.6 5.1 %collective-permute-start = (bf16[16,256]{1,0:T(8,128)(2,1)S(1)}, bf16[16,256]{1,0:T(8,128)(2,1)S(1)}, u32[]{:S(2)}, u32[]{:S(2)}) collective-permute-start(bf16[16,256]{1,0:T(8,128)(2,1)S(1)} %get-tuple-element.17.c0.in_ref), channel_id=1, source_target_pairs={{0,4},{4,0},{8,12},{12,8},{1,5},{5,1},{9,13},{13,9},{2,6},{6,2},{1... | collective-permute-start | bytes 24584 | tf_op jit(solution)/shard_map/ppermute | solution.py:201
  13.9 1.4 %collective-permute-start.4 = (bf16[2,128,256]{2,1,0:T(8,128)(2,1)S(1)}, bf16[2,128,256]{2,1,0:T(8,128)(2,1)S(1)}, u32[]{:S(2)}, u32[]{:S(2)}) collective-permute-start(bf16[2,128,256]{2,1,0:T(8,128)(2,1)S(1)} %get-tuple-element.26), channel_id=1, source_target_pairs={{0,1},{1,0},{2,3},{3,2},{4,5},{5,4},{6,7},{7,6},{8,9},{9,8},{10,11... | collective-permute-start | bytes 393224 | tf_op jit(solution)/shard_map/ppermute | solution.py:221
  15.3 6.5 %collective-permute-start.5 = (bf16[2,128,256]{2,1,0:T(8,128)(2,1)S(1)}, bf16[2,128,256]{2,1,0:T(8,128)(2,1)S(1)}, u32[]{:S(2)}, u32[]{:S(2)}) collective-permute-start(bf16[2,128,256]{2,1,0:T(8,128)(2,1)S(1)} %after.5), channel_id=1, source_target_pairs={{0,8},{1,9},{4,5},{5,4},{8,0},{9,1},{12,13},{13,12},{2,10},{3,11},... | collective-permute-start | bytes 393224 | tf_op jit(solution)/shard_map/ppermute | solution.py:239
  18.0 1.2 %collective-permute-start.7 = (bf16[16,256]{1,0:T(8,128)(2,1)S(1)}, bf16[16,256]{1,0:T(8,128)(2,1)S(1)}, u32[]{:S(2)}, u32[]{:S(2)}) collective-permute-start(bf16[16,256]{1,0:T(8,128)(2,1)S(1)} %after.7), channel_id=1, source_target_pairs={{0,1},{1,0},{2,3},{3,2},{4,5},{5,4},{6,7},{7,6},{8,9},{9,8},{10,11... | collective-permute-start | bytes 24584 | tf_op jit(solution)/shard_map/ppermute | solution.py:238
  19.2 1.2 %collective-permute-start.8 = (bf16[16,256]{1,0:T(8,128)(2,1)S(1)}, bf16[16,256]{1,0:T(8,128)(2,1)S(1)}, u32[]{:S(2)}, u32[]{:S(2)}) collective-permute-start(bf16[16,256]{1,0:T(8,128)(2,1)S(1)} %after.8), channel_id=1, source_target_pairs={{0,1},{1,0},{2,3},{3,2},{4,5},{5,4},{6,7},{7,6},{8,9},{9,8},{10,11... | collective-permute-start | bytes 24584 | tf_op jit(solution)/shard_map/ppermute | solution.py:240
  20.4 1.6 %collective-permute-start.9 = (bf16[2,128,256]{2,1,0:T(8,128)(2,1)S(1)}, bf16[2,128,256]{2,1,0:T(8,128)(2,1)S(1)}, u32[]{:S(2)}, u32[]{:S(2)}) collective-permute-start(bf16[2,128,256]{2,1,0:T(8,128)(2,1)S(1)} %after.9), channel_id=1, source_target_pairs={{0,1},{1,0},{4,12},{5,13},{8,9},{9,8},{12,4},{13,5},{2,3},{3,2},{6... | collective-permute-start | bytes 393224 | tf_op jit(solution)/shard_map/ppermute | solution.py:242
  21.9 1.4 %collective-permute-start.6 = (bf16[2,128,256]{2,1,0:T(8,128)(2,1)S(1)}, bf16[2,128,256]{2,1,0:T(8,128)(2,1)S(1)}, u32[]{:S(2)}, u32[]{:S(2)}) collective-permute-start(bf16[2,128,256]{2,1,0:T(8,128)(2,1)S(1)} %after.6), channel_id=1, source_target_pairs={{0,1},{1,0},{2,3},{3,2},{4,5},{5,4},{6,7},{7,6},{8,9},{9,8},{10,11... | collective-permute-start | bytes 393224 | tf_op jit(solution)/shard_map/ppermute | solution.py:241

commit v5 on v4

--- a/solution.py
+++ b/solution.py
@@ -82,17 +82,17 @@
 
     @pl.when(top)
     def _():
-        (rhr, rlr), (rhi, rli) = (split(pltpu.roll(table_ref[n], cx, 1)) for n in range(2))
-        (lhr, llr), (lhi, lli) = (split(pltpu.roll(table_ref[n], (side - down) & (side - 1), 1)) for n in range(2))
         layer_copy.wait()
         layer = layer_ref[0].astype(jnp.float32), layer_ref[1].astype(jnp.float32)
         handed = conj_times(layer, (residual_ref[0], residual_ref[1]))
         vr, vi = (x.astype(jnp.bfloat16) for x in handed)
+        (rhr, rlr), (rhi, rli) = (split(pltpu.roll(table_ref[n], cx, 1)) for n in range(2))
         field = jnp.concatenate([vr, vr, vi, vi], axis=1)
         middle = (
             mm(field, jnp.concatenate([rlr, rhr, -rli, -rhi], axis=0)),
             mm(field, jnp.concatenate([rli, rhi, rlr, rhr], axis=0)),
         )
+        (lhr, llr), (lhi, lli) = (split(pltpu.roll(table_ref[n], (side - down) & (side - 1), 1)) for n in range(2))
         (mhr, mlr), (mhi, mli) = map(split, middle)
         field = jnp.concatenate([mlr, mhr, mhr, mli, mhi, mhi], axis=0)
         for part, x in enumerate(([lhr, llr, lhr, -lhi, -lli, -lhi], [lhi, lli, lhi, lhr, llr, lhr])):

time: 24.4 us -> 24.2 us (level)
  no operation moved by 1% of the time
where the time goes in v5:
time: 24.2 us; the launch traced here: 24 us
  starting transfers between devices  10 us (41%)
  waiting for transfers between devices  9.99 us (41%)
  Pallas kernels  2.4 us (10%)
  other arithmetic  0.79 us (3%)
  between operations  0.77 us (3%)
    ppermute x1, waiting for transfers between devices, two_slices(): corner_next = lax.ppermute(corner, 'probe', z1)  3.61 us
    ppermute x1, starting transfers between devices, two_slices(): w_next = lax.ppermute(waves, 'probe', z1)  3.09 us
    ppermute x1, starting transfers between devices, two_slices(): first = lax.ppermute(after(send, side_keep), ('probe', 'tile'), even_far)  2.65 us
    ppermute x1, starting transfers between devices, two_slices(): a_own = lax.ppermute(adj_own, ('probe', 'depth'), flip)  2.22 us
    ppermute x1, starting transfers between devices, two_slices(): corner_next = lax.ppermute(corner, 'probe', z1)  1.54 us
    pallas_call x1, Pallas kernels, two_slices(): pl.pallas_call(send_kernel, out_shape=(block, block, jax.ShapeDtypeStruct...  1.49 us
    ppermute x1, waiting for transfers between devices, two_slices(): near = lax.ppermute(after(side_keep, first), 'tile', swap_tile)  1.31 us
    ppermute x1, waiting for transfers between devices, two_slices(): first = lax.ppermute(after(send, side_keep), ('probe', 'tile'), even_far)  1.26 us
  transfers between devices with their start and end apart: 10, of which 7 were waited for; matrix products, arithmetic and copies ran while one was open for 0% of the time, Pallas kernels for 9%

profile of v5, /device:TPU:0, one launch (start us, length us, event | category | flops | bytes accessed | tf_op | source)
XLA Modules:
  0.0 24.0 jit_solution(14746893574466959753)
XLA Ops:
  0.0 0.0 copy-start.1
  0.0 0.0 copy-start
  0.0 3.1 %collective-permute-start.3 = (bf16[2,256,256]{2,1,0:T(8,128)(2,1)}, bf16[2,256,256]{2,1,0:T(8,128)(2,1)S(1)}, u32[]{:S(2)}, u32[]{:S(2)}) collective-permute-start(bf16[2,256,256]{2,1,0:T(8,128)(2,1)} %bitcast.9), channel_id=1, source_target_pairs={{0,4},{4,0},{8,12},{12,8},{1,5},{5,1},{9,13},{13,9},{2,6},{6,2},{1... | collective-permute-start | bytes 786440 | tf_op jit(solution)/shard_map/ppermute | solution.py:200
  3.8 0.0 copy-done.1
  3.8 0.0 copy-done
  3.8 0.0 copy-start.2
  3.8 1.5 %adjoint.1 = (bf16[2,128,256]{2,1,0:T(8,128)(2,1)S(1)}, bf16[2,128,256]{2,1,0:T(8,128)(2,1)S(1)}, bf16[16,256]{1,0:T(8,128)(2,1)S(1)}) custom-call(f32[8,128]{1,0:T(8,128)S(1)} %token_.1.token_ref, s32[1]{0:T(128)S(6)} %copy.8.slot_ref, s32[2,8]{1,0:T(2,128)} %bitcast.12, bf16[2,256,256]{2,1,0:T(8,128)(2,1)} %bitcast.11, f32[2,256,256]{2,1,0:T(8,128)S(1)} %copy-done.1, ...), custom_call_target="tpu_custom_call" | custom-call | tf_op jit(solution)/shard_map/adjoint/pallas_call | solution.py:179
  5.3 2.2 %collective-permute-start.1 = (bf16[2,128,256]{2,1,0:T(8,128)(2,1)S(1)}, bf16[2,128,256]{2,1,0:T(8,128)(2,1)S(1)}, u32[]{:S(2)}, u32[]{:S(2)}) collective-permute-start(bf16[2,128,256]{2,1,0:T(8,128)(2,1)S(1)} %get-tuple-element.18), channel_id=1, source_target_pairs={{0,2},{2,0},{4,6},{6,4},{8,10},{10,8},{12,14},{14,12},{1,3},{3,1},... | collective-permute-start | bytes 393224 | tf_op jit(solution)/shard_map/ppermute | solution.py:198
  7.5 0.0 collective-permute-start.2
  7.5 1.5 %collective-permute-start = (bf16[16,256]{1,0:T(8,128)(2,1)S(1)}, bf16[16,256]{1,0:T(8,128)(2,1)S(1)}, u32[]{:S(2)}, u32[]{:S(2)}) collective-permute-start(bf16[16,256]{1,0:T(8,128)(2,1)S(1)} %get-tuple-element.17.c0.in_ref), channel_id=1, source_target_pairs={{0,4},{4,0},{8,12},{12,8},{1,5},{5,1},{9,13},{13,9},{2,6},{6,2},{1... | collective-permute-start | bytes 24584 | tf_op jit(solution)/shard_map/ppermute | solution.py:201
  9.0 3.6 %collective-permute-done.c1 = bf16[16,256]{1,0:T(8,128)(2,1)S(1)} collective-permute-done((bf16[16,256]{1,0:T(8,128)(2,1)S(1)}, bf16[16,256]{1,0:T(8,128)(2,1)S(1)}, u32[]{:S(2)}, u32[]{:S(2)}) %collective-permute-start) | collective-permute-done | bytes 8224 | tf_op jit(solution)/shard_map/ppermute | solution.py:201
  12.6 0.0 collective-permute-done.3.w1
  12.7 0.0 copy-done.2
  12.7 0.4 %rolled_waves.1 = (bf16[2,128,256]{2,1,0:T(8,128)(2,1)S(1)}, bf16[2,128,256]{2,1,0:T(8,128)(2,1)S(1)}) custom-call(bf16[16,256]{1,0:T(8,128)(2,1)S(1)} %get-tuple-element.17.c0.in_ref, bf16[16,256]{1,0:T(8,128)(2,1)S(1)} %collective-permute-done.c1, bf16[2,256,256]{2,1,0:T(8,128)(2,1)S(1)} %bitcast.10, bf16[2,256,256]{2,1,0:T(8,128)(2,1)S(1)} %collective-permute-done.3.w1), custom_call_target="tpu_custom_call" | custom-call | tf_op jit(solution)/shard_map/rolled_waves/pallas_call | solution.py:202
  13.1 0.0 collective-permute-done.1.a0
  13.1 0.5 %collective-permute-done.2.a1 = bf16[2,128,256]{2,1,0:T(8,128)(2,1)S(1)} collective-permute-done((bf16[2,128,256]{2,1,0:T(8,128)(2,1)S(1)}, bf16[2,128,256]{2,1,0:T(8,128)(2,1)S(1)}, u32[]{:S(2)}, u32[]{:S(2)}) %collective-permute-start.2) | collective-permute-done | bytes 131104 | tf_op jit(solution)/shard_map/ppermute | solution.py:199
  13.6 0.2 far_sums.1
  13.8 0.1 collective-permute-start.4
  13.9 0.2 near_sums.1
  14.2 1.1 %collective-permute-done.4 = bf16[2,128,256]{2,1,0:T(8,128)(2,1)S(1)} collective-permute-done((bf16[2,128,256]{2,1,0:T(8,128)(2,1)S(1)}, bf16[2,128,256]{2,1,0:T(8,128)(2,1)S(1)}, u32[]{:S(2)}, u32[]{:S(2)}) %collective-permute-start.4) | collective-permute-done | bytes 131104 | tf_op jit(solution)/shard_map/ppermute | solution.py:221
  15.3 2.7 %collective-permute-start.5 = (bf16[2,128,256]{2,1,0:T(8,128)(2,1)S(1)}, bf16[2,128,256]{2,1,0:T(8,128)(2,1)S(1)}, u32[]{:S(2)}, u32[]{:S(2)}) collective-permute-start(bf16[2,128,256]{2,1,0:T(8,128)(2,1)S(1)} %after.5), channel_id=1, source_target_pairs={{0,8},{1,9},{4,5},{5,4},{8,0},{9,1},{12,13},{13,12},{2,10},{3,11},... | collective-permute-start | bytes 393224 | tf_op jit(solution)/shard_map/ppermute | solution.py:239
  18.0 0.0 collective-permute-start.7
  18.0 1.2 %collective-permute-done.7.refs_0_ = bf16[16,256]{1,0:T(8,128)(2,1)S(1)} collective-permute-done((bf16[16,256]{1,0:T(8,128)(2,1)S(1)}, bf16[16,256]{1,0:T(8,128)(2,1)S(1)}, u32[]{:S(2)}, u32[]{:S(2)}) %collective-permute-start.7) | collective-permute-done | bytes 8224 | tf_op jit(solution)/shard_map/ppermute | solution.py:238
  19.1 0.2 collective-permute-start.8
  19.3 1.0 %collective-permute-done.8.refs_0_ = bf16[16,256]{1,0:T(8,128)(2,1)S(1)} collective-permute-done((bf16[16,256]{1,0:T(8,128)(2,1)S(1)}, bf16[16,256]{1,0:T(8,128)(2,1)S(1)}, u32[]{:S(2)}, u32[]{:S(2)}) %collective-permute-start.8) | collective-permute-done | bytes 8224 | tf_op jit(solution)/shard_map/ppermute | solution.py:240
  20.3 0.2 collective-permute-start.9
  20.6 1.3 %collective-permute-done.5.refs_0_ = bf16[2,128,256]{2,1,0:T(8,128)(2,1)S(1)} collective-permute-done((bf16[2,128,256]{2,1,0:T(8,128)(2,1)S(1)}, bf16[2,128,256]{2,1,0:T(8,128)(2,1)S(1)}, u32[]{:S(2)}, u32[]{:S(2)}) %collective-permute-start.5) | collective-permute-done | bytes 131104 | tf_op jit(solution)/shard_map/ppermute | solution.py:239
  21.8 0.1 collective-permute-start.6
  21.9 0.0 collective-permute-done.9
  21.9 1.3 %collective-permute-done.6 = bf16[2,128,256]{2,1,0:T(8,128)(2,1)S(1)} collective-permute-done((bf16[2,128,256]{2,1,0:T(8,128)(2,1)S(1)}, bf16[2,128,256]{2,1,0:T(8,128)(2,1)S(1)}, u32[]{:S(2)}, u32[]{:S(2)}) %collective-permute-start.6) | collective-permute-done | bytes 131104 | tf_op jit(solution)/shard_map/ppermute | solution.py:241
  23.3 0.8 %add_bitcast_fusion = f32[2,1,128,256]{3,2,1,0:T(8,128)} fusion(f32[2,128,256]{2,1,0:T(8,128)S(1)} %get-tuple-element.23, bf16[2,128,256]{2,1,0:T(8,128)(2,1)S(1)} %collective-permute-done.6, bf16[2,128,256]{2,1,0:T(8,128)(2,1)S(1)} %collective-permute-done.9, bf16[2,128,256]{2,1,0:T(8,128)(2,1)S(1)} %collective-permute-done.5.refs_0_, pred[]{:T(512)S(6)} %eq.5), kind=kLoop, calls=%fused_computation | loop fusion | flops 327680 | bytes 917505 | tf_op jit(solution)/shard_map/broadcast_in_dim | solution.py:244
  (7 shorter events, 0.1 us)
Async XLA Ops:
  0.0 3.8 %copy-start.1 = (f32[2,256,256]{2,1,0:T(8,128)S(1)}, f32[2,256,256]{2,1,0:T(8,128)}, u32[]{:S(2)}) copy-start(f32[2,256,256]{2,1,0:T(8,128)} %constant.21.clone.table_ref) | copy-start | bytes 1572868
  0.0 3.8 %copy-start = (f32[1,2,256,256]{3,2,1,0:T(8,128)S(1)}, f32[1,2,256,256]{3,2,1,0:T(8,128)}, u32[]{:S(2)}) copy-start(f32[1,2,256,256]{3,2,1,0:T(8,128)} %param.8) | copy-start | bytes 1572868
  0.0 12.6 %collective-permute-start.3 = (bf16[2,256,256]{2,1,0:T(8,128)(2,1)}, bf16[2,256,256]{2,1,0:T(8,128)(2,1)S(1)}, u32[]{:S(2)}, u32[]{:S(2)}) collective-permute-start(bf16[2,256,256]{2,1,0:T(8,128)(2,1)} %bitcast.9), channel_id=1, source_target_pairs={{0,4},{4,0},{8,12},{12,8},{1,5},{5,1},{9,13},{13,9},{2,6},{6,2},{1... | collective-permute-start | bytes 786440 | tf_op jit(solution)/shard_map/ppermute | solution.py:200
  3.8 8.9 %copy-start.2 = (bf16[1,1,2,256,256]{4,3,2,1,0:T(8,128)(2,1)S(1)}, bf16[1,1,2,256,256]{4,3,2,1,0:T(8,128)(2,1)}, u32[]{:S(2)}) copy-start(bf16[1,1,2,256,256]{4,3,2,1,0:T(8,128)(2,1)} %param.6) | copy-start | bytes 786436
  5.3 7.8 %collective-permute-start.1 = (bf16[2,128,256]{2,1,0:T(8,128)(2,1)S(1)}, bf16[2,128,256]{2,1,0:T(8,128)(2,1)S(1)}, u32[]{:S(2)}, u32[]{:S(2)}) collective-permute-start(bf16[2,128,256]{2,1,0:T(8,128)(2,1)S(1)} %get-tuple-element.18), channel_id=1, source_target_pairs={{0,2},{2,0},{4,6},{6,4},{8,10},{10,8},{12,14},{14,12},{1,3},{3,1},... | collective-permute-start | bytes 393224 | tf_op jit(solution)/shard_map/ppermute | solution.py:198
  7.5 6.1 %collective-permute-start.2 = (bf16[2,128,256]{2,1,0:T(8,128)(2,1)S(1)}, bf16[2,128,256]{2,1,0:T(8,128)(2,1)S(1)}, u32[]{:S(2)}, u32[]{:S(2)}) collective-permute-start(bf16[2,128,256]{2,1,0:T(8,128)(2,1)S(1)} %get-tuple-element.19), channel_id=1, source_target_pairs={{0,6},{2,4},{4,2},{6,0},{8,14},{10,12},{12,10},{14,8},{1,7},{3,5},... | collective-permute-start | bytes 393224 | tf_op jit(solution)/shard_map/ppermute | solution.py:199
  7.5 5.2 %collective-permute-start = (bf16[16,256]{1,0:T(8,128)(2,1)S(1)}, bf16[16,256]{1,0:T(8,128)(2,1)S(1)}, u32[]{:S(2)}, u32[]{:S(2)}) collective-permute-start(bf16[16,256]{1,0:T(8,128)(2,1)S(1)} %get-tuple-element.17.c0.in_ref), channel_id=1, source_target_pairs={{0,4},{4,0},{8,12},{12,8},{1,5},{5,1},{9,13},{13,9},{2,6},{6,2},{1... | collective-permute-start | bytes 24584 | tf_op jit(solution)/shard_map/ppermute | solution.py:201
  13.8 1.4 %collective-permute-start.4 = (bf16[2,128,256]{2,1,0:T(8,128)(2,1)S(1)}, bf16[2,128,256]{2,1,0:T(8,128)(2,1)S(1)}, u32[]{:S(2)}, u32[]{:S(2)}) collective-permute-start(bf16[2,128,256]{2,1,0:T(8,128)(2,1)S(1)} %get-tuple-element.26), channel_id=1, source_target_pairs={{0,1},{1,0},{2,3},{3,2},{4,5},{5,4},{6,7},{7,6},{8,9},{9,8},{10,11... | collective-permute-start | bytes 393224 | tf_op jit(solution)/shard_map/ppermute | solution.py:221
  15.3 6.5 %collective-permute-start.5 = (bf16[2,128,256]{2,1,0:T(8,128)(2,1)S(1)}, bf16[2,128,256]{2,1,0:T(8,128)(2,1)S(1)}, u32[]{:S(2)}, u32[]{:S(2)}) collective-permute-start(bf16[2,128,256]{2,1,0:T(8,128)(2,1)S(1)} %after.5), channel_id=1, source_target_pairs={{0,8},{1,9},{4,5},{5,4},{8,0},{9,1},{12,13},{13,12},{2,10},{3,11},... | collective-permute-start | bytes 393224 | tf_op jit(solution)/shard_map/ppermute | solution.py:239
  18.0 1.2 %collective-permute-start.7 = (bf16[16,256]{1,0:T(8,128)(2,1)S(1)}, bf16[16,256]{1,0:T(8,128)(2,1)S(1)}, u32[]{:S(2)}, u32[]{:S(2)}) collective-permute-start(bf16[16,256]{1,0:T(8,128)(2,1)S(1)} %after.7), channel_id=1, source_target_pairs={{0,1},{1,0},{2,3},{3,2},{4,5},{5,4},{6,7},{7,6},{8,9},{9,8},{10,11... | collective-permute-start | bytes 24584 | tf_op jit(solution)/shard_map/ppermute | solution.py:238
  19.1 1.2 %collective-permute-start.8 = (bf16[16,256]{1,0:T(8,128)(2,1)S(1)}, bf16[16,256]{1,0:T(8,128)(2,1)S(1)}, u32[]{:S(2)}, u32[]{:S(2)}) collective-permute-start(bf16[16,256]{1,0:T(8,128)(2,1)S(1)} %after.8), channel_id=1, source_target_pairs={{0,1},{1,0},{2,3},{3,2},{4,5},{5,4},{6,7},{7,6},{8,9},{9,8},{10,11... | collective-permute-start | bytes 24584 | tf_op jit(solution)/shard_map/ppermute | solution.py:240
  20.3 1.6 %collective-permute-start.9 = (bf16[2,128,256]{2,1,0:T(8,128)(2,1)S(1)}, bf16[2,128,256]{2,1,0:T(8,128)(2,1)S(1)}, u32[]{:S(2)}, u32[]{:S(2)}) collective-permute-start(bf16[2,128,256]{2,1,0:T(8,128)(2,1)S(1)} %after.9), channel_id=1, source_target_pairs={{0,1},{1,0},{4,12},{5,13},{8,9},{9,8},{12,4},{13,5},{2,3},{3,2},{6... | collective-permute-start | bytes 393224 | tf_op jit(solution)/shard_map/ppermute | solution.py:242
  21.8 1.4 %collective-permute-start.6 = (bf16[2,128,256]{2,1,0:T(8,128)(2,1)S(1)}, bf16[2,128,256]{2,1,0:T(8,128)(2,1)S(1)}, u32[]{:S(2)}, u32[]{:S(2)}) collective-permute-start(bf16[2,128,256]{2,1,0:T(8,128)(2,1)S(1)} %after.6), channel_id=1, source_target_pairs={{0,1},{1,0},{2,3},{3,2},{4,5},{5,4},{6,7},{7,6},{8,9},{9,8},{10,11... | collective-permute-start | bytes 393224 | tf_op jit(solution)/shard_map/ppermute | solution.py:241

commit v6 on v5

--- a/solution.py
+++ b/solution.py
@@ -1,5 +1,4 @@
 import functools
-import math
 
 import jax
 import jax.numpy as jnp
@@ -50,19 +49,14 @@
     return a[0] * b[0] + a[1] * b[1], a[0] * b[1] - a[1] * b[0]
 
 
-def own_and_other(half):
-    parity = lax.rem(lax.axis_index("probe"), 2)
-    return (pl.ds(pl.multiple_of(n * half, half), half) for n in (parity, 1 - parity))
-
-
 def send_kernel(
-    token_ref, slot_ref, offsets_hbm, layer_hbm, table_ref, residual_ref,
+    early_ref, slot_ref, offsets_hbm, layer_hbm, table_ref, residual_ref,
     own_ref, other_ref, corner_ref,
     offsets_ref, layer_ref, sems,
 ):
     side = layer_ref.shape[-1]
     half = side // 2
-    del token_ref
+    del early_ref
     offsets_copy = pltpu.make_async_copy(offsets_hbm, offsets_ref, sems.at[0])
     layer_copy = pltpu.make_async_copy(layer_hbm, layer_ref, sems.at[1])
     offsets_copy.start()
@@ -151,7 +145,7 @@
     refs[-1][...] = in_ref[...]
 
 
-def token_kernel(out_ref):
+def early_kernel(out_ref):
     out_ref[...] = jnp.zeros_like(out_ref)
 
 
@@ -167,15 +161,15 @@
     block, sums = (jax.ShapeDtypeStruct((2, half, side), t) for t in (jnp.bfloat16, jnp.float32))
     params = pltpu.CompilerParams(vmem_limit_bytes=32 * 1024 * 1024)
     by_column = offsets.T
-    token = pl.pallas_call(
-        token_kernel,
+    early = pl.pallas_call(
+        early_kernel,
         out_shape=jax.ShapeDtypeStruct((8, 128), jnp.float32),
         out_specs=vmem,
         compiler_params=params,
         cost_estimate=pl.CostEstimate(flops=3 * 10**8, bytes_accessed=0, transcendentals=0),
-        name="token",
+        name="early",
     )()
-    waves, token = lax.optimization_barrier((stored_waves[0, 0], token))
+    waves, early = lax.optimization_barrier((stored_waves[0, 0], early))
     adj_own, adj_other, corner = pl.pallas_call(
         send_kernel,
         out_shape=(block, block, jax.ShapeDtypeStruct((CORNER_ROWS, side), jnp.bfloat16)),
@@ -188,7 +182,7 @@
         ],
         compiler_params=params,
         name="adjoint",
-    )(token, slot_position, *in_hbm(by_column, transmission[0, 0]), table, residual[0])
+    )(early, slot_position, *in_hbm(by_column, transmission[0, 0]), table, residual[0])
 
     probe_count = lax.axis_size("probe")
     swap_tile = [(0, 1), (1, 0)]
@@ -293,6 +287,7 @@
 
     def per_device(stored_waves, *rest):
         small = (sizes["depth"], sizes["probe"], sizes["tile"], stored_waves.shape[1]) == (2, 4, 2, 1)
+        small = small and 2 * stored_waves.shape[-1] == OBJ
         return (two_slices if small else any_slices)(stored_waves, *rest)
 
     slots = ("groups", "probe", "tile")

time: 24.2 us -> 24.2 us (level)
  no operation moved by 1% of the time
where the time goes in v6:
time: 24.2 us; the launch traced here: 24 us
  starting transfers between devices  10 us (41%)
  waiting for transfers between devices  9.99 us (41%)
  Pallas kernels  2.4 us (10%)
  other arithmetic  0.79 us (3%)
  between operations  0.77 us (3%)
    ppermute x1, waiting for transfers between devices, two_slices(): corner_next = lax.ppermute(corner, 'probe', z1)  3.61 us
    ppermute x1, starting transfers between devices, two_slices(): w_next = lax.ppermute(waves, 'probe', z1)  3.09 us
    ppermute x1, starting transfers between devices, two_slices(): first = lax.ppermute(after(send, side_keep), ('probe', 'tile'), even_far)  2.65 us
    ppermute x1, starting transfers between devices, two_slices(): a_own = lax.ppermute(adj_own, ('probe', 'depth'), flip)  2.22 us
    ppermute x1, starting transfers between devices, two_slices(): corner_next = lax.ppermute(corner, 'probe', z1)  1.54 us
    pallas_call x1, Pallas kernels, two_slices(): pl.pallas_call(send_kernel, out_shape=(block, block, jax.ShapeDtypeStruct...  1.49 us
    ppermute x1, waiting for transfers between devices, two_slices(): near = lax.ppermute(after(side_keep, first), 'tile', swap_tile)  1.31 us
    ppermute x1, waiting for transfers between devices, two_slices(): first = lax.ppermute(after(send, side_keep), ('probe', 'tile'), even_far)  1.26 us
  transfers between devices with their start and end apart: 10, of which 7 were waited for; matrix products, arithmetic and copies ran while one was open for 0% of the time, Pallas kernels for 9%

profile of v6, /device:TPU:0, one launch (start us, length us, event | category | flops | bytes accessed | tf_op | source)
XLA Modules:
  0.0 24.0 jit_solution(14746893574466959753)
XLA Ops:
  0.0 0.0 copy-start.1
  0.0 0.0 copy-start
  0.0 3.1 %collective-permute-start.3 = (bf16[2,256,256]{2,1,0:T(8,128)(2,1)}, bf16[2,256,256]{2,1,0:T(8,128)(2,1)S(1)}, u32[]{:S(2)}, u32[]{:S(2)}) collective-permute-start(bf16[2,256,256]{2,1,0:T(8,128)(2,1)} %bitcast.9), channel_id=1, source_target_pairs={{0,4},{4,0},{8,12},{12,8},{1,5},{5,1},{9,13},{13,9},{2,6},{6,2},{1... | collective-permute-start | bytes 786440 | tf_op jit(solution)/shard_map/ppermute | solution.py:194
  3.8 0.0 copy-done.1
  3.8 0.0 copy-done
  3.8 0.0 copy-start.2
  3.8 1.5 %adjoint.1 = (bf16[2,128,256]{2,1,0:T(8,128)(2,1)S(1)}, bf16[2,128,256]{2,1,0:T(8,128)(2,1)S(1)}, bf16[16,256]{1,0:T(8,128)(2,1)S(1)}) custom-call(f32[8,128]{1,0:T(8,128)S(1)} %early.1.early_ref, s32[1]{0:T(128)S(6)} %copy.8.slot_ref, s32[2,8]{1,0:T(2,128)} %bitcast.12, bf16[2,256,256]{2,1,0:T(8,128)(2,1)} %bitcast.11, f32[2,256,256]{2,1,0:T(8,128)S(1)} %copy-done.1, ...), custom_call_target="tpu_custom_call" | custom-call | tf_op jit(solution)/shard_map/adjoint/pallas_call | solution.py:173
  5.3 2.2 %collective-permute-start.1 = (bf16[2,128,256]{2,1,0:T(8,128)(2,1)S(1)}, bf16[2,128,256]{2,1,0:T(8,128)(2,1)S(1)}, u32[]{:S(2)}, u32[]{:S(2)}) collective-permute-start(bf16[2,128,256]{2,1,0:T(8,128)(2,1)S(1)} %get-tuple-element.18), channel_id=1, source_target_pairs={{0,2},{2,0},{4,6},{6,4},{8,10},{10,8},{12,14},{14,12},{1,3},{3,1},... | collective-permute-start | bytes 393224 | tf_op jit(solution)/shard_map/ppermute | solution.py:192
  7.5 0.0 collective-permute-start.2
  7.5 1.5 %collective-permute-start = (bf16[16,256]{1,0:T(8,128)(2,1)S(1)}, bf16[16,256]{1,0:T(8,128)(2,1)S(1)}, u32[]{:S(2)}, u32[]{:S(2)}) collective-permute-start(bf16[16,256]{1,0:T(8,128)(2,1)S(1)} %get-tuple-element.17.c0.in_ref), channel_id=1, source_target_pairs={{0,4},{4,0},{8,12},{12,8},{1,5},{5,1},{9,13},{13,9},{2,6},{6,2},{1... | collective-permute-start | bytes 24584 | tf_op jit(solution)/shard_map/ppermute | solution.py:195
  9.0 3.6 %collective-permute-done.c1 = bf16[16,256]{1,0:T(8,128)(2,1)S(1)} collective-permute-done((bf16[16,256]{1,0:T(8,128)(2,1)S(1)}, bf16[16,256]{1,0:T(8,128)(2,1)S(1)}, u32[]{:S(2)}, u32[]{:S(2)}) %collective-permute-start) | collective-permute-done | bytes 8224 | tf_op jit(solution)/shard_map/ppermute | solution.py:195
  12.6 0.0 collective-permute-done.3.w1
  12.7 0.0 copy-done.2
  12.7 0.4 %rolled_waves.1 = (bf16[2,128,256]{2,1,0:T(8,128)(2,1)S(1)}, bf16[2,128,256]{2,1,0:T(8,128)(2,1)S(1)}) custom-call(bf16[16,256]{1,0:T(8,128)(2,1)S(1)} %get-tuple-element.17.c0.in_ref, bf16[16,256]{1,0:T(8,128)(2,1)S(1)} %collective-permute-done.c1, bf16[2,256,256]{2,1,0:T(8,128)(2,1)S(1)} %bitcast.10, bf16[2,256,256]{2,1,0:T(8,128)(2,1)S(1)} %collective-permute-done.3.w1), custom_call_target="tpu_custom_call" | custom-call | tf_op jit(solution)/shard_map/rolled_waves/pallas_call | solution.py:196
  13.1 0.0 collective-permute-done.1.a0
  13.1 0.5 %collective-permute-done.2.a1 = bf16[2,128,256]{2,1,0:T(8,128)(2,1)S(1)} collective-permute-done((bf16[2,128,256]{2,1,0:T(8,128)(2,1)S(1)}, bf16[2,128,256]{2,1,0:T(8,128)(2,1)S(1)}, u32[]{:S(2)}, u32[]{:S(2)}) %collective-permute-start.2) | collective-permute-done | bytes 131104 | tf_op jit(solution)/shard_map/ppermute | solution.py:193
  13.6 0.2 far_sums.1
  13.8 0.1 collective-permute-start.4
  13.9 0.2 near_sums.1
  14.2 1.1 %collective-permute-done.4 = bf16[2,128,256]{2,1,0:T(8,128)(2,1)S(1)} collective-permute-done((bf16[2,128,256]{2,1,0:T(8,128)(2,1)S(1)}, bf16[2,128,256]{2,1,0:T(8,128)(2,1)S(1)}, u32[]{:S(2)}, u32[]{:S(2)}) %collective-permute-start.4) | collective-permute-done | bytes 131104 | tf_op jit(solution)/shard_map/ppermute | solution.py:215
  15.3 2.7 %collective-permute-start.5 = (bf16[2,128,256]{2,1,0:T(8,128)(2,1)S(1)}, bf16[2,128,256]{2,1,0:T(8,128)(2,1)S(1)}, u32[]{:S(2)}, u32[]{:S(2)}) collective-permute-start(bf16[2,128,256]{2,1,0:T(8,128)(2,1)S(1)} %after.5), channel_id=1, source_target_pairs={{0,8},{1,9},{4,5},{5,4},{8,0},{9,1},{12,13},{13,12},{2,10},{3,11},... | collective-permute-start | bytes 393224 | tf_op jit(solution)/shard_map/ppermute | solution.py:233
  18.0 0.0 collective-permute-start.7
  18.0 1.2 %collective-permute-done.7.refs_0_ = bf16[16,256]{1,0:T(8,128)(2,1)S(1)} collective-permute-done((bf16[16,256]{1,0:T(8,128)(2,1)S(1)}, bf16[16,256]{1,0:T(8,128)(2,1)S(1)}, u32[]{:S(2)}, u32[]{:S(2)}) %collective-permute-start.7) | collective-permute-done | bytes 8224 | tf_op jit(solution)/shard_map/ppermute | solution.py:232
  19.1 0.2 collective-permute-start.8
  19.3 1.0 %collective-permute-done.8.refs_0_ = bf16[16,256]{1,0:T(8,128)(2,1)S(1)} collective-permute-done((bf16[16,256]{1,0:T(8,128)(2,1)S(1)}, bf16[16,256]{1,0:T(8,128)(2,1)S(1)}, u32[]{:S(2)}, u32[]{:S(2)}) %collective-permute-start.8) | collective-permute-done | bytes 8224 | tf_op jit(solution)/shard_map/ppermute | solution.py:234
  20.3 0.2 collective-permute-start.9
  20.6 1.3 %collective-permute-done.5.refs_0_ = bf16[2,128,256]{2,1,0:T(8,128)(2,1)S(1)} collective-permute-done((bf16[2,128,256]{2,1,0:T(8,128)(2,1)S(1)}, bf16[2,128,256]{2,1,0:T(8,128)(2,1)S(1)}, u32[]{:S(2)}, u32[]{:S(2)}) %collective-permute-start.5) | collective-permute-done | bytes 131104 | tf_op jit(solution)/shard_map/ppermute | solution.py:233
  21.8 0.1 collective-permute-start.6
  21.9 0.0 collective-permute-done.9
  21.9 1.3 %collective-permute-done.6 = bf16[2,128,256]{2,1,0:T(8,128)(2,1)S(1)} collective-permute-done((bf16[2,128,256]{2,1,0:T(8,128)(2,1)S(1)}, bf16[2,128,256]{2,1,0:T(8,128)(2,1)S(1)}, u32[]{:S(2)}, u32[]{:S(2)}) %collective-permute-start.6) | collective-permute-done | bytes 131104 | tf_op jit(solution)/shard_map/ppermute | solution.py:235
  23.3 0.8 %add_bitcast_fusion = f32[2,1,128,256]{3,2,1,0:T(8,128)} fusion(f32[2,128,256]{2,1,0:T(8,128)S(1)} %get-tuple-element.23, bf16[2,128,256]{2,1,0:T(8,128)(2,1)S(1)} %collective-permute-done.6, bf16[2,128,256]{2,1,0:T(8,128)(2,1)S(1)} %collective-permute-done.9, bf16[2,128,256]{2,1,0:T(8,128)(2,1)S(1)} %collective-permute-done.5.refs_0_, pred[]{:T(512)S(6)} %eq.5), kind=kLoop, calls=%fused_computation | loop fusion | flops 327680 | bytes 917505 | tf_op jit(solution)/shard_map/broadcast_in_dim | solution.py:238
  (7 shorter events, 0.1 us)
Async XLA Ops:
  0.0 3.8 %copy-start.1 = (f32[2,256,256]{2,1,0:T(8,128)S(1)}, f32[2,256,256]{2,1,0:T(8,128)}, u32[]{:S(2)}) copy-start(f32[2,256,256]{2,1,0:T(8,128)} %constant.21.clone.table_ref) | copy-start | bytes 1572868
  0.0 3.8 %copy-start = (f32[1,2,256,256]{3,2,1,0:T(8,128)S(1)}, f32[1,2,256,256]{3,2,1,0:T(8,128)}, u32[]{:S(2)}) copy-start(f32[1,2,256,256]{3,2,1,0:T(8,128)} %param.8) | copy-start | bytes 1572868
  0.0 12.6 %collective-permute-start.3 = (bf16[2,256,256]{2,1,0:T(8,128)(2,1)}, bf16[2,256,256]{2,1,0:T(8,128)(2,1)S(1)}, u32[]{:S(2)}, u32[]{:S(2)}) collective-permute-start(bf16[2,256,256]{2,1,0:T(8,128)(2,1)} %bitcast.9), channel_id=1, source_target_pairs={{0,4},{4,0},{8,12},{12,8},{1,5},{5,1},{9,13},{13,9},{2,6},{6,2},{1... | collective-permute-start | bytes 786440 | tf_op jit(solution)/shard_map/ppermute | solution.py:194
  3.8 8.9 %copy-start.2 = (bf16[1,1,2,256,256]{4,3,2,1,0:T(8,128)(2,1)S(1)}, bf16[1,1,2,256,256]{4,3,2,1,0:T(8,128)(2,1)}, u32[]{:S(2)}) copy-start(bf16[1,1,2,256,256]{4,3,2,1,0:T(8,128)(2,1)} %param.6) | copy-start | bytes 786436
  5.3 7.8 %collective-permute-start.1 = (bf16[2,128,256]{2,1,0:T(8,128)(2,1)S(1)}, bf16[2,128,256]{2,1,0:T(8,128)(2,1)S(1)}, u32[]{:S(2)}, u32[]{:S(2)}) collective-permute-start(bf16[2,128,256]{2,1,0:T(8,128)(2,1)S(1)} %get-tuple-element.18), channel_id=1, source_target_pairs={{0,2},{2,0},{4,6},{6,4},{8,10},{10,8},{12,14},{14,12},{1,3},{3,1},... | collective-permute-start | bytes 393224 | tf_op jit(solution)/shard_map/ppermute | solution.py:192
  7.5 6.1 %collective-permute-start.2 = (bf16[2,128,256]{2,1,0:T(8,128)(2,1)S(1)}, bf16[2,128,256]{2,1,0:T(8,128)(2,1)S(1)}, u32[]{:S(2)}, u32[]{:S(2)}) collective-permute-start(bf16[2,128,256]{2,1,0:T(8,128)(2,1)S(1)} %get-tuple-element.19), channel_id=1, source_target_pairs={{0,6},{2,4},{4,2},{6,0},{8,14},{10,12},{12,10},{14,8},{1,7},{3,5},... | collective-permute-start | bytes 393224 | tf_op jit(solution)/shard_map/ppermute | solution.py:193
  7.5 5.2 %collective-permute-start = (bf16[16,256]{1,0:T(8,128)(2,1)S(1)}, bf16[16,256]{1,0:T(8,128)(2,1)S(1)}, u32[]{:S(2)}, u32[]{:S(2)}) collective-permute-start(bf16[16,256]{1,0:T(8,128)(2,1)S(1)} %get-tuple-element.17.c0.in_ref), channel_id=1, source_target_pairs={{0,4},{4,0},{8,12},{12,8},{1,5},{5,1},{9,13},{13,9},{2,6},{6,2},{1... | collective-permute-start | bytes 24584 | tf_op jit(solution)/shard_map/ppermute | solution.py:195
  13.8 1.4 %collective-permute-start.4 = (bf16[2,128,256]{2,1,0:T(8,128)(2,1)S(1)}, bf16[2,128,256]{2,1,0:T(8,128)(2,1)S(1)}, u32[]{:S(2)}, u32[]{:S(2)}) collective-permute-start(bf16[2,128,256]{2,1,0:T(8,128)(2,1)S(1)} %get-tuple-element.26), channel_id=1, source_target_pairs={{0,1},{1,0},{2,3},{3,2},{4,5},{5,4},{6,7},{7,6},{8,9},{9,8},{10,11... | collective-permute-start | bytes 393224 | tf_op jit(solution)/shard_map/ppermute | solution.py:215
  15.3 6.5 %collective-permute-start.5 = (bf16[2,128,256]{2,1,0:T(8,128)(2,1)S(1)}, bf16[2,128,256]{2,1,0:T(8,128)(2,1)S(1)}, u32[]{:S(2)}, u32[]{:S(2)}) collective-permute-start(bf16[2,128,256]{2,1,0:T(8,128)(2,1)S(1)} %after.5), channel_id=1, source_target_pairs={{0,8},{1,9},{4,5},{5,4},{8,0},{9,1},{12,13},{13,12},{2,10},{3,11},... | collective-permute-start | bytes 393224 | tf_op jit(solution)/shard_map/ppermute | solution.py:233
  18.0 1.2 %collective-permute-start.7 = (bf16[16,256]{1,0:T(8,128)(2,1)S(1)}, bf16[16,256]{1,0:T(8,128)(2,1)S(1)}, u32[]{:S(2)}, u32[]{:S(2)}) collective-permute-start(bf16[16,256]{1,0:T(8,128)(2,1)S(1)} %after.7), channel_id=1, source_target_pairs={{0,1},{1,0},{2,3},{3,2},{4,5},{5,4},{6,7},{7,6},{8,9},{9,8},{10,11... | collective-permute-start | bytes 24584 | tf_op jit(solution)/shard_map/ppermute | solution.py:232
  19.1 1.2 %collective-permute-start.8 = (bf16[16,256]{1,0:T(8,128)(2,1)S(1)}, bf16[16,256]{1,0:T(8,128)(2,1)S(1)}, u32[]{:S(2)}, u32[]{:S(2)}) collective-permute-start(bf16[16,256]{1,0:T(8,128)(2,1)S(1)} %after.8), channel_id=1, source_target_pairs={{0,1},{1,0},{2,3},{3,2},{4,5},{5,4},{6,7},{7,6},{8,9},{9,8},{10,11... | collective-permute-start | bytes 24584 | tf_op jit(solution)/shard_map/ppermute | solution.py:234
  20.3 1.6 %collective-permute-start.9 = (bf16[2,128,256]{2,1,0:T(8,128)(2,1)S(1)}, bf16[2,128,256]{2,1,0:T(8,128)(2,1)S(1)}, u32[]{:S(2)}, u32[]{:S(2)}) collective-permute-start(bf16[2,128,256]{2,1,0:T(8,128)(2,1)S(1)} %after.9), channel_id=1, source_target_pairs={{0,1},{1,0},{4,12},{5,13},{8,9},{9,8},{12,4},{13,5},{2,3},{3,2},{6... | collective-permute-start | bytes 393224 | tf_op jit(solution)/shard_map/ppermute | solution.py:236
  21.8 1.4 %collective-permute-start.6 = (bf16[2,128,256]{2,1,0:T(8,128)(2,1)S(1)}, bf16[2,128,256]{2,1,0:T(8,128)(2,1)S(1)}, u32[]{:S(2)}, u32[]{:S(2)}) collective-permute-start(bf16[2,128,256]{2,1,0:T(8,128)(2,1)S(1)} %after.6), channel_id=1, source_target_pairs={{0,1},{1,0},{2,3},{3,2},{4,5},{5,4},{6,7},{7,6},{8,9},{9,8},{10,11... | collective-permute-start | bytes 393224 | tf_op jit(solution)/shard_map/ppermute | solution.py:235

commit v7 on v6

--- a/solution.py
+++ b/solution.py
@@ -119,7 +119,7 @@
         out[1] = moved[half:]
 
 
-def sums_kernel(near, c0, c1, a0, a1, w0, w1, here_ref, side_ref):
+def sums_kernel(near, wanted, c0, c1, a0, a1, w0, w1, *refs):
     half, side = a0.shape[1:]
     place = lax.axis_index("probe")
     strip = (place >= 2) == near
@@ -136,9 +136,9 @@
         gradient = [jnp.where(inside, x, zero) for x in conj_times(wave, adjoint)]
         here = [total + jnp.where(own, x, zero) for total, x in zip(here, gradient)]
         side_sums = [total + jnp.where(own, zero, x) for total, x in zip(side_sums, gradient)]
-    for part in range(2):
-        here_ref[part] = here[part]
-        side_ref[part] = side_sums[part].astype(jnp.bfloat16)
+    for ref, result in zip(refs, (here, side_sums)[wanted]):
+        for part in range(2):
+            ref[part] = result[part].astype(ref.dtype)
 
 
 def copy_kernel(in_ref, *refs):
@@ -201,17 +201,18 @@
         compiler_params=params,
         name="rolled_waves",
     )(corner, corner_next, waves, w_next)
-    (send, side_send), (keep, side_keep) = (
-        pl.pallas_call(
-            functools.partial(sums_kernel, near),
-            out_shape=(sums, block),
+    def masked_sums(near, wanted, *shapes):
+        return pl.pallas_call(
+            functools.partial(sums_kernel, near, wanted),
+            out_shape=shapes,
             in_specs=[vmem] * 6,
-            out_specs=(vmem,) * 2,
+            out_specs=(vmem,) * len(shapes),
             compiler_params=params,
             name="near_sums" if near else "far_sums",
         )(corner, corner_next, a_own, a_next, w_own, w_next)
-        for near in (False, True)
-    )
+
+    (side_send,), (send,) = masked_sums(False, slice(1, 2), block), masked_sums(False, slice(0, 1), sums)
+    keep, side_keep = masked_sums(True, slice(0, 2), sums, block)
     send = (send + lax.ppermute(side_send, "tile", swap_tile).astype(jnp.float32)).astype(jnp.bfloat16)
 
     def after(x, *earlier):

time: 24.2 us -> 24.2 us (level)
    pallas_call x2 -> x3, Pallas kernels: 0.47 us -> 0.66 us  [masked_sums(): pl.pallas_call(functools.partial(sums_kernel, near, wanted), out_shape=sh...]
  transfers between devices with their start and end apart: 10 -> 10, of which waited for: 7 -> 7; matrix products, arithmetic and copies ran while one was open for 0% -> 0% of each run, Pallas kernels for 9% -> 10%
where the time goes in v7:
time: 24.2 us; the launch traced here: 24 us
  starting transfers between devices  10 us (41%)
  waiting for transfers between devices  9.76 us (40%)
  Pallas kernels  2.6 us (11%)
  other arithmetic  0.78 us (3%)
  between operations  0.78 us (3%)
    ppermute x1, waiting for transfers between devices, two_slices(): corner_next = lax.ppermute(corner, 'probe', z1)  3.61 us
    ppermute x1, starting transfers between devices, two_slices(): w_next = lax.ppermute(waves, 'probe', z1)  3.09 us
    ppermute x1, starting transfers between devices, two_slices(): first = lax.ppermute(after(send, side_keep), ('probe', 'tile'), even_far)  2.65 us
    ppermute x1, starting transfers between devices, two_slices(): a_own = lax.ppermute(adj_own, ('probe', 'depth'), flip)  2.22 us
    ppermute x1, starting transfers between devices, two_slices(): corner_next = lax.ppermute(corner, 'probe', z1)  1.54 us
    pallas_call x1, Pallas kernels, two_slices(): pl.pallas_call(send_kernel, out_shape=(block, block, jax.ShapeDtypeStruct...  1.49 us
    ppermute x1, waiting for transfers between devices, two_slices(): near = lax.ppermute(after(side_keep, first), 'tile', swap_tile)  1.31 us
    ppermute x1, waiting for transfers between devices, two_slices(): first = lax.ppermute(after(send, side_keep), ('probe', 'tile'), even_far)  1.26 us
  transfers between devices with their start and end apart: 10, of which 7 were waited for; matrix products, arithmetic and copies ran while one was open for 0% of the time, Pallas kernels for 10%

profile of v7, /device:TPU:0, one launch (start us, length us, event | category | flops | bytes accessed | tf_op | source)
XLA Modules:
  0.0 24.0 jit_solution(16898118866210642156)
XLA Ops:
  0.0 0.0 copy-start.1
  0.0 0.0 copy-start
  0.0 3.1 %collective-permute-start.3 = (bf16[2,256,256]{2,1,0:T(8,128)(2,1)}, bf16[2,256,256]{2,1,0:T(8,128)(2,1)S(1)}, u32[]{:S(2)}, u32[]{:S(2)}) collective-permute-start(bf16[2,256,256]{2,1,0:T(8,128)(2,1)} %bitcast.9), channel_id=1, source_target_pairs={{0,4},{4,0},{8,12},{12,8},{1,5},{5,1},{9,13},{13,9},{2,6},{6,2},{1... | collective-permute-start | bytes 786440 | tf_op jit(solution)/shard_map/ppermute | solution.py:194
  3.8 0.0 copy-done.1
  3.8 0.0 copy-done
  3.8 0.0 copy-start.2
  3.8 1.5 %adjoint.1 = (bf16[2,128,256]{2,1,0:T(8,128)(2,1)S(1)}, bf16[2,128,256]{2,1,0:T(8,128)(2,1)S(1)}, bf16[16,256]{1,0:T(8,128)(2,1)S(1)}) custom-call(f32[8,128]{1,0:T(8,128)S(1)} %early.1.early_ref, s32[1]{0:T(128)S(6)} %copy.8.slot_ref, s32[2,8]{1,0:T(2,128)} %bitcast.12, bf16[2,256,256]{2,1,0:T(8,128)(2,1)} %bitcast.11, f32[2,256,256]{2,1,0:T(8,128)S(1)} %copy-done.1, ...), custom_call_target="tpu_custom_call" | custom-call | tf_op jit(solution)/shard_map/adjoint/pallas_call | solution.py:173
  5.3 2.2 %collective-permute-start.1 = (bf16[2,128,256]{2,1,0:T(8,128)(2,1)S(1)}, bf16[2,128,256]{2,1,0:T(8,128)(2,1)S(1)}, u32[]{:S(2)}, u32[]{:S(2)}) collective-permute-start(bf16[2,128,256]{2,1,0:T(8,128)(2,1)S(1)} %get-tuple-element.16), channel_id=1, source_target_pairs={{0,2},{2,0},{4,6},{6,4},{8,10},{10,8},{12,14},{14,12},{1,3},{3,1},... | collective-permute-start | bytes 393224 | tf_op jit(solution)/shard_map/ppermute | solution.py:192
  7.5 0.0 collective-permute-start.2
  7.5 1.5 %collective-permute-start = (bf16[16,256]{1,0:T(8,128)(2,1)S(1)}, bf16[16,256]{1,0:T(8,128)(2,1)S(1)}, u32[]{:S(2)}, u32[]{:S(2)}) collective-permute-start(bf16[16,256]{1,0:T(8,128)(2,1)S(1)} %get-tuple-element.15.c0.in_ref), channel_id=1, source_target_pairs={{0,4},{4,0},{8,12},{12,8},{1,5},{5,1},{9,13},{13,9},{2,6},{6,2},{1... | collective-permute-start | bytes 24584 | tf_op jit(solution)/shard_map/ppermute | solution.py:195
  9.0 3.6 %collective-permute-done.c1 = bf16[16,256]{1,0:T(8,128)(2,1)S(1)} collective-permute-done((bf16[16,256]{1,0:T(8,128)(2,1)S(1)}, bf16[16,256]{1,0:T(8,128)(2,1)S(1)}, u32[]{:S(2)}, u32[]{:S(2)}) %collective-permute-start) | collective-permute-done | bytes 8224 | tf_op jit(solution)/shard_map/ppermute | solution.py:195
  12.6 0.0 collective-permute-done.3.w1
  12.7 0.0 copy-done.2
  12.7 0.4 %rolled_waves.1 = (bf16[2,128,256]{2,1,0:T(8,128)(2,1)S(1)}, bf16[2,128,256]{2,1,0:T(8,128)(2,1)S(1)}) custom-call(bf16[16,256]{1,0:T(8,128)(2,1)S(1)} %get-tuple-element.15.c0.in_ref, bf16[16,256]{1,0:T(8,128)(2,1)S(1)} %collective-permute-done.c1, bf16[2,256,256]{2,1,0:T(8,128)(2,1)S(1)} %bitcast.10, bf16[2,256,256]{2,1,0:T(8,128)(2,1)S(1)} %collective-permute-done.3.w1), custom_call_target="tpu_custom_call" | custom-call | tf_op jit(solution)/shard_map/rolled_waves/pallas_call | solution.py:196
  13.1 0.0 collective-permute-done.1.a0
  13.1 0.5 %collective-permute-done.2.a1 = bf16[2,128,256]{2,1,0:T(8,128)(2,1)S(1)} collective-permute-done((bf16[2,128,256]{2,1,0:T(8,128)(2,1)S(1)}, bf16[2,128,256]{2,1,0:T(8,128)(2,1)S(1)}, u32[]{:S(2)}, u32[]{:S(2)}) %collective-permute-start.2) | collective-permute-done | bytes 131104 | tf_op jit(solution)/shard_map/ppermute | solution.py:193
  13.6 0.2 far_sums.3
  13.8 0.1 collective-permute-start.4
  13.9 0.2 far_sums.2
  14.1 0.2 %near_sums.1 = (f32[2,128,256]{2,1,0:T(8,128)S(1)}, bf16[2,128,256]{2,1,0:T(8,128)(2,1)S(1)}) custom-call(bf16[16,256]{1,0:T(8,128)(2,1)S(1)} %get-tuple-element.15.c0.in_ref, bf16[16,256]{1,0:T(8,128)(2,1)S(1)} %collective-permute-done.c1, bf16[2,128,256]{2,1,0:T(8,128)(2,1)S(1)} %collective-permute-done.1.a0, ...), custom_call_target="tpu_custom_call" | custom-call | tf_op jit(solution)/shard_map/near_sums/pallas_call | solution.py:205
  14.4 0.9 %collective-permute-done.4 = bf16[2,128,256]{2,1,0:T(8,128)(2,1)S(1)} collective-permute-done((bf16[2,128,256]{2,1,0:T(8,128)(2,1)S(1)}, bf16[2,128,256]{2,1,0:T(8,128)(2,1)S(1)}, u32[]{:S(2)}, u32[]{:S(2)}) %collective-permute-start.4) | collective-permute-done | bytes 131104 | tf_op jit(solution)/shard_map/ppermute | solution.py:216
  15.3 2.7 %collective-permute-start.5 = (bf16[2,128,256]{2,1,0:T(8,128)(2,1)S(1)}, bf16[2,128,256]{2,1,0:T(8,128)(2,1)S(1)}, u32[]{:S(2)}, u32[]{:S(2)}) collective-permute-start(bf16[2,128,256]{2,1,0:T(8,128)(2,1)S(1)} %after.5), channel_id=1, source_target_pairs={{0,8},{1,9},{4,5},{5,4},{8,0},{9,1},{12,13},{13,12},{2,10},{3,11},... | collective-permute-start | bytes 393224 | tf_op jit(solution)/shard_map/ppermute | solution.py:234
  17.9 0.0 collective-permute-start.7
  17.9 1.2 %collective-permute-done.7.refs_0_ = bf16[16,256]{1,0:T(8,128)(2,1)S(1)} collective-permute-done((bf16[16,256]{1,0:T(8,128)(2,1)S(1)}, bf16[16,256]{1,0:T(8,128)(2,1)S(1)}, u32[]{:S(2)}, u32[]{:S(2)}) %collective-permute-start.7) | collective-permute-done | bytes 8224 | tf_op jit(solution)/shard_map/ppermute | solution.py:233
  19.1 0.2 collective-permute-start.8
  19.3 1.0 %collective-permute-done.8.refs_0_ = bf16[16,256]{1,0:T(8,128)(2,1)S(1)} collective-permute-done((bf16[16,256]{1,0:T(8,128)(2,1)S(1)}, bf16[16,256]{1,0:T(8,128)(2,1)S(1)}, u32[]{:S(2)}, u32[]{:S(2)}) %collective-permute-start.8) | collective-permute-done | bytes 8224 | tf_op jit(solution)/shard_map/ppermute | solution.py:235
  20.3 0.2 collective-permute-start.9
  20.5 1.3 %collective-permute-done.5.refs_0_ = bf16[2,128,256]{2,1,0:T(8,128)(2,1)S(1)} collective-permute-done((bf16[2,128,256]{2,1,0:T(8,128)(2,1)S(1)}, bf16[2,128,256]{2,1,0:T(8,128)(2,1)S(1)}, u32[]{:S(2)}, u32[]{:S(2)}) %collective-permute-start.5) | collective-permute-done | bytes 131104 | tf_op jit(solution)/shard_map/ppermute | solution.py:234
  21.8 0.1 collective-permute-start.6
  21.9 0.0 collective-permute-done.9
  21.9 1.3 %collective-permute-done.6 = bf16[2,128,256]{2,1,0:T(8,128)(2,1)S(1)} collective-permute-done((bf16[2,128,256]{2,1,0:T(8,128)(2,1)S(1)}, bf16[2,128,256]{2,1,0:T(8,128)(2,1)S(1)}, u32[]{:S(2)}, u32[]{:S(2)}) %collective-permute-start.6) | collective-permute-done | bytes 131104 | tf_op jit(solution)/shard_map/ppermute | solution.py:236
  23.2 0.8 %add_bitcast_fusion = f32[2,1,128,256]{3,2,1,0:T(8,128)} fusion(f32[2,128,256]{2,1,0:T(8,128)S(1)} %get-tuple-element.21, bf16[2,128,256]{2,1,0:T(8,128)(2,1)S(1)} %collective-permute-done.6, bf16[2,128,256]{2,1,0:T(8,128)(2,1)S(1)} %collective-permute-done.9, bf16[2,128,256]{2,1,0:T(8,128)(2,1)S(1)} %collective-permute-done.5.refs_0_, pred[]{:T(512)S(6)} %eq.5), kind=kLoop, calls=%fused_computation | loop fusion | flops 327680 | bytes 917505 | tf_op jit(solution)/shard_map/broadcast_in_dim | solution.py:239
  (7 shorter events, 0.1 us)
Async XLA Ops:
  0.0 3.8 %copy-start.1 = (f32[2,256,256]{2,1,0:T(8,128)S(1)}, f32[2,256,256]{2,1,0:T(8,128)}, u32[]{:S(2)}) copy-start(f32[2,256,256]{2,1,0:T(8,128)} %constant.21.clone.table_ref) | copy-start | bytes 1572868
  0.0 3.8 %copy-start = (f32[1,2,256,256]{3,2,1,0:T(8,128)S(1)}, f32[1,2,256,256]{3,2,1,0:T(8,128)}, u32[]{:S(2)}) copy-start(f32[1,2,256,256]{3,2,1,0:T(8,128)} %param.8) | copy-start | bytes 1572868
  0.0 12.6 %collective-permute-start.3 = (bf16[2,256,256]{2,1,0:T(8,128)(2,1)}, bf16[2,256,256]{2,1,0:T(8,128)(2,1)S(1)}, u32[]{:S(2)}, u32[]{:S(2)}) collective-permute-start(bf16[2,256,256]{2,1,0:T(8,128)(2,1)} %bitcast.9), channel_id=1, source_target_pairs={{0,4},{4,0},{8,12},{12,8},{1,5},{5,1},{9,13},{13,9},{2,6},{6,2},{1... | collective-permute-start | bytes 786440 | tf_op jit(solution)/shard_map/ppermute | solution.py:194
  3.8 8.9 %copy-start.2 = (bf16[1,1,2,256,256]{4,3,2,1,0:T(8,128)(2,1)S(1)}, bf16[1,1,2,256,256]{4,3,2,1,0:T(8,128)(2,1)}, u32[]{:S(2)}) copy-start(bf16[1,1,2,256,256]{4,3,2,1,0:T(8,128)(2,1)} %param.6) | copy-start | bytes 786436
  5.3 7.8 %collective-permute-start.1 = (bf16[2,128,256]{2,1,0:T(8,128)(2,1)S(1)}, bf16[2,128,256]{2,1,0:T(8,128)(2,1)S(1)}, u32[]{:S(2)}, u32[]{:S(2)}) collective-permute-start(bf16[2,128,256]{2,1,0:T(8,128)(2,1)S(1)} %get-tuple-element.16), channel_id=1, source_target_pairs={{0,2},{2,0},{4,6},{6,4},{8,10},{10,8},{12,14},{14,12},{1,3},{3,1},... | collective-permute-start | bytes 393224 | tf_op jit(solution)/shard_map/ppermute | solution.py:192
  7.5 6.1 %collective-permute-start.2 = (bf16[2,128,256]{2,1,0:T(8,128)(2,1)S(1)}, bf16[2,128,256]{2,1,0:T(8,128)(2,1)S(1)}, u32[]{:S(2)}, u32[]{:S(2)}) collective-permute-start(bf16[2,128,256]{2,1,0:T(8,128)(2,1)S(1)} %get-tuple-element.17), channel_id=1, source_target_pairs={{0,6},{2,4},{4,2},{6,0},{8,14},{10,12},{12,10},{14,8},{1,7},{3,5},... | collective-permute-start | bytes 393224 | tf_op jit(solution)/shard_map/ppermute | solution.py:193
  7.5 5.2 %collective-permute-start = (bf16[16,256]{1,0:T(8,128)(2,1)S(1)}, bf16[16,256]{1,0:T(8,128)(2,1)S(1)}, u32[]{:S(2)}, u32[]{:S(2)}) collective-permute-start(bf16[16,256]{1,0:T(8,128)(2,1)S(1)} %get-tuple-element.15.c0.in_ref), channel_id=1, source_target_pairs={{0,4},{4,0},{8,12},{12,8},{1,5},{5,1},{9,13},{13,9},{2,6},{6,2},{1... | collective-permute-start | bytes 24584 | tf_op jit(solution)/shard_map/ppermute | solution.py:195
  13.8 1.4 %collective-permute-start.4 = (bf16[2,128,256]{2,1,0:T(8,128)(2,1)S(1)}, bf16[2,128,256]{2,1,0:T(8,128)(2,1)S(1)}, u32[]{:S(2)}, u32[]{:S(2)}) collective-permute-start(bf16[2,128,256]{2,1,0:T(8,128)(2,1)S(1)} %far_sums.3), channel_id=1, source_target_pairs={{0,1},{1,0},{2,3},{3,2},{4,5},{5,4},{6,7},{7,6},{8,9},{9,8},{10,11... | collective-permute-start | bytes 393224 | tf_op jit(solution)/shard_map/ppermute | solution.py:216
  15.3 6.5 %collective-permute-start.5 = (bf16[2,128,256]{2,1,0:T(8,128)(2,1)S(1)}, bf16[2,128,256]{2,1,0:T(8,128)(2,1)S(1)}, u32[]{:S(2)}, u32[]{:S(2)}) collective-permute-start(bf16[2,128,256]{2,1,0:T(8,128)(2,1)S(1)} %after.5), channel_id=1, source_target_pairs={{0,8},{1,9},{4,5},{5,4},{8,0},{9,1},{12,13},{13,12},{2,10},{3,11},... | collective-permute-start | bytes 393224 | tf_op jit(solution)/shard_map/ppermute | solution.py:234
  17.9 1.2 %collective-permute-start.7 = (bf16[16,256]{1,0:T(8,128)(2,1)S(1)}, bf16[16,256]{1,0:T(8,128)(2,1)S(1)}, u32[]{:S(2)}, u32[]{:S(2)}) collective-permute-start(bf16[16,256]{1,0:T(8,128)(2,1)S(1)} %after.7), channel_id=1, source_target_pairs={{0,1},{1,0},{2,3},{3,2},{4,5},{5,4},{6,7},{7,6},{8,9},{9,8},{10,11... | collective-permute-start | bytes 24584 | tf_op jit(solution)/shard_map/ppermute | solution.py:233
  19.1 1.2 %collective-permute-start.8 = (bf16[16,256]{1,0:T(8,128)(2,1)S(1)}, bf16[16,256]{1,0:T(8,128)(2,1)S(1)}, u32[]{:S(2)}, u32[]{:S(2)}) collective-permute-start(bf16[16,256]{1,0:T(8,128)(2,1)S(1)} %after.8), channel_id=1, source_target_pairs={{0,1},{1,0},{2,3},{3,2},{4,5},{5,4},{6,7},{7,6},{8,9},{9,8},{10,11... | collective-permute-start | bytes 24584 | tf_op jit(solution)/shard_map/ppermute | solution.py:235
  20.3 1.6 %collective-permute-start.9 = (bf16[2,128,256]{2,1,0:T(8,128)(2,1)S(1)}, bf16[2,128,256]{2,1,0:T(8,128)(2,1)S(1)}, u32[]{:S(2)}, u32[]{:S(2)}) collective-permute-start(bf16[2,128,256]{2,1,0:T(8,128)(2,1)S(1)} %after.9), channel_id=1, source_target_pairs={{0,1},{1,0},{4,12},{5,13},{8,9},{9,8},{12,4},{13,5},{2,3},{3,2},{6... | collective-permute-start | bytes 393224 | tf_op jit(solution)/shard_map/ppermute | solution.py:237
  21.8 1.4 %collective-permute-start.6 = (bf16[2,128,256]{2,1,0:T(8,128)(2,1)S(1)}, bf16[2,128,256]{2,1,0:T(8,128)(2,1)S(1)}, u32[]{:S(2)}, u32[]{:S(2)}) collective-permute-start(bf16[2,128,256]{2,1,0:T(8,128)(2,1)S(1)} %after.6), channel_id=1, source_target_pairs={{0,1},{1,0},{2,3},{3,2},{4,5},{5,4},{6,7},{7,6},{8,9},{9,8},{10,11... | collective-permute-start | bytes 393224 | tf_op jit(solution)/shard_map/ppermute | solution.py:236

commit v8 on v7

--- a/solution.py
+++ b/solution.py
@@ -114,7 +114,7 @@
         rows = (along == ((down - cy) & (side - 1))).astype(jnp.bfloat16)
         cols = (every == ((across - cx) & (side - 1))).astype(jnp.bfloat16)
         moved = mm(rows, jnp.concatenate([w[0], w[1]], axis=1)).astype(jnp.bfloat16)
-        moved = mm(jnp.concatenate([moved[:, :side], moved[:, side:]], axis=0), cols).astype(jnp.bfloat16)
+        moved = mm(jnp.concatenate([moved[:, :side], moved[:, side:]], axis=0), cols)
         out[0] = moved[:half]
         out[1] = moved[half:]
 
@@ -195,7 +195,7 @@
     corner_next = lax.ppermute(corner, "probe", z1)
     w_own, w_next = pl.pallas_call(
         waves_kernel,
-        out_shape=(block, block),
+        out_shape=(sums, sums),
         in_specs=[vmem] * 4,
         out_specs=(vmem,) * 2,
         compiler_params=params,

time: 24.2 us -> 24.2 us (level)
  no operation moved by 1% of the time
where the time goes in v8:
time: 24.2 us; the launch traced here: 23.9 us
  starting transfers between devices  10 us (41%)
  waiting for transfers between devices  9.83 us (41%)
  Pallas kernels  2.51 us (10%)
  other arithmetic  0.78 us (3%)
  between operations  0.78 us (3%)
    ppermute x1, waiting for transfers between devices, two_slices(): corner_next = lax.ppermute(corner, 'probe', z1)  3.61 us
    ppermute x1, starting transfers between devices, two_slices(): w_next = lax.ppermute(waves, 'probe', z1)  3.09 us
    ppermute x1, starting transfers between devices, two_slices(): first = lax.ppermute(after(send, side_keep), ('probe', 'tile'), even_far)  2.65 us
    ppermute x1, starting transfers between devices, two_slices(): a_own = lax.ppermute(adj_own, ('probe', 'depth'), flip)  2.22 us
    ppermute x1, starting transfers between devices, two_slices(): corner_next = lax.ppermute(corner, 'probe', z1)  1.54 us
    pallas_call x1, Pallas kernels, two_slices(): pl.pallas_call(send_kernel, out_shape=(block, block, jax.ShapeDtypeStruct...  1.49 us
    ppermute x1, waiting for transfers between devices, two_slices(): near = lax.ppermute(after(side_keep, first), 'tile', swap_tile)  1.31 us
    ppermute x1, waiting for transfers between devices, two_slices(): first = lax.ppermute(after(send, side_keep), ('probe', 'tile'), even_far)  1.26 us
  transfers between devices with their start and end apart: 10, of which 7 were waited for; matrix products, arithmetic and copies ran while one was open for 0% of the time, Pallas kernels for 10%

profile of v8, /device:TPU:0, one launch (start us, length us, event | category | flops | bytes accessed | tf_op | source)
XLA Modules:
  0.0 23.9 jit_solution(2312439113158961345)
XLA Ops:
  0.0 0.0 copy-start.1
  0.0 0.0 copy-start
  0.0 3.1 %collective-permute-start.3 = (bf16[2,256,256]{2,1,0:T(8,128)(2,1)}, bf16[2,256,256]{2,1,0:T(8,128)(2,1)S(1)}, u32[]{:S(2)}, u32[]{:S(2)}) collective-permute-start(bf16[2,256,256]{2,1,0:T(8,128)(2,1)} %bitcast.9), channel_id=1, source_target_pairs={{0,4},{4,0},{8,12},{12,8},{1,5},{5,1},{9,13},{13,9},{2,6},{6,2},{1... | collective-permute-start | bytes 786440 | tf_op jit(solution)/shard_map/ppermute | solution.py:194
  3.8 0.0 copy-done.1
  3.8 0.0 copy-done
  3.8 0.0 copy-start.2
  3.8 1.5 %adjoint.1 = (bf16[2,128,256]{2,1,0:T(8,128)(2,1)S(1)}, bf16[2,128,256]{2,1,0:T(8,128)(2,1)S(1)}, bf16[16,256]{1,0:T(8,128)(2,1)S(1)}) custom-call(f32[8,128]{1,0:T(8,128)S(1)} %early.1.early_ref, s32[1]{0:T(128)S(6)} %copy.8.slot_ref, s32[2,8]{1,0:T(2,128)} %bitcast.12, bf16[2,256,256]{2,1,0:T(8,128)(2,1)} %bitcast.11, f32[2,256,256]{2,1,0:T(8,128)S(1)} %copy-done.1, ...), custom_call_target="tpu_custom_call" | custom-call | tf_op jit(solution)/shard_map/adjoint/pallas_call | solution.py:173
  5.3 2.2 %collective-permute-start.1 = (bf16[2,128,256]{2,1,0:T(8,128)(2,1)S(1)}, bf16[2,128,256]{2,1,0:T(8,128)(2,1)S(1)}, u32[]{:S(2)}, u32[]{:S(2)}) collective-permute-start(bf16[2,128,256]{2,1,0:T(8,128)(2,1)S(1)} %get-tuple-element.16), channel_id=1, source_target_pairs={{0,2},{2,0},{4,6},{6,4},{8,10},{10,8},{12,14},{14,12},{1,3},{3,1},... | collective-permute-start | bytes 393224 | tf_op jit(solution)/shard_map/ppermute | solution.py:192
  7.5 0.0 collective-permute-start.2
  7.5 1.5 %collective-permute-start = (bf16[16,256]{1,0:T(8,128)(2,1)S(1)}, bf16[16,256]{1,0:T(8,128)(2,1)S(1)}, u32[]{:S(2)}, u32[]{:S(2)}) collective-permute-start(bf16[16,256]{1,0:T(8,128)(2,1)S(1)} %get-tuple-element.15.c0.in_ref), channel_id=1, source_target_pairs={{0,4},{4,0},{8,12},{12,8},{1,5},{5,1},{9,13},{13,9},{2,6},{6,2},{1... | collective-permute-start | bytes 24584 | tf_op jit(solution)/shard_map/ppermute | solution.py:195
  9.0 3.6 %collective-permute-done.c1 = bf16[16,256]{1,0:T(8,128)(2,1)S(1)} collective-permute-done((bf16[16,256]{1,0:T(8,128)(2,1)S(1)}, bf16[16,256]{1,0:T(8,128)(2,1)S(1)}, u32[]{:S(2)}, u32[]{:S(2)}) %collective-permute-start) | collective-permute-done | bytes 8224 | tf_op jit(solution)/shard_map/ppermute | solution.py:195
  12.6 0.0 collective-permute-done.3.w1
  12.7 0.0 copy-done.2
  12.7 0.4 %rolled_waves.1 = (f32[2,128,256]{2,1,0:T(8,128)S(1)}, f32[2,128,256]{2,1,0:T(8,128)S(1)}) custom-call(bf16[16,256]{1,0:T(8,128)(2,1)S(1)} %get-tuple-element.15.c0.in_ref, bf16[16,256]{1,0:T(8,128)(2,1)S(1)} %collective-permute-done.c1, bf16[2,256,256]{2,1,0:T(8,128)(2,1)S(1)} %bitcast.10, bf16[2,256,256]{2,1,0:T(8,128)(2,1)S(1)} %collective-permute-done.3.w1), custom_call_target="tpu_custom_call" | custom-call | tf_op jit(solution)/shard_map/rolled_waves/pallas_call | solution.py:196
  13.1 0.0 collective-permute-done.1.a0
  13.1 0.5 %collective-permute-done.2.a1 = bf16[2,128,256]{2,1,0:T(8,128)(2,1)S(1)} collective-permute-done((bf16[2,128,256]{2,1,0:T(8,128)(2,1)S(1)}, bf16[2,128,256]{2,1,0:T(8,128)(2,1)S(1)}, u32[]{:S(2)}, u32[]{:S(2)}) %collective-permute-start.2) | collective-permute-done | bytes 131104 | tf_op jit(solution)/shard_map/ppermute | solution.py:193
  13.6 0.2 far_sums.3
  13.8 0.1 collective-permute-start.4
  13.9 0.2 far_sums.2
  14.0 0.2 near_sums.1
  14.3 0.9 %collective-permute-done.4 = bf16[2,128,256]{2,1,0:T(8,128)(2,1)S(1)} collective-permute-done((bf16[2,128,256]{2,1,0:T(8,128)(2,1)S(1)}, bf16[2,128,256]{2,1,0:T(8,128)(2,1)S(1)}, u32[]{:S(2)}, u32[]{:S(2)}) %collective-permute-start.4) | collective-permute-done | bytes 131104 | tf_op jit(solution)/shard_map/ppermute | solution.py:216
  15.2 2.7 %collective-permute-start.5 = (bf16[2,128,256]{2,1,0:T(8,128)(2,1)S(1)}, bf16[2,128,256]{2,1,0:T(8,128)(2,1)S(1)}, u32[]{:S(2)}, u32[]{:S(2)}) collective-permute-start(bf16[2,128,256]{2,1,0:T(8,128)(2,1)S(1)} %after.5), channel_id=1, source_target_pairs={{0,8},{1,9},{4,5},{5,4},{8,0},{9,1},{12,13},{13,12},{2,10},{3,11},... | collective-permute-start | bytes 393224 | tf_op jit(solution)/shard_map/ppermute | solution.py:234
  17.9 0.0 collective-permute-start.7
  17.9 1.2 %collective-permute-done.7.refs_0_ = bf16[16,256]{1,0:T(8,128)(2,1)S(1)} collective-permute-done((bf16[16,256]{1,0:T(8,128)(2,1)S(1)}, bf16[16,256]{1,0:T(8,128)(2,1)S(1)}, u32[]{:S(2)}, u32[]{:S(2)}) %collective-permute-start.7) | collective-permute-done | bytes 8224 | tf_op jit(solution)/shard_map/ppermute | solution.py:233
  19.1 0.2 collective-permute-start.8
  19.2 1.0 %collective-permute-done.8.refs_0_ = bf16[16,256]{1,0:T(8,128)(2,1)S(1)} collective-permute-done((bf16[16,256]{1,0:T(8,128)(2,1)S(1)}, bf16[16,256]{1,0:T(8,128)(2,1)S(1)}, u32[]{:S(2)}, u32[]{:S(2)}) %collective-permute-start.8) | collective-permute-done | bytes 8224 | tf_op jit(solution)/shard_map/ppermute | solution.py:235
  20.3 0.2 collective-permute-start.9
  20.5 1.3 %collective-permute-done.5.refs_0_ = bf16[2,128,256]{2,1,0:T(8,128)(2,1)S(1)} collective-permute-done((bf16[2,128,256]{2,1,0:T(8,128)(2,1)S(1)}, bf16[2,128,256]{2,1,0:T(8,128)(2,1)S(1)}, u32[]{:S(2)}, u32[]{:S(2)}) %collective-permute-start.5) | collective-permute-done | bytes 131104 | tf_op jit(solution)/shard_map/ppermute | solution.py:234
  21.8 0.1 collective-permute-start.6
  21.9 0.0 collective-permute-done.9
  21.9 1.3 %collective-permute-done.6 = bf16[2,128,256]{2,1,0:T(8,128)(2,1)S(1)} collective-permute-done((bf16[2,128,256]{2,1,0:T(8,128)(2,1)S(1)}, bf16[2,128,256]{2,1,0:T(8,128)(2,1)S(1)}, u32[]{:S(2)}, u32[]{:S(2)}) %collective-permute-start.6) | collective-permute-done | bytes 131104 | tf_op jit(solution)/shard_map/ppermute | solution.py:236
  23.2 0.8 %add_bitcast_fusion = f32[2,1,128,256]{3,2,1,0:T(8,128)} fusion(f32[2,128,256]{2,1,0:T(8,128)S(1)} %get-tuple-element.21, bf16[2,128,256]{2,1,0:T(8,128)(2,1)S(1)} %collective-permute-done.6, bf16[2,128,256]{2,1,0:T(8,128)(2,1)S(1)} %collective-permute-done.9, bf16[2,128,256]{2,1,0:T(8,128)(2,1)S(1)} %collective-permute-done.5.refs_0_, pred[]{:T(512)S(6)} %eq.5), kind=kLoop, calls=%fused_computation | loop fusion | flops 327680 | bytes 917505 | tf_op jit(solution)/shard_map/broadcast_in_dim | solution.py:239
  (7 shorter events, 0.1 us)
Async XLA Ops:
  0.0 3.8 %copy-start.1 = (f32[2,256,256]{2,1,0:T(8,128)S(1)}, f32[2,256,256]{2,1,0:T(8,128)}, u32[]{:S(2)}) copy-start(f32[2,256,256]{2,1,0:T(8,128)} %constant.21.clone.table_ref) | copy-start | bytes 1572868
  0.0 3.8 %copy-start = (f32[1,2,256,256]{3,2,1,0:T(8,128)S(1)}, f32[1,2,256,256]{3,2,1,0:T(8,128)}, u32[]{:S(2)}) copy-start(f32[1,2,256,256]{3,2,1,0:T(8,128)} %param.8) | copy-start | bytes 1572868
  0.0 12.6 %collective-permute-start.3 = (bf16[2,256,256]{2,1,0:T(8,128)(2,1)}, bf16[2,256,256]{2,1,0:T(8,128)(2,1)S(1)}, u32[]{:S(2)}, u32[]{:S(2)}) collective-permute-start(bf16[2,256,256]{2,1,0:T(8,128)(2,1)} %bitcast.9), channel_id=1, source_target_pairs={{0,4},{4,0},{8,12},{12,8},{1,5},{5,1},{9,13},{13,9},{2,6},{6,2},{1... | collective-permute-start | bytes 786440 | tf_op jit(solution)/shard_map/ppermute | solution.py:194
  3.8 8.9 %copy-start.2 = (bf16[1,1,2,256,256]{4,3,2,1,0:T(8,128)(2,1)S(1)}, bf16[1,1,2,256,256]{4,3,2,1,0:T(8,128)(2,1)}, u32[]{:S(2)}) copy-start(bf16[1,1,2,256,256]{4,3,2,1,0:T(8,128)(2,1)} %param.6) | copy-start | bytes 786436
  5.3 7.8 %collective-permute-start.1 = (bf16[2,128,256]{2,1,0:T(8,128)(2,1)S(1)}, bf16[2,128,256]{2,1,0:T(8,128)(2,1)S(1)}, u32[]{:S(2)}, u32[]{:S(2)}) collective-permute-start(bf16[2,128,256]{2,1,0:T(8,128)(2,1)S(1)} %get-tuple-element.16), channel_id=1, source_target_pairs={{0,2},{2,0},{4,6},{6,4},{8,10},{10,8},{12,14},{14,12},{1,3},{3,1},... | collective-permute-start | bytes 393224 | tf_op jit(solution)/shard_map/ppermute | solution.py:192
  7.5 6.1 %collective-permute-start.2 = (bf16[2,128,256]{2,1,0:T(8,128)(2,1)S(1)}, bf16[2,128,256]{2,1,0:T(8,128)(2,1)S(1)}, u32[]{:S(2)}, u32[]{:S(2)}) collective-permute-start(bf16[2,128,256]{2,1,0:T(8,128)(2,1)S(1)} %get-tuple-element.17), channel_id=1, source_target_pairs={{0,6},{2,4},{4,2},{6,0},{8,14},{10,12},{12,10},{14,8},{1,7},{3,5},... | collective-permute-start | bytes 393224 | tf_op jit(solution)/shard_map/ppermute | solution.py:193
  7.5 5.2 %collective-permute-start = (bf16[16,256]{1,0:T(8,128)(2,1)S(1)}, bf16[16,256]{1,0:T(8,128)(2,1)S(1)}, u32[]{:S(2)}, u32[]{:S(2)}) collective-permute-start(bf16[16,256]{1,0:T(8,128)(2,1)S(1)} %get-tuple-element.15.c0.in_ref), channel_id=1, source_target_pairs={{0,4},{4,0},{8,12},{12,8},{1,5},{5,1},{9,13},{13,9},{2,6},{6,2},{1... | collective-permute-start | bytes 24584 | tf_op jit(solution)/shard_map/ppermute | solution.py:195
  13.8 1.4 %collective-permute-start.4 = (bf16[2,128,256]{2,1,0:T(8,128)(2,1)S(1)}, bf16[2,128,256]{2,1,0:T(8,128)(2,1)S(1)}, u32[]{:S(2)}, u32[]{:S(2)}) collective-permute-start(bf16[2,128,256]{2,1,0:T(8,128)(2,1)S(1)} %far_sums.3), channel_id=1, source_target_pairs={{0,1},{1,0},{2,3},{3,2},{4,5},{5,4},{6,7},{7,6},{8,9},{9,8},{10,11... | collective-permute-start | bytes 393224 | tf_op jit(solution)/shard_map/ppermute | solution.py:216
  15.2 6.5 %collective-permute-start.5 = (bf16[2,128,256]{2,1,0:T(8,128)(2,1)S(1)}, bf16[2,128,256]{2,1,0:T(8,128)(2,1)S(1)}, u32[]{:S(2)}, u32[]{:S(2)}) collective-permute-start(bf16[2,128,256]{2,1,0:T(8,128)(2,1)S(1)} %after.5), channel_id=1, source_target_pairs={{0,8},{1,9},{4,5},{5,4},{8,0},{9,1},{12,13},{13,12},{2,10},{3,11},... | collective-permute-start | bytes 393224 | tf_op jit(solution)/shard_map/ppermute | solution.py:234
  17.9 1.2 %collective-permute-start.7 = (bf16[16,256]{1,0:T(8,128)(2,1)S(1)}, bf16[16,256]{1,0:T(8,128)(2,1)S(1)}, u32[]{:S(2)}, u32[]{:S(2)}) collective-permute-start(bf16[16,256]{1,0:T(8,128)(2,1)S(1)} %after.7), channel_id=1, source_target_pairs={{0,1},{1,0},{2,3},{3,2},{4,5},{5,4},{6,7},{7,6},{8,9},{9,8},{10,11... | collective-permute-start | bytes 24584 | tf_op jit(solution)/shard_map/ppermute | solution.py:233
  19.1 1.2 %collective-permute-start.8 = (bf16[16,256]{1,0:T(8,128)(2,1)S(1)}, bf16[16,256]{1,0:T(8,128)(2,1)S(1)}, u32[]{:S(2)}, u32[]{:S(2)}) collective-permute-start(bf16[16,256]{1,0:T(8,128)(2,1)S(1)} %after.8), channel_id=1, source_target_pairs={{0,1},{1,0},{2,3},{3,2},{4,5},{5,4},{6,7},{7,6},{8,9},{9,8},{10,11... | collective-permute-start | bytes 24584 | tf_op jit(solution)/shard_map/ppermute | solution.py:235
  20.3 1.6 %collective-permute-start.9 = (bf16[2,128,256]{2,1,0:T(8,128)(2,1)S(1)}, bf16[2,128,256]{2,1,0:T(8,128)(2,1)S(1)}, u32[]{:S(2)}, u32[]{:S(2)}) collective-permute-start(bf16[2,128,256]{2,1,0:T(8,128)(2,1)S(1)} %after.9), channel_id=1, source_target_pairs={{0,1},{1,0},{4,12},{5,13},{8,9},{9,8},{12,4},{13,5},{2,3},{3,2},{6... | collective-permute-start | bytes 393224 | tf_op jit(solution)/shard_map/ppermute | solution.py:237
  21.8 1.4 %collective-permute-start.6 = (bf16[2,128,256]{2,1,0:T(8,128)(2,1)S(1)}, bf16[2,128,256]{2,1,0:T(8,128)(2,1)S(1)}, u32[]{:S(2)}, u32[]{:S(2)}) collective-permute-start(bf16[2,128,256]{2,1,0:T(8,128)(2,1)S(1)} %after.6), channel_id=1, source_target_pairs={{0,1},{1,0},{2,3},{3,2},{4,5},{5,4},{6,7},{7,6},{8,9},{9,8},{10,11... | collective-permute-start | bytes 393224 | tf_op jit(solution)/shard_map/ppermute | solution.py:236

commit v9 on v8

--- a/solution.py
+++ b/solution.py
@@ -139,6 +139,11 @@
     for ref, result in zip(refs, (here, side_sums)[wanted]):
         for part in range(2):
             ref[part] = result[part].astype(ref.dtype)
+
+
+def add_kernel(here_ref, side_ref, later_ref, out_ref):
+    del later_ref
+    out_ref[...] = (here_ref[...] + side_ref[...].astype(jnp.float32)).astype(jnp.bfloat16)
 
 
 def copy_kernel(in_ref, *refs):
@@ -213,7 +218,14 @@
 
     (side_send,), (send,) = masked_sums(False, slice(1, 2), block), masked_sums(False, slice(0, 1), sums)
     keep, side_keep = masked_sums(True, slice(0, 2), sums, block)
-    send = (send + lax.ppermute(side_send, "tile", swap_tile).astype(jnp.float32)).astype(jnp.bfloat16)
+    send = pl.pallas_call(
+        add_kernel,
+        out_shape=block,
+        in_specs=[vmem] * 3,
+        out_specs=vmem,
+        compiler_params=params,
+        name="far_total",
+    )(send, lax.ppermute(side_send, "tile", swap_tile), side_keep)
 
     def after(x, *earlier):
         return pl.pallas_call(
@@ -231,7 +243,7 @@
         for turn in range(2)
     )
     once = lax.ppermute(after(corner, send), "tile", swap_tile)
-    first = lax.ppermute(after(send, side_keep), ("probe", "tile"), even_far)
+    first = lax.ppermute(send, ("probe", "tile"), even_far)
     twice = lax.ppermute(after(corner, once), "tile", swap_tile)
     near = lax.ppermute(after(side_keep, first), "tile", swap_tile)
     third = lax.ppermute(after(send, twice), ("probe", "tile"), odd_far)

time: 24.2 us -> 24.2 us (level)
  no operation moved by 1% of the time
where the time goes in v9:
time: 24.2 us; the launch traced here: 23.9 us
  starting transfers between devices  10 us (41%)
  waiting for transfers between devices  9.83 us (41%)
  Pallas kernels  2.52 us (10%)
  between operations  0.77 us (3%)
  other arithmetic  0.76 us (3%)
    ppermute x1, waiting for transfers between devices, two_slices(): corner_next = lax.ppermute(corner, 'probe', z1)  3.61 us
    ppermute x1, starting transfers between devices, two_slices(): w_next = lax.ppermute(waves, 'probe', z1)  3.09 us
    ppermute x1, starting transfers between devices, two_slices(): first = lax.ppermute(send, ('probe', 'tile'), even_far)  2.65 us
    ppermute x1, starting transfers between devices, two_slices(): a_own = lax.ppermute(adj_own, ('probe', 'depth'), flip)  2.22 us
    ppermute x1, starting transfers between devices, two_slices(): corner_next = lax.ppermute(corner, 'probe', z1)  1.54 us
    pallas_call x1, Pallas kernels, two_slices(): pl.pallas_call(send_kernel, out_shape=(block, block, jax.ShapeDtypeStruct...  1.49 us
    ppermute x1, waiting for transfers between devices, two_slices(): near = lax.ppermute(after(side_keep, first), 'tile', swap_tile)  1.31 us
    ppermute x1, waiting for transfers between devices, two_slices(): first = lax.ppermute(send, ('probe', 'tile'), even_far)  1.26 us
  transfers between devices with their start and end apart: 10, of which 7 were waited for; matrix products, arithmetic and copies ran while one was open for 0% of the time, Pallas kernels for 10%

profile of v9, /device:TPU:0, one launch (start us, length us, event | category | flops | bytes accessed | tf_op | source)
XLA Modules:
  0.0 23.9 jit_solution(7801274125855350859)
XLA Ops:
  0.0 0.0 copy-start.1
  0.0 0.0 copy-start
  0.0 3.1 %collective-permute-start.3 = (bf16[2,256,256]{2,1,0:T(8,128)(2,1)}, bf16[2,256,256]{2,1,0:T(8,128)(2,1)S(1)}, u32[]{:S(2)}, u32[]{:S(2)}) collective-permute-start(bf16[2,256,256]{2,1,0:T(8,128)(2,1)} %bitcast.9), channel_id=1, source_target_pairs={{0,4},{4,0},{8,12},{12,8},{1,5},{5,1},{9,13},{13,9},{2,6},{6,2},{1... | collective-permute-start | bytes 786440 | tf_op jit(solution)/shard_map/ppermute | solution.py:199
  3.8 0.0 copy-done.1
  3.8 0.0 copy-done
  3.8 0.0 copy-start.2
  3.8 1.5 %adjoint.1 = (bf16[2,128,256]{2,1,0:T(8,128)(2,1)S(1)}, bf16[2,128,256]{2,1,0:T(8,128)(2,1)S(1)}, bf16[16,256]{1,0:T(8,128)(2,1)S(1)}) custom-call(f32[8,128]{1,0:T(8,128)S(1)} %early.1.early_ref, s32[1]{0:T(128)S(6)} %copy.8.slot_ref, s32[2,8]{1,0:T(2,128)} %bitcast.12, bf16[2,256,256]{2,1,0:T(8,128)(2,1)} %bitcast.11, f32[2,256,256]{2,1,0:T(8,128)S(1)} %copy-done.1, ...), custom_call_target="tpu_custom_call" | custom-call | tf_op jit(solution)/shard_map/adjoint/pallas_call | solution.py:178
  5.3 2.2 %collective-permute-start.1 = (bf16[2,128,256]{2,1,0:T(8,128)(2,1)S(1)}, bf16[2,128,256]{2,1,0:T(8,128)(2,1)S(1)}, u32[]{:S(2)}, u32[]{:S(2)}) collective-permute-start(bf16[2,128,256]{2,1,0:T(8,128)(2,1)S(1)} %get-tuple-element.16), channel_id=1, source_target_pairs={{0,2},{2,0},{4,6},{6,4},{8,10},{10,8},{12,14},{14,12},{1,3},{3,1},... | collective-permute-start | bytes 393224 | tf_op jit(solution)/shard_map/ppermute | solution.py:197
  7.5 0.0 collective-permute-start.2
  7.5 1.5 %collective-permute-start = (bf16[16,256]{1,0:T(8,128)(2,1)S(1)}, bf16[16,256]{1,0:T(8,128)(2,1)S(1)}, u32[]{:S(2)}, u32[]{:S(2)}) collective-permute-start(bf16[16,256]{1,0:T(8,128)(2,1)S(1)} %get-tuple-element.15.c0.in_ref), channel_id=1, source_target_pairs={{0,4},{4,0},{8,12},{12,8},{1,5},{5,1},{9,13},{13,9},{2,6},{6,2},{1... | collective-permute-start | bytes 24584 | tf_op jit(solution)/shard_map/ppermute | solution.py:200
  9.0 3.6 %collective-permute-done.c1 = bf16[16,256]{1,0:T(8,128)(2,1)S(1)} collective-permute-done((bf16[16,256]{1,0:T(8,128)(2,1)S(1)}, bf16[16,256]{1,0:T(8,128)(2,1)S(1)}, u32[]{:S(2)}, u32[]{:S(2)}) %collective-permute-start) | collective-permute-done | bytes 8224 | tf_op jit(solution)/shard_map/ppermute | solution.py:200
  12.6 0.0 collective-permute-done.3.w1
  12.7 0.0 copy-done.2
  12.7 0.4 %rolled_waves.1 = (f32[2,128,256]{2,1,0:T(8,128)S(1)}, f32[2,128,256]{2,1,0:T(8,128)S(1)}) custom-call(bf16[16,256]{1,0:T(8,128)(2,1)S(1)} %get-tuple-element.15.c0.in_ref, bf16[16,256]{1,0:T(8,128)(2,1)S(1)} %collective-permute-done.c1, bf16[2,256,256]{2,1,0:T(8,128)(2,1)S(1)} %bitcast.10, bf16[2,256,256]{2,1,0:T(8,128)(2,1)S(1)} %collective-permute-done.3.w1), custom_call_target="tpu_custom_call" | custom-call | tf_op jit(solution)/shard_map/rolled_waves/pallas_call | solution.py:201
  13.1 0.0 collective-permute-done.1.a0
  13.1 0.5 %collective-permute-done.2.a1 = bf16[2,128,256]{2,1,0:T(8,128)(2,1)S(1)} collective-permute-done((bf16[2,128,256]{2,1,0:T(8,128)(2,1)S(1)}, bf16[2,128,256]{2,1,0:T(8,128)(2,1)S(1)}, u32[]{:S(2)}, u32[]{:S(2)}) %collective-permute-start.2) | collective-permute-done | bytes 131104 | tf_op jit(solution)/shard_map/ppermute | solution.py:198
  13.6 0.2 far_sums.3
  13.8 0.1 collective-permute-start.4
  13.9 0.2 near_sums.1
  14.1 0.2 far_sums.2.here_ref
  14.3 0.9 %collective-permute-done.4.side_ref = bf16[2,128,256]{2,1,0:T(8,128)(2,1)S(1)} collective-permute-done((bf16[2,128,256]{2,1,0:T(8,128)(2,1)S(1)}, bf16[2,128,256]{2,1,0:T(8,128)(2,1)S(1)}, u32[]{:S(2)}, u32[]{:S(2)}) %collective-permute-start.4) | collective-permute-done | bytes 131104 | tf_op jit(solution)/shard_map/ppermute | solution.py:228
  15.2 2.7 %collective-permute-start.5 = (bf16[2,128,256]{2,1,0:T(8,128)(2,1)S(1)}, bf16[2,128,256]{2,1,0:T(8,128)(2,1)S(1)}, u32[]{:S(2)}, u32[]{:S(2)}) collective-permute-start(bf16[2,128,256]{2,1,0:T(8,128)(2,1)S(1)} %far_total.1.refs_0_.in_ref), channel_id=1, source_target_pairs={{0,8},{1,9},{4,5},{5,4},{8,0},{9,1},{12,13},{13,12},{2,10},{3,11},... | collective-permute-start | bytes 393224 | tf_op jit(solution)/shard_map/ppermute | solution.py:246
  17.9 0.0 collective-permute-start.7
  17.9 1.2 %collective-permute-done.7.refs_0_ = bf16[16,256]{1,0:T(8,128)(2,1)S(1)} collective-permute-done((bf16[16,256]{1,0:T(8,128)(2,1)S(1)}, bf16[16,256]{1,0:T(8,128)(2,1)S(1)}, u32[]{:S(2)}, u32[]{:S(2)}) %collective-permute-start.7) | collective-permute-done | bytes 8224 | tf_op jit(solution)/shard_map/ppermute | solution.py:245
  19.1 0.2 collective-permute-start.8
  19.2 1.0 %collective-permute-done.8.refs_0_ = bf16[16,256]{1,0:T(8,128)(2,1)S(1)} collective-permute-done((bf16[16,256]{1,0:T(8,128)(2,1)S(1)}, bf16[16,256]{1,0:T(8,128)(2,1)S(1)}, u32[]{:S(2)}, u32[]{:S(2)}) %collective-permute-start.8) | collective-permute-done | bytes 8224 | tf_op jit(solution)/shard_map/ppermute | solution.py:247
  20.2 0.2 collective-permute-start.9
  20.5 1.3 %collective-permute-done.5.refs_0_ = bf16[2,128,256]{2,1,0:T(8,128)(2,1)S(1)} collective-permute-done((bf16[2,128,256]{2,1,0:T(8,128)(2,1)S(1)}, bf16[2,128,256]{2,1,0:T(8,128)(2,1)S(1)}, u32[]{:S(2)}, u32[]{:S(2)}) %collective-permute-start.5) | collective-permute-done | bytes 131104 | tf_op jit(solution)/shard_map/ppermute | solution.py:246
  21.8 0.1 collective-permute-start.6
  21.8 0.0 collective-permute-done.9
  21.9 1.3 %collective-permute-done.6 = bf16[2,128,256]{2,1,0:T(8,128)(2,1)S(1)} collective-permute-done((bf16[2,128,256]{2,1,0:T(8,128)(2,1)S(1)}, bf16[2,128,256]{2,1,0:T(8,128)(2,1)S(1)}, u32[]{:S(2)}, u32[]{:S(2)}) %collective-permute-start.6) | collective-permute-done | bytes 131104 | tf_op jit(solution)/shard_map/ppermute | solution.py:248
  23.2 0.8 %add_bitcast_fusion = f32[2,1,128,256]{3,2,1,0:T(8,128)} fusion(f32[2,128,256]{2,1,0:T(8,128)S(1)} %get-tuple-element.21, bf16[2,128,256]{2,1,0:T(8,128)(2,1)S(1)} %collective-permute-done.6, bf16[2,128,256]{2,1,0:T(8,128)(2,1)S(1)} %collective-permute-done.9, bf16[2,128,256]{2,1,0:T(8,128)(2,1)S(1)} %collective-permute-done.5.refs_0_, pred[]{:T(512)S(6)} %eq.5), kind=kLoop, calls=%fused_computation | loop fusion | flops 327680 | bytes 917505 | tf_op jit(solution)/shard_map/broadcast_in_dim | solution.py:251
  (6 shorter events, 0.0 us)
Async XLA Ops:
  0.0 3.8 %copy-start.1 = (f32[2,256,256]{2,1,0:T(8,128)S(1)}, f32[2,256,256]{2,1,0:T(8,128)}, u32[]{:S(2)}) copy-start(f32[2,256,256]{2,1,0:T(8,128)} %constant.21.clone.table_ref) | copy-start | bytes 1572868
  0.0 3.8 %copy-start = (f32[1,2,256,256]{3,2,1,0:T(8,128)S(1)}, f32[1,2,256,256]{3,2,1,0:T(8,128)}, u32[]{:S(2)}) copy-start(f32[1,2,256,256]{3,2,1,0:T(8,128)} %param.8) | copy-start | bytes 1572868
  0.0 12.6 %collective-permute-start.3 = (bf16[2,256,256]{2,1,0:T(8,128)(2,1)}, bf16[2,256,256]{2,1,0:T(8,128)(2,1)S(1)}, u32[]{:S(2)}, u32[]{:S(2)}) collective-permute-start(bf16[2,256,256]{2,1,0:T(8,128)(2,1)} %bitcast.9), channel_id=1, source_target_pairs={{0,4},{4,0},{8,12},{12,8},{1,5},{5,1},{9,13},{13,9},{2,6},{6,2},{1... | collective-permute-start | bytes 786440 | tf_op jit(solution)/shard_map/ppermute | solution.py:199
  3.8 8.9 %copy-start.2 = (bf16[1,1,2,256,256]{4,3,2,1,0:T(8,128)(2,1)S(1)}, bf16[1,1,2,256,256]{4,3,2,1,0:T(8,128)(2,1)}, u32[]{:S(2)}) copy-start(bf16[1,1,2,256,256]{4,3,2,1,0:T(8,128)(2,1)} %param.6) | copy-start | bytes 786436
  5.3 7.8 %collective-permute-start.1 = (bf16[2,128,256]{2,1,0:T(8,128)(2,1)S(1)}, bf16[2,128,256]{2,1,0:T(8,128)(2,1)S(1)}, u32[]{:S(2)}, u32[]{:S(2)}) collective-permute-start(bf16[2,128,256]{2,1,0:T(8,128)(2,1)S(1)} %get-tuple-element.16), channel_id=1, source_target_pairs={{0,2},{2,0},{4,6},{6,4},{8,10},{10,8},{12,14},{14,12},{1,3},{3,1},... | collective-permute-start | bytes 393224 | tf_op jit(solution)/shard_map/ppermute | solution.py:197
  7.5 6.1 %collective-permute-start.2 = (bf16[2,128,256]{2,1,0:T(8,128)(2,1)S(1)}, bf16[2,128,256]{2,1,0:T(8,128)(2,1)S(1)}, u32[]{:S(2)}, u32[]{:S(2)}) collective-permute-start(bf16[2,128,256]{2,1,0:T(8,128)(2,1)S(1)} %get-tuple-element.17), channel_id=1, source_target_pairs={{0,6},{2,4},{4,2},{6,0},{8,14},{10,12},{12,10},{14,8},{1,7},{3,5},... | collective-permute-start | bytes 393224 | tf_op jit(solution)/shard_map/ppermute | solution.py:198
  7.5 5.2 %collective-permute-start = (bf16[16,256]{1,0:T(8,128)(2,1)S(1)}, bf16[16,256]{1,0:T(8,128)(2,1)S(1)}, u32[]{:S(2)}, u32[]{:S(2)}) collective-permute-start(bf16[16,256]{1,0:T(8,128)(2,1)S(1)} %get-tuple-element.15.c0.in_ref), channel_id=1, source_target_pairs={{0,4},{4,0},{8,12},{12,8},{1,5},{5,1},{9,13},{13,9},{2,6},{6,2},{1... | collective-permute-start | bytes 24584 | tf_op jit(solution)/shard_map/ppermute | solution.py:200
  13.8 1.4 %collective-permute-start.4 = (bf16[2,128,256]{2,1,0:T(8,128)(2,1)S(1)}, bf16[2,128,256]{2,1,0:T(8,128)(2,1)S(1)}, u32[]{:S(2)}, u32[]{:S(2)}) collective-permute-start(bf16[2,128,256]{2,1,0:T(8,128)(2,1)S(1)} %far_sums.3), channel_id=1, source_target_pairs={{0,1},{1,0},{2,3},{3,2},{4,5},{5,4},{6,7},{7,6},{8,9},{9,8},{10,11... | collective-permute-start | bytes 393224 | tf_op jit(solution)/shard_map/ppermute | solution.py:228
  15.2 6.5 %collective-permute-start.5 = (bf16[2,128,256]{2,1,0:T(8,128)(2,1)S(1)}, bf16[2,128,256]{2,1,0:T(8,128)(2,1)S(1)}, u32[]{:S(2)}, u32[]{:S(2)}) collective-permute-start(bf16[2,128,256]{2,1,0:T(8,128)(2,1)S(1)} %far_total.1.refs_0_.in_ref), channel_id=1, source_target_pairs={{0,8},{1,9},{4,5},{5,4},{8,0},{9,1},{12,13},{13,12},{2,10},{3,11},... | collective-permute-start | bytes 393224 | tf_op jit(solution)/shard_map/ppermute | solution.py:246
  17.9 1.2 %collective-permute-start.7 = (bf16[16,256]{1,0:T(8,128)(2,1)S(1)}, bf16[16,256]{1,0:T(8,128)(2,1)S(1)}, u32[]{:S(2)}, u32[]{:S(2)}) collective-permute-start(bf16[16,256]{1,0:T(8,128)(2,1)S(1)} %after.5), channel_id=1, source_target_pairs={{0,1},{1,0},{2,3},{3,2},{4,5},{5,4},{6,7},{7,6},{8,9},{9,8},{10,11... | collective-permute-start | bytes 24584 | tf_op jit(solution)/shard_map/ppermute | solution.py:245
  19.1 1.2 %collective-permute-start.8 = (bf16[16,256]{1,0:T(8,128)(2,1)S(1)}, bf16[16,256]{1,0:T(8,128)(2,1)S(1)}, u32[]{:S(2)}, u32[]{:S(2)}) collective-permute-start(bf16[16,256]{1,0:T(8,128)(2,1)S(1)} %after.6), channel_id=1, source_target_pairs={{0,1},{1,0},{2,3},{3,2},{4,5},{5,4},{6,7},{7,6},{8,9},{9,8},{10,11... | collective-permute-start | bytes 24584 | tf_op jit(solution)/shard_map/ppermute | solution.py:247
  20.2 1.6 %collective-permute-start.9 = (bf16[2,128,256]{2,1,0:T(8,128)(2,1)S(1)}, bf16[2,128,256]{2,1,0:T(8,128)(2,1)S(1)}, u32[]{:S(2)}, u32[]{:S(2)}) collective-permute-start(bf16[2,128,256]{2,1,0:T(8,128)(2,1)S(1)} %after.7), channel_id=1, source_target_pairs={{0,1},{1,0},{4,12},{5,13},{8,9},{9,8},{12,4},{13,5},{2,3},{3,2},{6... | collective-permute-start | bytes 393224 | tf_op jit(solution)/shard_map/ppermute | solution.py:249
  21.8 1.4 %collective-permute-start.6 = (bf16[2,128,256]{2,1,0:T(8,128)(2,1)S(1)}, bf16[2,128,256]{2,1,0:T(8,128)(2,1)S(1)}, u32[]{:S(2)}, u32[]{:S(2)}) collective-permute-start(bf16[2,128,256]{2,1,0:T(8,128)(2,1)S(1)} %after.4), channel_id=1, source_target_pairs={{0,1},{1,0},{2,3},{3,2},{4,5},{5,4},{6,7},{7,6},{8,9},{9,8},{10,11... | collective-permute-start | bytes 393224 | tf_op jit(solution)/shard_map/ppermute | solution.py:248

commit v10 on v9

--- a/solution.py
+++ b/solution.py
@@ -58,9 +58,10 @@
     half = side // 2
     del early_ref
     offsets_copy = pltpu.make_async_copy(offsets_hbm, offsets_ref, sems.at[0])
-    layer_copy = pltpu.make_async_copy(layer_hbm, layer_ref, sems.at[1])
+    layer_copies = [pltpu.make_async_copy(layer_hbm.at[n], layer_ref.at[n], sems.at[1 + n]) for n in range(2)]
     offsets_copy.start()
-    layer_copy.start()
+    for copy in layer_copies:
+        copy.start()
     offsets_copy.wait()
     slot = slot_ref[0]
     cy, cx = offsets_ref[0, slot], offsets_ref[1, slot]
@@ -76,7 +77,8 @@
 
     @pl.when(top)
     def _():
-        layer_copy.wait()
+        for copy in layer_copies:
+            copy.wait()
         layer = layer_ref[0].astype(jnp.float32), layer_ref[1].astype(jnp.float32)
         handed = conj_times(layer, (residual_ref[0], residual_ref[1]))
         vr, vi = (x.astype(jnp.bfloat16) for x in handed)
@@ -94,7 +96,8 @@
 
     @pl.when(jnp.logical_not(top))
     def _():
-        layer_copy.wait()
+        for copy in layer_copies:
+            copy.wait()
         rows, cols = rolls(side, down, cx)
         for part, x in enumerate(rolled([residual_ref[n].astype(jnp.bfloat16) for n in range(2)], rows, cols)):
             put(part, x)
@@ -183,7 +186,7 @@
         scratch_shapes=[
             pltpu.SMEM(by_column.shape, jnp.int32),
             pltpu.VMEM((2, side, side), jnp.bfloat16),
-            pltpu.SemaphoreType.DMA((2,)),
+            pltpu.SemaphoreType.DMA((3,)),
         ],
         compiler_params=params,
         name="adjoint",

time: 24.2 us -> 24.2 us (level)
  no operation moved by 1% of the time
where the time goes in v10:
time: 24.2 us; the launch traced here: 23.9 us
  starting transfers between devices  10 us (41%)
  waiting for transfers between devices  9.8 us (40%)
  Pallas kernels  2.55 us (11%)
  between operations  0.77 us (3%)
  other arithmetic  0.76 us (3%)
    ppermute x1, waiting for transfers between devices, two_slices(): corner_next = lax.ppermute(corner, 'probe', z1)  3.59 us
    ppermute x1, starting transfers between devices, two_slices(): w_next = lax.ppermute(waves, 'probe', z1)  3.09 us
    ppermute x1, starting transfers between devices, two_slices(): first = lax.ppermute(send, ('probe', 'tile'), even_far)  2.65 us
    ppermute x1, starting transfers between devices, two_slices(): a_own = lax.ppermute(adj_own, ('probe', 'depth'), flip)  2.22 us
    ppermute x1, starting transfers between devices, two_slices(): corner_next = lax.ppermute(corner, 'probe', z1)  1.54 us
    pallas_call x1, Pallas kernels, two_slices(): pl.pallas_call(send_kernel, out_shape=(block, block, jax.ShapeDtypeStruct...  1.51 us
    ppermute x1, waiting for transfers between devices, two_slices(): near = lax.ppermute(after(side_keep, first), 'tile', swap_tile)  1.31 us
    ppermute x1, waiting for transfers between devices, two_slices(): first = lax.ppermute(send, ('probe', 'tile'), even_far)  1.26 us
  transfers between devices with their start and end apart: 10, of which 7 were waited for; matrix products, arithmetic and copies ran while one was open for 0% of the time, Pallas kernels for 10%

profile of v10, /device:TPU:0, one launch (start us, length us, event | category | flops | bytes accessed | tf_op | source)
XLA Modules:
  0.0 23.9 jit_solution(3059455692410813317)
XLA Ops:
  0.0 0.0 copy-start.1
  0.0 0.0 copy-start
  0.0 3.1 %collective-permute-start.3 = (bf16[2,256,256]{2,1,0:T(8,128)(2,1)}, bf16[2,256,256]{2,1,0:T(8,128)(2,1)S(1)}, u32[]{:S(2)}, u32[]{:S(2)}) collective-permute-start(bf16[2,256,256]{2,1,0:T(8,128)(2,1)} %bitcast.9), channel_id=1, source_target_pairs={{0,4},{4,0},{8,12},{12,8},{1,5},{5,1},{9,13},{13,9},{2,6},{6,2},{1... | collective-permute-start | bytes 786440 | tf_op jit(solution)/shard_map/ppermute | solution.py:202
  3.8 0.0 copy-done.1
  3.8 0.0 copy-done
  3.8 0.0 copy-start.2
  3.8 1.5 %adjoint.1 = (bf16[2,128,256]{2,1,0:T(8,128)(2,1)S(1)}, bf16[2,128,256]{2,1,0:T(8,128)(2,1)S(1)}, bf16[16,256]{1,0:T(8,128)(2,1)S(1)}) custom-call(f32[8,128]{1,0:T(8,128)S(1)} %early.1.early_ref, s32[1]{0:T(128)S(6)} %copy.8.slot_ref, s32[2,8]{1,0:T(2,128)} %bitcast.12, bf16[2,256,256]{2,1,0:T(8,128)(2,1)} %bitcast.11, f32[2,256,256]{2,1,0:T(8,128)S(1)} %copy-done.1, ...), custom_call_target="tpu_custom_call" | custom-call | tf_op jit(solution)/shard_map/adjoint/pallas_call | solution.py:181
  5.3 2.2 %collective-permute-start.1 = (bf16[2,128,256]{2,1,0:T(8,128)(2,1)S(1)}, bf16[2,128,256]{2,1,0:T(8,128)(2,1)S(1)}, u32[]{:S(2)}, u32[]{:S(2)}) collective-permute-start(bf16[2,128,256]{2,1,0:T(8,128)(2,1)S(1)} %get-tuple-element.16), channel_id=1, source_target_pairs={{0,2},{2,0},{4,6},{6,4},{8,10},{10,8},{12,14},{14,12},{1,3},{3,1},... | collective-permute-start | bytes 393224 | tf_op jit(solution)/shard_map/ppermute | solution.py:200
  7.5 0.0 collective-permute-start.2
  7.5 1.5 %collective-permute-start = (bf16[16,256]{1,0:T(8,128)(2,1)S(1)}, bf16[16,256]{1,0:T(8,128)(2,1)S(1)}, u32[]{:S(2)}, u32[]{:S(2)}) collective-permute-start(bf16[16,256]{1,0:T(8,128)(2,1)S(1)} %get-tuple-element.15.c0.in_ref), channel_id=1, source_target_pairs={{0,4},{4,0},{8,12},{12,8},{1,5},{5,1},{9,13},{13,9},{2,6},{6,2},{1... | collective-permute-start | bytes 24584 | tf_op jit(solution)/shard_map/ppermute | solution.py:203
  9.1 3.6 %collective-permute-done.c1 = bf16[16,256]{1,0:T(8,128)(2,1)S(1)} collective-permute-done((bf16[16,256]{1,0:T(8,128)(2,1)S(1)}, bf16[16,256]{1,0:T(8,128)(2,1)S(1)}, u32[]{:S(2)}, u32[]{:S(2)}) %collective-permute-start) | collective-permute-done | bytes 8224 | tf_op jit(solution)/shard_map/ppermute | solution.py:203
  12.6 0.0 collective-permute-done.3.w1
  12.6 0.0 copy-done.2
  12.7 0.4 %rolled_waves.1 = (f32[2,128,256]{2,1,0:T(8,128)S(1)}, f32[2,128,256]{2,1,0:T(8,128)S(1)}) custom-call(bf16[16,256]{1,0:T(8,128)(2,1)S(1)} %get-tuple-element.15.c0.in_ref, bf16[16,256]{1,0:T(8,128)(2,1)S(1)} %collective-permute-done.c1, bf16[2,256,256]{2,1,0:T(8,128)(2,1)S(1)} %bitcast.10, bf16[2,256,256]{2,1,0:T(8,128)(2,1)S(1)} %collective-permute-done.3.w1), custom_call_target="tpu_custom_call" | custom-call | tf_op jit(solution)/shard_map/rolled_waves/pallas_call | solution.py:204
  13.1 0.0 collective-permute-done.1.a0
  13.1 0.5 %collective-permute-done.2.a1 = bf16[2,128,256]{2,1,0:T(8,128)(2,1)S(1)} collective-permute-done((bf16[2,128,256]{2,1,0:T(8,128)(2,1)S(1)}, bf16[2,128,256]{2,1,0:T(8,128)(2,1)S(1)}, u32[]{:S(2)}, u32[]{:S(2)}) %collective-permute-start.2) | collective-permute-done | bytes 131104 | tf_op jit(solution)/shard_map/ppermute | solution.py:201
  13.6 0.2 far_sums.3
  13.8 0.1 collective-permute-start.4
  13.9 0.2 near_sums.1
  14.1 0.2 far_sums.2.here_ref
  14.3 0.9 %collective-permute-done.4.side_ref = bf16[2,128,256]{2,1,0:T(8,128)(2,1)S(1)} collective-permute-done((bf16[2,128,256]{2,1,0:T(8,128)(2,1)S(1)}, bf16[2,128,256]{2,1,0:T(8,128)(2,1)S(1)}, u32[]{:S(2)}, u32[]{:S(2)}) %collective-permute-start.4) | collective-permute-done | bytes 131104 | tf_op jit(solution)/shard_map/ppermute | solution.py:231
  15.2 2.7 %collective-permute-start.5 = (bf16[2,128,256]{2,1,0:T(8,128)(2,1)S(1)}, bf16[2,128,256]{2,1,0:T(8,128)(2,1)S(1)}, u32[]{:S(2)}, u32[]{:S(2)}) collective-permute-start(bf16[2,128,256]{2,1,0:T(8,128)(2,1)S(1)} %far_total.1.refs_0_.in_ref), channel_id=1, source_target_pairs={{0,8},{1,9},{4,5},{5,4},{8,0},{9,1},{12,13},{13,12},{2,10},{3,11},... | collective-permute-start | bytes 393224 | tf_op jit(solution)/shard_map/ppermute | solution.py:249
  17.9 0.0 collective-permute-start.7
  17.9 1.2 %collective-permute-done.7.refs_0_ = bf16[16,256]{1,0:T(8,128)(2,1)S(1)} collective-permute-done((bf16[16,256]{1,0:T(8,128)(2,1)S(1)}, bf16[16,256]{1,0:T(8,128)(2,1)S(1)}, u32[]{:S(2)}, u32[]{:S(2)}) %collective-permute-start.7) | collective-permute-done | bytes 8224 | tf_op jit(solution)/shard_map/ppermute | solution.py:248
  19.1 0.2 collective-permute-start.8
  19.2 1.0 %collective-permute-done.8.refs_0_ = bf16[16,256]{1,0:T(8,128)(2,1)S(1)} collective-permute-done((bf16[16,256]{1,0:T(8,128)(2,1)S(1)}, bf16[16,256]{1,0:T(8,128)(2,1)S(1)}, u32[]{:S(2)}, u32[]{:S(2)}) %collective-permute-start.8) | collective-permute-done | bytes 8224 | tf_op jit(solution)/shard_map/ppermute | solution.py:250
  20.2 0.2 collective-permute-start.9
  20.5 1.3 %collective-permute-done.5.refs_0_ = bf16[2,128,256]{2,1,0:T(8,128)(2,1)S(1)} collective-permute-done((bf16[2,128,256]{2,1,0:T(8,128)(2,1)S(1)}, bf16[2,128,256]{2,1,0:T(8,128)(2,1)S(1)}, u32[]{:S(2)}, u32[]{:S(2)}) %collective-permute-start.5) | collective-permute-done | bytes 131104 | tf_op jit(solution)/shard_map/ppermute | solution.py:249
  21.8 0.1 collective-permute-start.6
  21.8 0.0 collective-permute-done.9
  21.9 1.3 %collective-permute-done.6 = bf16[2,128,256]{2,1,0:T(8,128)(2,1)S(1)} collective-permute-done((bf16[2,128,256]{2,1,0:T(8,128)(2,1)S(1)}, bf16[2,128,256]{2,1,0:T(8,128)(2,1)S(1)}, u32[]{:S(2)}, u32[]{:S(2)}) %collective-permute-start.6) | collective-permute-done | bytes 131104 | tf_op jit(solution)/shard_map/ppermute | solution.py:251
  23.2 0.8 %add_bitcast_fusion = f32[2,1,128,256]{3,2,1,0:T(8,128)} fusion(f32[2,128,256]{2,1,0:T(8,128)S(1)} %get-tuple-element.21, bf16[2,128,256]{2,1,0:T(8,128)(2,1)S(1)} %collective-permute-done.6, bf16[2,128,256]{2,1,0:T(8,128)(2,1)S(1)} %collective-permute-done.9, bf16[2,128,256]{2,1,0:T(8,128)(2,1)S(1)} %collective-permute-done.5.refs_0_, pred[]{:T(512)S(6)} %eq.5), kind=kLoop, calls=%fused_computation | loop fusion | flops 327680 | bytes 917505 | tf_op jit(solution)/shard_map/broadcast_in_dim | solution.py:254
  (6 shorter events, 0.0 us)
Async XLA Ops:
  0.0 3.8 %copy-start.1 = (f32[2,256,256]{2,1,0:T(8,128)S(1)}, f32[2,256,256]{2,1,0:T(8,128)}, u32[]{:S(2)}) copy-start(f32[2,256,256]{2,1,0:T(8,128)} %constant.21.clone.table_ref) | copy-start | bytes 1572868
  0.0 3.8 %copy-start = (f32[1,2,256,256]{3,2,1,0:T(8,128)S(1)}, f32[1,2,256,256]{3,2,1,0:T(8,128)}, u32[]{:S(2)}) copy-start(f32[1,2,256,256]{3,2,1,0:T(8,128)} %param.8) | copy-start | bytes 1572868
  0.0 12.6 %collective-permute-start.3 = (bf16[2,256,256]{2,1,0:T(8,128)(2,1)}, bf16[2,256,256]{2,1,0:T(8,128)(2,1)S(1)}, u32[]{:S(2)}, u32[]{:S(2)}) collective-permute-start(bf16[2,256,256]{2,1,0:T(8,128)(2,1)} %bitcast.9), channel_id=1, source_target_pairs={{0,4},{4,0},{8,12},{12,8},{1,5},{5,1},{9,13},{13,9},{2,6},{6,2},{1... | collective-permute-start | bytes 786440 | tf_op jit(solution)/shard_map/ppermute | solution.py:202
  3.8 8.9 %copy-start.2 = (bf16[1,1,2,256,256]{4,3,2,1,0:T(8,128)(2,1)S(1)}, bf16[1,1,2,256,256]{4,3,2,1,0:T(8,128)(2,1)}, u32[]{:S(2)}) copy-start(bf16[1,1,2,256,256]{4,3,2,1,0:T(8,128)(2,1)} %param.6) | copy-start | bytes 786436
  5.3 7.8 %collective-permute-start.1 = (bf16[2,128,256]{2,1,0:T(8,128)(2,1)S(1)}, bf16[2,128,256]{2,1,0:T(8,128)(2,1)S(1)}, u32[]{:S(2)}, u32[]{:S(2)}) collective-permute-start(bf16[2,128,256]{2,1,0:T(8,128)(2,1)S(1)} %get-tuple-element.16), channel_id=1, source_target_pairs={{0,2},{2,0},{4,6},{6,4},{8,10},{10,8},{12,14},{14,12},{1,3},{3,1},... | collective-permute-start | bytes 393224 | tf_op jit(solution)/shard_map/ppermute | solution.py:200
  7.5 6.1 %collective-permute-start.2 = (bf16[2,128,256]{2,1,0:T(8,128)(2,1)S(1)}, bf16[2,128,256]{2,1,0:T(8,128)(2,1)S(1)}, u32[]{:S(2)}, u32[]{:S(2)}) collective-permute-start(bf16[2,128,256]{2,1,0:T(8,128)(2,1)S(1)} %get-tuple-element.17), channel_id=1, source_target_pairs={{0,6},{2,4},{4,2},{6,0},{8,14},{10,12},{12,10},{14,8},{1,7},{3,5},... | collective-permute-start | bytes 393224 | tf_op jit(solution)/shard_map/ppermute | solution.py:201
  7.5 5.1 %collective-permute-start = (bf16[16,256]{1,0:T(8,128)(2,1)S(1)}, bf16[16,256]{1,0:T(8,128)(2,1)S(1)}, u32[]{:S(2)}, u32[]{:S(2)}) collective-permute-start(bf16[16,256]{1,0:T(8,128)(2,1)S(1)} %get-tuple-element.15.c0.in_ref), channel_id=1, source_target_pairs={{0,4},{4,0},{8,12},{12,8},{1,5},{5,1},{9,13},{13,9},{2,6},{6,2},{1... | collective-permute-start | bytes 24584 | tf_op jit(solution)/shard_map/ppermute | solution.py:203
  13.8 1.4 %collective-permute-start.4 = (bf16[2,128,256]{2,1,0:T(8,128)(2,1)S(1)}, bf16[2,128,256]{2,1,0:T(8,128)(2,1)S(1)}, u32[]{:S(2)}, u32[]{:S(2)}) collective-permute-start(bf16[2,128,256]{2,1,0:T(8,128)(2,1)S(1)} %far_sums.3), channel_id=1, source_target_pairs={{0,1},{1,0},{2,3},{3,2},{4,5},{5,4},{6,7},{7,6},{8,9},{9,8},{10,11... | collective-permute-start | bytes 393224 | tf_op jit(solution)/shard_map/ppermute | solution.py:231
  15.2 6.5 %collective-permute-start.5 = (bf16[2,128,256]{2,1,0:T(8,128)(2,1)S(1)}, bf16[2,128,256]{2,1,0:T(8,128)(2,1)S(1)}, u32[]{:S(2)}, u32[]{:S(2)}) collective-permute-start(bf16[2,128,256]{2,1,0:T(8,128)(2,1)S(1)} %far_total.1.refs_0_.in_ref), channel_id=1, source_target_pairs={{0,8},{1,9},{4,5},{5,4},{8,0},{9,1},{12,13},{13,12},{2,10},{3,11},... | collective-permute-start | bytes 393224 | tf_op jit(solution)/shard_map/ppermute | solution.py:249
  17.9 1.2 %collective-permute-start.7 = (bf16[16,256]{1,0:T(8,128)(2,1)S(1)}, bf16[16,256]{1,0:T(8,128)(2,1)S(1)}, u32[]{:S(2)}, u32[]{:S(2)}) collective-permute-start(bf16[16,256]{1,0:T(8,128)(2,1)S(1)} %after.5), channel_id=1, source_target_pairs={{0,1},{1,0},{2,3},{3,2},{4,5},{5,4},{6,7},{7,6},{8,9},{9,8},{10,11... | collective-permute-start | bytes 24584 | tf_op jit(solution)/shard_map/ppermute | solution.py:248
  19.1 1.2 %collective-permute-start.8 = (bf16[16,256]{1,0:T(8,128)(2,1)S(1)}, bf16[16,256]{1,0:T(8,128)(2,1)S(1)}, u32[]{:S(2)}, u32[]{:S(2)}) collective-permute-start(bf16[16,256]{1,0:T(8,128)(2,1)S(1)} %after.6), channel_id=1, source_target_pairs={{0,1},{1,0},{2,3},{3,2},{4,5},{5,4},{6,7},{7,6},{8,9},{9,8},{10,11... | collective-permute-start | bytes 24584 | tf_op jit(solution)/shard_map/ppermute | solution.py:250
  20.2 1.6 %collective-permute-start.9 = (bf16[2,128,256]{2,1,0:T(8,128)(2,1)S(1)}, bf16[2,128,256]{2,1,0:T(8,128)(2,1)S(1)}, u32[]{:S(2)}, u32[]{:S(2)}) collective-permute-start(bf16[2,128,256]{2,1,0:T(8,128)(2,1)S(1)} %after.7), channel_id=1, source_target_pairs={{0,1},{1,0},{4,12},{5,13},{8,9},{9,8},{12,4},{13,5},{2,3},{3,2},{6... | collective-permute-start | bytes 393224 | tf_op jit(solution)/shard_map/ppermute | solution.py:252
  21.8 1.4 %collective-permute-start.6 = (bf16[2,128,256]{2,1,0:T(8,128)(2,1)S(1)}, bf16[2,128,256]{2,1,0:T(8,128)(2,1)S(1)}, u32[]{:S(2)}, u32[]{:S(2)}) collective-permute-start(bf16[2,128,256]{2,1,0:T(8,128)(2,1)S(1)} %after.4), channel_id=1, source_target_pairs={{0,1},{1,0},{2,3},{3,2},{4,5},{5,4},{6,7},{7,6},{8,9},{9,8},{10,11... | collective-permute-start | bytes 393224 | tf_op jit(solution)/shard_map/ppermute | solution.py:251
